TPU v7x, 128 devices: a whole 4x4x4 slice. The times are simulated.
128 devices in a mesh: section: 2 (over core), tensor: 4 (over z), dp: 16 (over x, y).
Axes of the slice: x: 4, y: 4, z: 4, core: 2. Of those that a mesh axis runs over, the one named last changes fastest.
Arguments:
- layer_input: bfloat16 [2048, 2560], P('dp'), may hold values from -6 to 6
- cotangent: bfloat16 [2048, 2560], P('dp'), may hold values from -6 to 6
- seq_lengths: int32 [32, 4], P('dp'), may hold values from 0 to 64, as said below
- g_attn: bfloat16 [2, 2560], P('section', 'dp'), may hold values from 0.5 to 1.5
- w_qa: bfloat16 [2, 2560, 768], P('section', 'dp'), may hold values from -0.125 to 0.125
- g_q: bfloat16 [2, 768], P('section', 'dp'), may hold values from 0.5 to 1.5
- w_qb: bfloat16 [2, 768, 3840], P('section', 'dp', 'tensor'), may hold values from -0.21875 to 0.21875
- w_kva: bfloat16 [2, 2560, 288], P('section', 'dp'), may hold values from -0.125 to 0.125
- g_kv: bfloat16 [2, 256], P('section', 'dp'), may hold values from 0.5 to 1.5
- w_kvb: bfloat16 [2, 256, 5120], P('section', 'dp', 'tensor'), may hold values from -0.375 to 0.375
- w_o: bfloat16 [2, 2560, 2560], P('section', 'tensor', 'dp'), may hold values from -2 to 2
- g_ffn: bfloat16 [2, 2560], P('section', 'dp'), may hold values from 0.5 to 1.5
- w_gate: bfloat16 [2, 2560, 6400], P('section', 'dp', 'tensor'), may hold values from -0.125 to 0.125
- w_up: bfloat16 [2, 2560, 6400], P('section', 'dp', 'tensor'), may hold values from -0.125 to 0.125
- w_down: bfloat16 [2, 6400, 2560], P('section', 'tensor', 'dp'), may hold values from -0.625 to 0.625
Outputs:
- layer_out: bfloat16 [2, 2048, 2560], P('section', 'dp')
- input_grad: bfloat16 [2, 2048, 2560], P('section', 'dp')
- g_attn_grad: float32 [2, 2560], P('section', 'dp')
- w_qa_grad: float32 [2, 2560, 768], P('section', 'dp')
- g_q_grad: float32 [2, 768], P('section', 'dp')
- w_qb_grad: float32 [2, 768, 3840], P('section', 'dp', 'tensor')
- w_kva_grad: float32 [2, 2560, 288], P('section', 'dp')
- g_kv_grad: float32 [2, 256], P('section', 'dp')
- w_kvb_grad: float32 [2, 256, 5120], P('section', 'dp', 'tensor')
- w_o_grad: float32 [2, 2560, 2560], P('section', 'tensor', 'dp')
- g_ffn_grad: float32 [2, 2560], P('section', 'dp')
- w_gate_grad: float32 [2, 2560, 6400], P('section', 'dp', 'tensor')
- w_up_grad: float32 [2, 2560, 6400], P('section', 'dp', 'tensor')
- w_down_grad: float32 [2, 6400, 2560], P('section', 'tensor', 'dp')
Inputs may be any that keep to these rules, and one draw needn't show every extreme that they name: `seq_lengths`: each row sums to 64; lengths may be 0; in one row, drawn from the seed, a single sequence fills the pack.
All inputs are finite; a program needn't handle non-finite values.
Results may differ from a plain program's by a relative error of at most 0.03.
Values may be sent and summed in bfloat16 or wider, within the bound.
No kernel may reach another device: no remote copies, remote signals or barrier semaphores. Data moves between devices by JAX's collectives and lax.ppermute only.
A program may use at most 256 MiB of HBM per device.

v0:
```python
import math

import jax
import jax.numpy as jnp
from jax import lax
from jax.sharding import PartitionSpec as P

NOPE = 64
ROPE = 32
VD = 64
KVR = 256
PACK = 64
MB = 2


RES_SCALE = 1.4 / math.sqrt(62.0)
EPSILON = 1e-05


def shifted(x, axis, by):
    devices = lax.axis_size(axis)
    pairs = [(i, i + by) for i in range(devices) if 0 <= i + by < devices]
    return lax.ppermute(x, axis, pairs)


def product(left_side, right_side):
    return jnp.dot(left_side, right_side, preferred_element_type=jnp.float32)


def product_left(left_side, right_side):
    return lax.dot_general(
        left_side, right_side, (((0,), (0,)), ((), ())), preferred_element_type=jnp.float32
    )


def product_right(left_side, right_side):
    return lax.dot_general(
        left_side, right_side, (((1,), (1,)), ((), ())), preferred_element_type=jnp.float32
    )


def rms_scale(inputs, gain_vec):
    return (
        inputs * lax.rsqrt(jnp.mean(inputs * inputs, axis=-1, keepdims=True) + EPSILON) * gain_vec
    )


def rotate(inputs, cosine, sine_table):
    half_width = inputs.shape[-1] // 2
    turned = jnp.concatenate([-inputs[..., half_width:], inputs[..., :half_width]], axis=-1)
    return inputs * cosine + turned * sine_table


def rotate_back(grads_in, cosine, sine_table):
    half_width = grads_in.shape[-1] // 2
    scaled_grad = grads_in * sine_table
    return grads_in * cosine + jnp.concatenate(
        [scaled_grad[..., half_width:], -scaled_grad[..., :half_width]], axis=-1
    )


def pack_tables(seq_row):
    row_index = jnp.arange(PACK, dtype=jnp.int32)
    seq_ends = jnp.cumsum(seq_row)
    past_end = row_index[:, None] >= seq_ends[None, :]
    segment = jnp.sum(past_end.astype(jnp.int32), axis=1)
    seq_start = jnp.sum(jnp.where(past_end, seq_row[None, :], 0), axis=1)
    position = (row_index - seq_start).astype(jnp.float32)
    frequency = 10000.0 ** (-2.0 * jnp.arange(ROPE // 2, dtype=jnp.float32) / ROPE)
    angles = position[:, None] * frequency[None, :]
    cosine = jnp.concatenate([jnp.cos(angles), jnp.cos(angles)], axis=1)
    sine_table = jnp.concatenate([jnp.sin(angles), jnp.sin(angles)], axis=1)
    allowed = (segment[:, None] == segment[None, :]) & (row_index[None, :] <= row_index[:, None])
    return (cosine, sine_table, allowed)


def score_probs(query_all, key_all, allowed):
    scores = jnp.einsum("qhd,khd->hqk", query_all, key_all, preferred_element_type=jnp.float32) * (
        NOPE + ROPE
    ) ** (-0.5)
    return jax.nn.softmax(jnp.where(allowed[None], scores, -1e30), axis=-1)


def swish_product(gate_act, up_act):
    return jax.nn.silu(gate_act) * up_act


def collect_once(weight_shards):
    gathered = (
        lax.all_gather(weight_shards[0], "dp", axis=1, tiled=True),
        lax.all_gather(weight_shards[1], "dp", axis=1, tiled=True),
        lax.all_gather(weight_shards[2], "dp", axis=1, tiled=True),
        lax.all_gather(weight_shards[3], "dp", axis=1, tiled=True),
        lax.all_gather(weight_shards[4], "dp", axis=1, tiled=True),
        lax.all_gather(weight_shards[5], "dp", axis=1, tiled=True),
        lax.all_gather(weight_shards[6], "dp", axis=1, tiled=True),
        lax.all_gather(weight_shards[7], "dp", axis=2, tiled=True),
        lax.all_gather(weight_shards[8], "dp", axis=1, tiled=True),
        lax.all_gather(weight_shards[9], "dp", axis=1, tiled=True),
        lax.all_gather(weight_shards[10], "dp", axis=1, tiled=True),
        lax.all_gather(weight_shards[11], "dp", axis=2, tiled=True),
    )
    return tuple((member[0] for member in gathered))


def spread_end(weight_grads):
    return (
        lax.psum_scatter(
            weight_grads[0].astype(jnp.bfloat16), "dp", scatter_dimension=0, tiled=True
        ).astype(jnp.float32),
        lax.psum_scatter(
            weight_grads[1].astype(jnp.bfloat16), "dp", scatter_dimension=0, tiled=True
        ).astype(jnp.float32),
        lax.psum_scatter(
            weight_grads[2].astype(jnp.bfloat16), "dp", scatter_dimension=0, tiled=True
        ).astype(jnp.float32),
        lax.psum_scatter(
            weight_grads[3].astype(jnp.bfloat16), "dp", scatter_dimension=0, tiled=True
        ).astype(jnp.float32),
        lax.psum_scatter(
            weight_grads[4].astype(jnp.bfloat16), "dp", scatter_dimension=0, tiled=True
        ).astype(jnp.float32),
        lax.psum_scatter(
            weight_grads[5].astype(jnp.bfloat16), "dp", scatter_dimension=0, tiled=True
        ).astype(jnp.float32),
        lax.psum_scatter(
            weight_grads[6].astype(jnp.bfloat16), "dp", scatter_dimension=0, tiled=True
        ).astype(jnp.float32),
        lax.psum_scatter(
            weight_grads[7].astype(jnp.bfloat16), "dp", scatter_dimension=1, tiled=True
        ).astype(jnp.float32),
        lax.psum_scatter(
            weight_grads[8].astype(jnp.bfloat16), "dp", scatter_dimension=0, tiled=True
        ).astype(jnp.float32),
        lax.psum_scatter(
            weight_grads[9].astype(jnp.bfloat16), "dp", scatter_dimension=0, tiled=True
        ).astype(jnp.float32),
        lax.psum_scatter(
            weight_grads[10].astype(jnp.bfloat16), "dp", scatter_dimension=0, tiled=True
        ).astype(jnp.float32),
        lax.psum_scatter(
            weight_grads[11].astype(jnp.bfloat16), "dp", scatter_dimension=1, tiled=True
        ).astype(jnp.float32),
    )


def layer_forward(block_in, full_weights, tables):
    g_attn, w_qa, g_q, w_qb, w_kva, g_kv, w_kvb, w_o, g_ffn, w_gate, w_up, w_down = full_weights
    cosine, sine_table, allowed = tables
    row_count = block_in.shape[0]
    head_count = w_o.shape[0] // VD
    normed = rms_scale(block_in, g_attn.astype(jnp.float32)).astype(jnp.bfloat16)
    latent_q = product(normed, w_qa)
    squeezed = rms_scale(latent_q, g_q.astype(jnp.float32)).astype(jnp.bfloat16)
    query_raw = product(squeezed, w_qb).reshape(row_count, head_count, NOPE + ROPE)
    query_all = jnp.concatenate(
        [
            query_raw[..., :NOPE],
            rotate(query_raw[..., NOPE:], cosine[:, None, :], sine_table[:, None, :]),
        ],
        axis=-1,
    ).astype(jnp.bfloat16)
    latent_kv = product(normed, w_kva)
    compact = rms_scale(latent_kv[:, :KVR], g_kv.astype(jnp.float32)).astype(jnp.bfloat16)
    key_rope = rotate(latent_kv[:, KVR:], cosine, sine_table).astype(jnp.bfloat16)
    key_value = product(compact, w_kvb).reshape(row_count, head_count, NOPE + VD)
    key_all = jnp.concatenate(
        [
            key_value[..., :NOPE].astype(jnp.bfloat16),
            jnp.broadcast_to(key_rope[:, None, :], (row_count, head_count, ROPE)),
        ],
        axis=-1,
    )
    value_all = key_value[..., NOPE:].astype(jnp.bfloat16)
    attn_probs = score_probs(query_all, key_all, allowed)
    mixed_heads = (
        jnp.einsum(
            "hqk,khd->qhd",
            attn_probs.astype(jnp.bfloat16),
            value_all,
            preferred_element_type=jnp.float32,
        )
        .reshape(row_count, head_count * VD)
        .astype(jnp.bfloat16)
    )
    attended = lax.psum(product(mixed_heads, w_o), "tensor")
    middle = block_in + RES_SCALE * attended
    normed_two = rms_scale(middle, g_ffn.astype(jnp.float32)).astype(jnp.bfloat16)
    gate_act = product(normed_two, w_gate)
    up_act = product(normed_two, w_up)
    hidden = swish_product(gate_act, up_act).astype(jnp.bfloat16)
    mlp_out = lax.psum(product(hidden, w_down), "tensor")
    saved_acts = (
        block_in,
        normed,
        latent_q,
        squeezed,
        query_all,
        latent_kv,
        compact,
        key_all,
        value_all,
        mixed_heads,
        middle,
        normed_two,
        gate_act,
        up_act,
        hidden,
    )
    return (middle + RES_SCALE * mlp_out, saved_acts)


def layer_backward(grad_out, saved_acts, full_weights, tables):
    g_attn, w_qa, g_q, w_qb, w_kva, g_kv, w_kvb, w_o, g_ffn, w_gate, w_up, w_down = full_weights
    cosine, sine_table, allowed = tables
    (
        block_in,
        normed,
        latent_q,
        squeezed,
        query_all,
        latent_kv,
        compact,
        key_all,
        value_all,
        mixed_heads,
        middle,
        normed_two,
        gate_act,
        up_act,
        hidden,
    ) = saved_acts
    row_count = block_in.shape[0]
    head_count = key_all.shape[1]
    d_mlp = (RES_SCALE * grad_out).astype(jnp.bfloat16)
    down_grad = product_left(hidden, d_mlp)
    d_hidden = product_right(d_mlp, w_down)
    d_gate, d_up = jax.vjp(swish_product, gate_act, up_act)[1](d_hidden)
    d_gate = d_gate.astype(jnp.bfloat16)
    d_up = d_up.astype(jnp.bfloat16)
    gate_grad = product_left(normed_two, d_gate)
    up_grad = product_left(normed_two, d_up)
    d_normed_two = lax.psum(product_right(d_gate, w_gate) + product_right(d_up, w_up), "tensor")
    d_middle, ffn_gain_grad = jax.vjp(rms_scale, middle, g_ffn.astype(jnp.float32))[1](d_normed_two)
    d_middle = d_middle + grad_out
    d_attended = (RES_SCALE * d_middle).astype(jnp.bfloat16)
    out_grad = product_left(mixed_heads, d_attended)
    d_mixed = product_right(d_attended, w_o).astype(jnp.bfloat16).reshape(row_count, head_count, VD)
    attn_probs = score_probs(query_all, key_all, allowed)
    d_probs = jnp.einsum("qhd,khd->hqk", d_mixed, value_all, preferred_element_type=jnp.float32)
    d_scores = (
        attn_probs * (d_probs - jnp.sum(attn_probs * d_probs, axis=-1, keepdims=True))
    ).astype(jnp.bfloat16)
    score_scale = (NOPE + ROPE) ** (-0.5)
    d_query = (
        jnp.einsum("hqk,khd->qhd", d_scores, key_all, preferred_element_type=jnp.float32)
        * score_scale
    )
    d_keys = (
        jnp.einsum("hqk,qhd->khd", d_scores, query_all, preferred_element_type=jnp.float32)
        * score_scale
    )
    d_values = jnp.einsum(
        "hqk,qhd->khd", attn_probs.astype(jnp.bfloat16), d_mixed, preferred_element_type=jnp.float32
    )
    d_query_raw = jnp.concatenate(
        [
            d_query[..., :NOPE],
            rotate_back(d_query[..., NOPE:], cosine[:, None, :], sine_table[:, None, :]),
        ],
        axis=-1,
    )
    d_query_raw = d_query_raw.reshape(row_count, head_count * (NOPE + ROPE)).astype(jnp.bfloat16)
    query_up_grad = product_left(squeezed, d_query_raw)
    d_kv_raw = (
        jnp.concatenate([d_keys[..., :NOPE], d_values], axis=-1)
        .reshape(row_count, head_count * (NOPE + VD))
        .astype(jnp.bfloat16)
    )
    kv_up_grad = product_left(compact, d_kv_raw)
    rope_part = rotate_back(jnp.sum(d_keys[..., NOPE:], axis=1), cosine, sine_table)
    d_squeezed, d_compact, d_rope = lax.psum(
        (product_right(d_query_raw, w_qb), product_right(d_kv_raw, w_kvb), rope_part), "tensor"
    )
    d_latent_q, q_gain_grad = jax.vjp(rms_scale, latent_q, g_q.astype(jnp.float32))[1](d_squeezed)
    d_latent_c, kv_gain_grad = jax.vjp(rms_scale, latent_kv[:, :KVR], g_kv.astype(jnp.float32))[1](
        d_compact
    )
    d_latent_q = d_latent_q.astype(jnp.bfloat16)
    d_latent_kv = jnp.concatenate([d_latent_c, d_rope], axis=1).astype(jnp.bfloat16)
    q_down_grad = product_left(normed, d_latent_q)
    kv_down_grad = product_left(normed, d_latent_kv)
    d_normed = product_right(d_latent_q, w_qa) + product_right(d_latent_kv, w_kva)
    d_block, attn_gain_grad = jax.vjp(rms_scale, block_in, g_attn.astype(jnp.float32))[1](d_normed)
    weight_grads = (
        attn_gain_grad,
        q_down_grad,
        q_gain_grad,
        query_up_grad,
        kv_down_grad,
        kv_gain_grad,
        kv_up_grad,
        out_grad,
        ffn_gain_grad,
        gate_grad,
        up_grad,
        down_grad,
    )
    return (d_block + d_middle, weight_grads)


def body(
    layer_input,
    cotangent,
    seq_lengths,
    g_attn,
    w_qa,
    g_q,
    w_qb,
    w_kva,
    g_kv,
    w_kvb,
    w_o,
    g_ffn,
    w_gate,
    w_up,
    w_down,
):
    weight_shards = (g_attn, w_qa, g_q, w_qb, w_kva, g_kv, w_kvb, w_o, g_ffn, w_gate, w_up, w_down)
    section_index = lax.axis_index("section")
    model_width = layer_input.shape[1]
    inputs = layer_input.reshape(MB, PACK, model_width)
    cot_packs = cotangent.reshape(MB, PACK, model_width)
    kept_weights = collect_once(weight_shards)
    carried = jnp.zeros((PACK, model_width), jnp.bfloat16)
    layer_out = jnp.zeros((MB, PACK, model_width), jnp.bfloat16)
    records = []
    for tick_index in range(MB + 1):
        micro_index = tick_index - section_index
        is_live = (micro_index >= 0) & (micro_index < MB)
        micro_index = jnp.clip(micro_index, 0, MB - 1)
        full_weights = kept_weights
        block_in = jnp.where(section_index == 0, inputs[min(tick_index, MB - 1)], carried)
        tables = pack_tables(lax.dynamic_index_in_dim(seq_lengths, micro_index, 0, keepdims=False))
        result, saved_acts = layer_forward(block_in.astype(jnp.float32), full_weights, tables)
        outgoing = result.astype(jnp.bfloat16)
        layer_out = jnp.where(
            is_live, lax.dynamic_update_index_in_dim(layer_out, outgoing, micro_index, 0), layer_out
        )
        records.append((tables, saved_acts))
        if tick_index < MB:
            carried = shifted(outgoing, "section", 1)
    incoming = jnp.zeros((PACK, model_width), jnp.bfloat16)
    input_grad = jnp.zeros((MB, PACK, model_width), jnp.bfloat16)
    grad_totals = None
    for turn_index in range(MB + 1):
        micro_index = MB - turn_index - section_index
        is_live = (micro_index >= 0) & (micro_index < MB)
        micro_index = jnp.clip(micro_index, 0, MB - 1)
        full_weights = kept_weights
        tables, saved_acts = records[MB - turn_index]
        grad_start = jnp.where(
            section_index == 1, cot_packs[max(MB - 1 - turn_index, 0)], incoming
        ).astype(jnp.float32)
        grad_start = jnp.where(is_live, grad_start, 0.0)
        d_block, weight_grads = layer_backward(grad_start, saved_acts, full_weights, tables)
        outgoing = d_block.astype(jnp.bfloat16)
        input_grad = jnp.where(
            is_live,
            lax.dynamic_update_index_in_dim(input_grad, outgoing, micro_index, 0),
            input_grad,
        )
        if turn_index == 0:
            grad_totals = weight_grads
        else:
            grad_totals = tuple(
                (first + second for first, second in zip(grad_totals, weight_grads))
            )
        if turn_index < MB:
            incoming = shifted(outgoing, "section", -1)
    grad_totals = spread_end(grad_totals)
    layer_rows = layer_out.reshape(1, MB * PACK, model_width)
    grad_rows = input_grad.reshape(1, MB * PACK, model_width)
    return (
        layer_rows,
        grad_rows,
        grad_totals[0][None],
        grad_totals[1][None],
        grad_totals[2][None],
        grad_totals[3][None],
        grad_totals[4][None],
        grad_totals[5][None],
        grad_totals[6][None],
        grad_totals[7][None],
        grad_totals[8][None],
        grad_totals[9][None],
        grad_totals[10][None],
        grad_totals[11][None],
    )


def solution(mesh):
    in_specs = (
        P("dp", None),
        P("dp", None),
        P("dp", None),
        P("section", "dp"),
        P("section", "dp", None),
        P("section", "dp"),
        P("section", "dp", "tensor"),
        P("section", "dp", None),
        P("section", "dp"),
        P("section", "dp", "tensor"),
        P("section", "tensor", "dp"),
        P("section", "dp"),
        P("section", "dp", "tensor"),
        P("section", "dp", "tensor"),
        P("section", "tensor", "dp"),
    )
    out_specs = (
        P("section", "dp", None),
        P("section", "dp", None),
        P("section", "dp"),
        P("section", "dp", None),
        P("section", "dp"),
        P("section", "dp", "tensor"),
        P("section", "dp", None),
        P("section", "dp"),
        P("section", "dp", "tensor"),
        P("section", "tensor", "dp"),
        P("section", "dp"),
        P("section", "dp", "tensor"),
        P("section", "dp", "tensor"),
        P("section", "tensor", "dp"),
    )
    return jax.shard_map(body, mesh=mesh, in_specs=in_specs, out_specs=out_specs, check_vma=False)
```

profile of v0, /device:TPU:1, one launch (start us, length us, event | category | flops | bytes accessed | tf_op | source)
XLA Modules:
  0.0 1777.8 jit_solution(13274868518566392962)
XLA Ops:
  38.0 58.8 %all-reduce.12 = (bf16[2560]{0:T(1024)(128)(2,1)S(1)}, bf16[256]{0:T(256)(128)(2,1)S(1)}, bf16[768]{0:T(1024)(128)(2,1)S(1)}, bf16[2560]{0:T(1024)(128)(2,1)}) all-reduce(bf16[2560]{0:T(1024)(128)(2,1)S(1)} %dynamic-update-slice.6, bf16[256]{0:T(256)(128)(2,1)S(1)} %dynamic-update-slice.7, ...), channel_id=1, replica_groups=mesh['section'=2,'tensor'=4,'dp'=16] {'dp'}, use_global_device_ids=true, to_apply=%add | all-reduce | flops 6144 | bytes 24576
  110.7 44.5 %all-gather.10.cloned.1.call-done = bf16[1,2560,768]{2,1,0:T(8,128)(2,1)} async-done(((bf16[1,160,768]{2,1,0:T(8,128)(2,1)}), bf16[1,2560,768]{2,1,0:T(8,128)(2,1)}) %all-gather.10.cloned.1.call-update) | async-done | bytes 3932176 | tf_op jit(solution)/shard_map/all_gather | solution.py:91
  163.1 41.9 %all-gather.14.cloned.1.call-done = bf16[1,640,2560]{1,2,0:T(8,128)(2,1)} async-done(((bf16[1,640,160]{1,2,0:T(8,128)(2,1)}), bf16[1,640,2560]{1,2,0:T(8,128)(2,1)}) %all-gather.14.cloned.1.call-update) | async-done | bytes 3276816 | tf_op jit(solution)/shard_map/all_gather | solution.py:97
  211.1 39.2 %all-reduce.25.cloned.1.call-done = f32[64,2560]{1,0:T(8,128)} async-done(((f32[64,2560]{1,0:T(8,128)}), f32[64,2560]{1,0:T(8,128)}) %all-reduce.25.cloned.1.call-update) | async-done | bytes 655376 | tf_op jit(solution)/shard_map/psum | solution.py:186
  252.9 73.0 %all-gather.16.cloned.1.call-done = bf16[1,2560,1600]{2,1,0:T(8,128)(2,1)} async-done(((bf16[1,160,1600]{2,1,0:T(8,128)(2,1)}), bf16[1,2560,1600]{2,1,0:T(8,128)(2,1)}) %all-gather.16.cloned.1.call-update) | async-done | bytes 8192016 | tf_op jit(solution)/shard_map/all_gather | solution.py:99
  330.9 68.1 %all-gather.18.cloned.1.call-done = bf16[1,2560,1600]{2,1,0:T(8,128)(2,1)} async-done(((bf16[1,160,1600]{2,1,0:T(8,128)(2,1)}), bf16[1,2560,1600]{2,1,0:T(8,128)(2,1)}) %all-gather.18.cloned.1.call-update) | async-done | bytes 8192016 | tf_op jit(solution)/shard_map/all_gather | solution.py:100
  404.8 67.3 %all-gather.20.cloned.1.call-done = bf16[1,1600,2560]{1,2,0:T(8,128)(2,1)} async-done(((bf16[1,1600,160]{1,2,0:T(8,128)(2,1)}), bf16[1,1600,2560]{1,2,0:T(8,128)(2,1)}) %all-gather.20.cloned.1.call-update) | async-done | bytes 8192016 | tf_op jit(solution)/shard_map/all_gather | solution.py:101
  479.2 41.9 %all-reduce.27.cloned.1.call-done = f32[64,2560]{1,0:T(8,128)} async-done(((f32[64,2560]{1,0:T(8,128)}), f32[64,2560]{1,0:T(8,128)}) %all-reduce.27.cloned.1.call-update) | async-done | bytes 655376 | tf_op jit(solution)/shard_map/psum | solution.py:192
  542.6 42.9 %all-reduce.29.cloned.1.call-done = f32[64,2560]{1,0:T(8,128)} async-done(((f32[64,2560]{1,0:T(8,128)}), f32[64,2560]{1,0:T(8,128)}) %all-reduce.29.cloned.1.call-update) | async-done | bytes 655376 | tf_op jit(solution)/shard_map/psum | solution.py:186
  603.3 44.5 %all-reduce.31.cloned.1.call-done = f32[64,2560]{1,0:T(8,128)} async-done(((f32[64,2560]{1,0:T(8,128)}), f32[64,2560]{1,0:T(8,128)}) %all-reduce.31.cloned.1.call-update) | async-done | bytes 655376 | tf_op jit(solution)/shard_map/psum | solution.py:192
  677.7 36.2 %all-reduce.33.cloned.1.call-done = f32[64,2560]{1,0:T(8,128)} async-done(((f32[64,2560]{1,0:T(8,128)}), f32[64,2560]{1,0:T(8,128)}) %all-reduce.33.cloned.1.call-update) | async-done | bytes 655376 | tf_op jit(solution)/shard_map/psum | solution.py:186
  730.4 44.5 %all-reduce.35.cloned.1.call-done = f32[64,2560]{1,0:T(8,128)} async-done(((f32[64,2560]{1,0:T(8,128)}), f32[64,2560]{1,0:T(8,128)}) %all-reduce.35.cloned.1.call-update) | async-done | bytes 655376 | tf_op jit(solution)/shard_map/psum | solution.py:243
  813.3 26.4 %all-reduce.45.cloned.1.call-done = (f32[64,256]{1,0:T(8,128)}, f32[64,768]{1,0:T(8,128)}) async-done(((f32[64,256]{1,0:T(8,128)}, f32[64,768]{1,0:T(8,128)}), (f32[64,256]{1,0:T(8,128)}, f32[64,768]{1,0:T(8,128)})) %all-reduce.45.cloned.1.call-update) | async-done | bytes 262160 | tf_op jit(solution)/shard_map/psum | solution.py:282
  871.2 42.2 %all-reduce.37.cloned.1.call-done = f32[64,2560]{1,0:T(8,128)} async-done(((f32[64,2560]{1,0:T(8,128)}), f32[64,2560]{1,0:T(8,128)}) %all-reduce.37.cloned.1.call-update) | async-done | bytes 655376 | tf_op jit(solution)/shard_map/psum | solution.py:243
  951.9 26.3 %all-reduce.43.cloned.1.call-done = (f32[64,256]{1,0:T(8,128)}, f32[64,768]{1,0:T(8,128)}) async-done(((f32[64,256]{1,0:T(8,128)}, f32[64,768]{1,0:T(8,128)}), (f32[64,256]{1,0:T(8,128)}, f32[64,768]{1,0:T(8,128)})) %all-reduce.43.cloned.1.call-update) | async-done | bytes 262160 | tf_op jit(solution)/shard_map/psum | solution.py:282
  1016.8 35.1 %all-reduce.39.cloned.1.call-done = f32[64,2560]{1,0:T(8,128)} async-done(((f32[64,2560]{1,0:T(8,128)}), f32[64,2560]{1,0:T(8,128)}) %all-reduce.39.cloned.1.call-update) | async-done | bytes 655376 | tf_op jit(solution)/shard_map/psum | solution.py:243
  1093.0 21.8 %all-reduce.41.cloned.1.call-done = (f32[64,2560]{1,0:T(8,128)}, f32[64,256]{1,0:T(8,128)}, f32[64,768]{1,0:T(8,128)}) async-done(((f32[64,2560]{1,0:T(8,128)}, f32[64,256]{1,0:T(8,128)}, f32[64,768]{1,0:T(8,128)}), (f32[64,2560]{1,0:T(8,128)}, f32[64,256]{1,0:T(8,128)}, f32[64,768]{1,0:T(8,128)})) %all-reduce.41.cloned.1.call-update) | async-done | bytes 917520 | tf_op jit(solution)/shard_map/psum | solution.py:192
  1239.7 60.5 %all-reduce.11 = (bf16[2560]{0:T(1024)(128)(2,1)S(1)}, bf16[768]{0:T(1024)(128)(2,1)S(1)}, bf16[256]{0:T(256)(128)(2,1)S(1)}, bf16[2560]{0:T(1024)(128)(2,1)S(1)}) all-reduce(bf16[2560]{0:T(1024)(128)(2,1)S(1)} %add_convert_fusion.10, ...), channel_id=2, replica_groups=mesh['section'=2,'tensor'=4,'dp'=16] {'dp'}, use_global_device_ids=true, to_apply=%region_66.67.clone | all-reduce | flops 6144 | bytes 24576
  1308.1 35.8 %reduce-scatter.13.cloned.1.call-done = bf16[160,288]{1,0:T(8,128)(2,1)} async-done(((bf16[2560,288]{1,0:T(8,128)(2,1)}), bf16[160,288]{1,0:T(8,128)(2,1)}) %reduce-scatter.13.cloned.1.call-update) | async-done | bytes 92176 | tf_op jit(solution)/shard_map/reduce_scatter | solution.py:120
  1345.5 77.1 %reduce-scatter.17.cloned.1.call-done = bf16[640,160]{0,1:T(8,128)(2,1)} async-done(((bf16[640,2560]{0,1:T(8,128)(2,1)}), bf16[640,160]{0,1:T(8,128)(2,1)}) %reduce-scatter.17.cloned.1.call-update) | async-done | bytes 204816 | tf_op jit(solution)/shard_map/reduce_scatter | solution.py:129
  1424.4 78.0 %reduce-scatter.9.cloned.1.call-done = bf16[160,768]{1,0:T(8,128)(2,1)} async-done(((bf16[2560,768]{1,0:T(8,128)(2,1)}), bf16[160,768]{1,0:T(8,128)(2,1)}) %reduce-scatter.9.cloned.1.call-update) | async-done | bytes 245776 | tf_op jit(solution)/shard_map/reduce_scatter | solution.py:111
  1504.2 87.5 %reduce-scatter.19.cloned.1.call-done = bf16[160,1600]{1,0:T(8,128)(2,1)} async-done(((bf16[2560,1600]{1,0:T(8,128)(2,1)}), bf16[160,1600]{1,0:T(8,128)(2,1)}) %reduce-scatter.19.cloned.1.call-update) | async-done | bytes 512016 | tf_op jit(solution)/shard_map/reduce_scatter | solution.py:135
  1593.7 86.4 %reduce-scatter.21.cloned.1.call-done = bf16[160,1600]{1,0:T(8,128)(2,1)} async-done(((bf16[2560,1600]{1,0:T(8,128)(2,1)}), bf16[160,1600]{1,0:T(8,128)(2,1)}) %reduce-scatter.21.cloned.1.call-update) | async-done | bytes 512016 | tf_op jit(solution)/shard_map/reduce_scatter | solution.py:138
  1682.2 86.5 %reduce-scatter.23.cloned.1.call-done = bf16[1600,160]{0,1:T(8,128)(2,1)} async-done(((bf16[1600,2560]{0,1:T(8,128)(2,1)}), bf16[1600,160]{0,1:T(8,128)(2,1)}) %reduce-scatter.23.cloned.1.call-update) | async-done | bytes 512016 | tf_op jit(solution)/shard_map/reduce_scatter | solution.py:141
  (808 shorter events, 489.0 us)
Async XLA Ops:
  8.7 146.6 %all-gather.10.cloned.1.call-start = ((), (), s32[]{:S(2)}) async-start(), calls=%async_computation.9 | async-start | bytes 4177920 | tf_op jit(solution)/shard_map/all_gather | solution.py:91
  9.4 195.5 %all-gather.14.cloned.1.call-start = ((), (), s32[]{:S(2)}) async-start(), calls=%async_computation.11 | async-start | bytes 3481600 | tf_op jit(solution)/shard_map/all_gather | solution.py:97
  10.0 240.3 %all-reduce.25.cloned.1.call-start = ((), (), s32[]{:S(2)}) async-start(), calls=%async_computation.12 | async-start | bytes 1310720 | tf_op jit(solution)/shard_map/psum | solution.py:186
  208.9 117.0 %all-gather.16.cloned.1.call-start = ((), (), s32[]{:S(2)}) async-start(), calls=%async_computation.13 | async-start | bytes 9052160 | tf_op jit(solution)/shard_map/all_gather | solution.py:99
  209.5 189.5 %all-gather.18.cloned.1.call-start = ((), (), s32[]{:S(2)}) async-start(), calls=%async_computation.14 | async-start | bytes 9052160 | tf_op jit(solution)/shard_map/all_gather | solution.py:100
  210.2 261.9 %all-gather.20.cloned.1.call-start = ((), (), s32[]{:S(2)}) async-start(), calls=%async_computation.15 | async-start | bytes 9052160 | tf_op jit(solution)/shard_map/all_gather | solution.py:101
  211.0 310.1 %all-reduce.27.cloned.1.call-start = ((), (), s32[]{:S(2)}) async-start(), calls=%async_computation.16 | async-start | bytes 1310720 | tf_op jit(solution)/shard_map/psum | solution.py:192
  479.1 106.3 %all-reduce.29.cloned.1.call-start = ((), (), s32[]{:S(2)}) async-start(), calls=%async_computation.17 | async-start | bytes 1310720 | tf_op jit(solution)/shard_map/psum | solution.py:186
  542.5 105.3 %all-reduce.31.cloned.1.call-start = ((), (), s32[]{:S(2)}) async-start(), calls=%async_computation.18 | async-start | bytes 1310720 | tf_op jit(solution)/shard_map/psum | solution.py:192
  603.3 110.6 %all-reduce.33.cloned.1.call-start = ((), (), s32[]{:S(2)}) async-start(), calls=%async_computation.19 | async-start | bytes 1310720 | tf_op jit(solution)/shard_map/psum | solution.py:186
  671.6 103.3 %all-reduce.35.cloned.1.call-start = ((), (), s32[]{:S(2)}) async-start(), calls=%async_computation.20 | async-start | bytes 1310720 | tf_op jit(solution)/shard_map/psum | solution.py:243
  730.4 109.3 %all-reduce.45.cloned.1.call-start = ((), (), s32[]{:S(2)}) async-start(), calls=%async_computation.33 | async-start | bytes 524288 | tf_op jit(solution)/shard_map/psum | solution.py:282
  797.3 116.1 %all-reduce.37.cloned.1.call-start = ((), (), s32[]{:S(2)}) async-start(), calls=%async_computation.21 | async-start | bytes 1310720 | tf_op jit(solution)/shard_map/psum | solution.py:243
  871.2 107.1 %all-reduce.43.cloned.1.call-start = ((), (), s32[]{:S(2)}) async-start(), calls=%async_computation.32 | async-start | bytes 524288 | tf_op jit(solution)/shard_map/psum | solution.py:282
  935.9 116.1 %all-reduce.39.cloned.1.call-start = ((), (), s32[]{:S(2)}) async-start(), calls=%async_computation.22 | async-start | bytes 1310720 | tf_op jit(solution)/shard_map/psum | solution.py:243
  1009.7 105.1 %all-reduce.41.cloned.1.call-start = ((), (), s32[]{:S(2)}) async-start(), calls=%async_computation.31 | async-start | bytes 1835008 | tf_op jit(solution)/shard_map/psum | solution.py:192
  1068.2 236.8 %reduce-scatter.15.cloned.1.call-start = ((), (), s32[]{:S(2)}) async-start(), calls=%async_computation.26 | async-start | bytes 696320 | tf_op jit(solution)/shard_map/reduce_scatter | solution.py:126
  1071.9 234.7 %reduce-scatter.11.cloned.1.call-start = ((), (), s32[]{:S(2)}) async-start(), calls=%async_computation.24 | async-start | bytes 1671168 | tf_op jit(solution)/shard_map/reduce_scatter | solution.py:117
  1075.2 268.7 %reduce-scatter.13.cloned.1.call-start = ((), (), s32[]{:S(2)}) async-start(), calls=%async_computation.25 | async-start | bytes 2088960 | tf_op jit(solution)/shard_map/reduce_scatter | solution.py:120
  1121.2 301.5 %reduce-scatter.17.cloned.1.call-start = ((), (), s32[]{:S(2)}) async-start(), calls=%async_computation.27 | async-start | bytes 3481600 | tf_op jit(solution)/shard_map/reduce_scatter | solution.py:129
  1126.5 375.9 %reduce-scatter.9.cloned.1.call-start = ((), (), s32[]{:S(2)}) async-start(), calls=%async_computation.23 | async-start | bytes 4177920 | tf_op jit(solution)/shard_map/reduce_scatter | solution.py:111
  1132.8 458.8 %reduce-scatter.19.cloned.1.call-start = ((), (), s32[]{:S(2)}) async-start(), calls=%async_computation.28 | async-start | bytes 9052160 | tf_op jit(solution)/shard_map/reduce_scatter | solution.py:135
  1166.2 513.9 %reduce-scatter.21.cloned.1.call-start = ((), (), s32[]{:S(2)}) async-start(), calls=%async_computation.29 | async-start | bytes 9052160 | tf_op jit(solution)/shard_map/reduce_scatter | solution.py:138
  1199.3 569.4 %reduce-scatter.23.cloned.1.call-start = ((), (), s32[]{:S(2)}) async-start(), calls=%async_computation.30 | async-start | bytes 9052160 | tf_op jit(solution)/shard_map/reduce_scatter | solution.py:141
  (242 other events, 4310.5 us)
Sparse Core Ops, SparseCore 0:
  10.2 46.0 all-gather.11
  58.5 44.0 all-gather.7
  104.7 50.4 all-gather.9
  157.3 47.6 all-gather.13
  252.3 73.4 all-gather.15
  328.1 70.9 all-gather.17
  401.2 70.9 all-gather.19
  542.7 42.7 all-reduce.28
  603.4 44.3 all-reduce.30
  671.8 42.1 all-reduce.32
  730.5 44.4 all-reduce.34
  797.4 42.1 all-reduce.44
  871.3 42.1 all-reduce.36
  936.0 42.2 all-reduce.42
  1009.8 42.0 all-reduce.38
  1068.3 46.4 all-reduce.40
  1117.9 73.2 reduce-scatter.14
  1194.3 73.0 reduce-scatter.10
  1270.6 73.2 reduce-scatter.12
  1347.6 74.9 reduce-scatter.16
  1426.4 75.9 reduce-scatter.8
  1506.1 85.5 reduce-scatter.18
  1595.1 84.9 reduce-scatter.20
  1683.8 84.8 reduce-scatter.22
  (2 shorter events, 83.0 us)
where the time goes:
time: 1790 us; the launch traced here: 1780 us
  waiting for transfers between devices  1160 us (65%)
  matrix products  290 us (16%)
  blocking collectives  181 us (10%)
  other arithmetic  81.6 us (5%)
  local copies, waits for them, and re-layouts  28.7 us (2%)
  between operations  22.1 us (1%)
    dot_general x24, matrix products, product_left(): lax.dot_general(left_side, right_side, (((0,), (0,)), ((), ())), preferre...  122 us
    psum x3, waiting for transfers between devices, layer_backward(): lax.psum(product_right(d_gate, w_gate) + product_right(d_up, w_up), 'tens...  122 us
    unnamed x2, blocking collectives  119 us
    psum x3, waiting for transfers between devices, layer_forward(): attended = lax.psum(product(mixed_heads, w_o), 'tensor')  118 us
    psum x3, waiting for transfers between devices, layer_forward(): mlp_out = lax.psum(product(hidden, w_down), 'tensor')  108 us
    reduce_scatter x1, waiting for transfers between devices, spread_end(): lax.psum_scatter(weight_grads[9].astype(jnp.bfloat16), 'dp', scatter_dime...  87.5 us
    reduce_scatter x1, waiting for transfers between devices, spread_end(): lax.psum_scatter(weight_grads[11].astype(jnp.bfloat16), 'dp', scatter_dim...  86.5 us
    reduce_scatter x1, waiting for transfers between devices, spread_end(): lax.psum_scatter(weight_grads[10].astype(jnp.bfloat16), 'dp', scatter_dim...  86.4 us
  transfers between devices with their start and end apart: 30, of which 26 were waited for; matrix products, arithmetic and copies ran while one was open for 11% of the time, Pallas kernels for 0%

commit v1 on v0

v1 whole, which is shorter than its diff:
```python
import math

import jax
import jax.numpy as jnp
from jax import lax
from jax.experimental import pallas as pl
from jax.experimental.pallas import tpu as pltpu
from jax.sharding import PartitionSpec as P

D = 2560
NOPE = 64
ROPE = 32
VD = 64
QR = 768
KVR = 256
PACK = 64
MB = 2
N_DP = 16
N_Z = 4
HEADS = 5
SLICE = D // N_DP
FF_PART = 100
LANES = 128
SHARD = 16
RES_SCALE = 1.4 / math.sqrt(62.0)
EPSILON = 1e-05
SCORE_SCALE = (NOPE + ROPE) ** (-0.5)
BF16 = jnp.bfloat16
F32 = jnp.float32


def dot(a, b):
    return jnp.dot(a, b, preferred_element_type=F32)


def dot_tn(a, b):
    return lax.dot_general(a, b, (((0,), (0,)), ((), ())), preferred_element_type=F32)


def dot_nt(a, b):
    return lax.dot_general(a, b, (((1,), (1,)), ((), ())), preferred_element_type=F32)


def to_core(x):
    return lax.ppermute(x, "section", [(0, 1), (1, 0)])


def z_hop(x, by):
    return lax.ppermute(x, "tensor", [(i, (i + by) % N_Z) for i in range(N_Z)])


def by_core(core, mine, other):
    return jnp.where(core == 0, mine, other), jnp.where(core == 0, other, mine)


def from_here(x):
    return lax.dynamic_slice_in_dim(jnp.concatenate([x, x]), lax.axis_index("tensor"), N_Z, 0)


def from_zero(x):
    at = (N_Z - lax.axis_index("tensor")) % N_Z
    return lax.dynamic_slice_in_dim(jnp.concatenate([x, x]), at, N_Z, 0)


def gather_z(x):
    return [x, z_hop(x, -1), z_hop(x, 2), z_hop(x, 1)]


def gather_tokens(x):
    mine = jnp.concatenate(gather_z(x), axis=0)
    return mine, to_core(mine)


def in_order(mine, other):
    core = lax.axis_index("section")
    shape = (N_Z, SHARD, mine.shape[-1])
    mine, other = from_zero(mine.reshape(shape)), from_zero(other.reshape(shape))
    return jnp.concatenate(by_core(core, mine, other), axis=0).reshape(-1, shape[-1])


def scatter_tokens(part):
    half = part[:PACK].astype(F32) + to_core(part[PACK:]).astype(F32)
    sent = half.astype(BF16)
    total = half[:SHARD]
    for by in (2, 1, 3):
        total = total + z_hop(sent[SHARD * by : SHARD * (by + 1)], by).astype(F32)
    return total


def gather_dp(x):
    copies = jnp.broadcast_to(x[None], (N_DP,) + x.shape)
    return lax.all_to_all(copies, "dp", 0, 0).reshape(N_DP * x.shape[0], x.shape[1])


def scatter_dp(part):
    pieces = lax.all_to_all(part.reshape(N_DP, SHARD, D), "dp", 0, 0)
    return jnp.sum(pieces.astype(F32), axis=0)


def norm_scale(x):
    return lax.rsqrt(jnp.mean(x * x, axis=-1, keepdims=True) + EPSILON)


def norm(x, gain):
    return x * norm_scale(x) * gain


def norm_back(x, gain, d):
    q = norm_scale(x)
    along = jnp.mean(gain * d * x, axis=-1, keepdims=True)
    return q * gain * d - x * (q * q * q) * along, jnp.sum(d * x * q, axis=0)


MATS = 3 * LANES
TOKENS = N_DP * SHARD
FF_VMEM = 56 * 1024 * 1024
FF_SCRATCH = [
    pltpu.VMEM((N_Z, D, MATS), BF16),
    pltpu.VMEM((TOKENS, D), F32),
    pltpu.SemaphoreType.DMA((N_Z,)),
]


def ffn_copies(own_ref, mine, other, w_ref, sems):
    copies = [pltpu.make_async_copy(mine[z], w_ref.at[z], sems.at[z]) for z in range(N_Z)]
    others = [pltpu.make_async_copy(other[z], w_ref.at[z], sems.at[z]) for z in range(N_Z)]

    @pl.when(own_ref[0] == 1)
    def _():
        for copy in copies:
            copy.start()

    @pl.when(own_ref[0] != 1)
    def _():
        for copy in others:
            copy.start()

    return copies


def ffn_forward_kernel(own_ref, n_ref, *refs):
    mine, other = refs[:N_Z], refs[N_Z : 2 * N_Z]
    part_ref, gu_ref, hid_ref, w_ref, acc_ref, sems = refs[2 * N_Z :]
    copies = ffn_copies(own_ref, mine, other, w_ref, sems)
    for z in range(N_Z):
        copies[z].wait()
        gu = dot(n_ref[...], w_ref[z, :, : 2 * LANES])
        gu_ref[:, 2 * LANES * z : 2 * LANES * (z + 1)] = gu
        gate, up = gu[:, :LANES], gu[:, LANES:]
        hidden = (gate * jax.nn.sigmoid(gate) * up).astype(BF16)
        hid_ref[:, LANES * z : LANES * (z + 1)] = hidden
        out = dot_nt(hidden, w_ref[z, :, 2 * LANES :])
        if z == 0:
            acc_ref[...] = out
        elif z < N_Z - 1:
            acc_ref[...] += out
        else:
            part_ref[...] = (acc_ref[...] + out).astype(BF16)


def ffn_specs(arrays):
    vmem = pl.BlockSpec(memory_space=pltpu.VMEM)
    smem = pl.BlockSpec(memory_space=pltpu.SMEM)
    return [smem] + [vmem] * arrays + [pl.BlockSpec(memory_space=pl.ANY)] * (2 * N_Z)


def ffn_forward(own, rows, weights):
    return pl.pallas_call(
        ffn_forward_kernel,
        out_shape=(
            jax.ShapeDtypeStruct((TOKENS, D), BF16),
            jax.ShapeDtypeStruct((TOKENS, 2 * LANES * N_Z), F32),
            jax.ShapeDtypeStruct((TOKENS, LANES * N_Z), BF16),
        ),
        in_specs=ffn_specs(1),
        out_specs=(pl.BlockSpec(memory_space=pltpu.VMEM),) * 3,
        scratch_shapes=FF_SCRATCH,
        compiler_params=pltpu.CompilerParams(vmem_limit_bytes=FF_VMEM),
        name="ffn_forward",
    )(own, rows, *weights)


def ffn_backward_kernel(own_ref, dm_ref, n_ref, gu_ref, hid_ref, *refs):
    mine, other, part_ref = refs[:N_Z], refs[N_Z : 2 * N_Z], refs[2 * N_Z]
    grads = refs[2 * N_Z + 1 : 3 * N_Z + 1]
    w_ref, acc_ref, sems = refs[3 * N_Z + 1 :]
    copies = ffn_copies(own_ref, mine, other, w_ref, sems)
    for z in range(N_Z):
        hidden = hid_ref[:, LANES * z : LANES * (z + 1)]
        grads[z][:, 2 * LANES :] = dot_tn(dm_ref[...], hidden).astype(BF16)
        copies[z].wait()
        d_hidden = dot(dm_ref[...], w_ref[z, :, 2 * LANES :])
        gate = gu_ref[:, 2 * LANES * z : 2 * LANES * z + LANES]
        up = gu_ref[:, 2 * LANES * z + LANES : 2 * LANES * (z + 1)]
        s = jax.nn.sigmoid(gate)
        d_gate = d_hidden * up * (s + gate * s * (1.0 - s))
        d_up = d_hidden * (gate * s)
        d_gu = jnp.concatenate([d_gate.astype(BF16), d_up.astype(BF16)], axis=1)
        grads[z][:, : 2 * LANES] = dot_tn(n_ref[...], d_gu).astype(BF16)
        out = dot_nt(d_gu, w_ref[z, :, : 2 * LANES])
        if z == 0:
            acc_ref[...] = out
        elif z < N_Z - 1:
            acc_ref[...] += out
        else:
            part_ref[...] = (acc_ref[...] + out).astype(BF16)


def ffn_backward(own, d_rows, rows, gu, hidden, weights):
    out = pl.pallas_call(
        ffn_backward_kernel,
        out_shape=(jax.ShapeDtypeStruct((TOKENS, D), BF16),)
        + tuple(jax.ShapeDtypeStruct((D, MATS), BF16) for _ in range(N_Z)),
        in_specs=ffn_specs(4),
        out_specs=(pl.BlockSpec(memory_space=pltpu.VMEM),) * (N_Z + 1),
        scratch_shapes=FF_SCRATCH,
        compiler_params=pltpu.CompilerParams(vmem_limit_bytes=FF_VMEM),
        name="ffn_backward",
    )(own, d_rows, rows, gu, hidden, *weights)
    return out[0], out[1:]


FF = N_DP * FF_PART
WINDOW = 2 * LANES
FF_PADDED = (FF - FF_PART) // LANES * LANES + WINDOW


def identity(n):
    at = lax.broadcasted_iota(jnp.int32, (n, n), 0)
    return jnp.where(at == lax.broadcasted_iota(jnp.int32, (n, n), 1), 1.0, 0.0).astype(BF16)


def ffn_pack_kernel(gate_ref, up_ref, down_ref, out_ref, wide_ref):
    wide_ref[0, :, :FF] = gate_ref[...].astype(F32)
    wide_ref[1, :, :FF] = up_ref[...].astype(F32)
    wide_ref[2, :, :FF] = dot_nt(identity(SLICE), down_ref[...])
    valid = lax.broadcasted_iota(jnp.int32, (SLICE, LANES), 1) < FF_PART
    for p in range(N_DP):
        at = FF_PART * p // LANES * LANES
        by = FF_PART * p - at
        for m in range(3):
            window = wide_ref[m, :, at : at + WINDOW]
            if by > 0:
                window = pltpu.roll(window, WINDOW - by, 1)
            block = jnp.where(valid, window[:, :LANES], 0.0)
            out_ref[p, :, LANES * m : LANES * (m + 1)] = block.astype(BF16)


def ffn_pack(w_gate, w_up, w_down):
    return pl.pallas_call(
        ffn_pack_kernel,
        out_shape=jax.ShapeDtypeStruct((N_DP, SLICE, MATS), BF16),
        scratch_shapes=[pltpu.VMEM((3, SLICE, FF_PADDED), F32)],
        compiler_params=pltpu.CompilerParams(vmem_limit_bytes=FF_VMEM),
        name="ffn_pack",
    )(w_gate, w_up, w_down)


def ffn_unpack_kernel(in_ref, gate_ref, up_ref, down_ref, wide_ref):
    wide_ref[...] = jnp.zeros(wide_ref.shape, F32)
    valid = lax.broadcasted_iota(jnp.int32, (SLICE, LANES), 1) < FF_PART
    for p in range(N_DP):
        at = FF_PART * p // LANES * LANES
        by = FF_PART * p - at
        for m in range(3):
            block = in_ref[p, :, LANES * m : LANES * (m + 1)].astype(F32)
            block = jnp.where(valid, block, 0.0)
            window = jnp.concatenate([block, jnp.zeros_like(block)], axis=1)
            if by > 0:
                window = pltpu.roll(window, by, 1)
            wide_ref[m, :, at : at + WINDOW] += window
    gate_ref[...] = wide_ref[0, :, :FF]
    up_ref[...] = wide_ref[1, :, :FF]
    down_ref[...] = dot_tn(wide_ref[2, :, :FF].astype(BF16), identity(SLICE))


def ffn_unpack(blocks):
    return pl.pallas_call(
        ffn_unpack_kernel,
        out_shape=(
            jax.ShapeDtypeStruct((SLICE, FF), F32),
            jax.ShapeDtypeStruct((SLICE, FF), F32),
            jax.ShapeDtypeStruct((FF, SLICE), F32),
        ),
        scratch_shapes=[pltpu.VMEM((3, SLICE, FF_PADDED), F32)],
        compiler_params=pltpu.CompilerParams(vmem_limit_bytes=FF_VMEM),
        name="ffn_unpack",
    )(blocks)


A_ROWS = SLICE + QR // N_DP + KVR // N_DP
A_COLS = 896
LAT = 640
WO_AT = 512
WO = 384
HEAD = 128
ROWS = MB * PACK
QB_ROWS = slice(SLICE, SLICE + QR // N_DP)
KVB_ROWS = slice(SLICE + QR // N_DP, A_ROWS)
E_ROWS = 2 * A_ROWS - SLICE
ATT_VMEM = 48 * 1024 * 1024


def latent_kernel(mine_ref, other_ref, gain_ref, pack_ref, normed_ref, lat_ref, w_ref, sem):
    copy = pltpu.make_async_copy(pack_ref.at[:, 0:SLICE, 0:LAT], w_ref, sem)
    copy.start()
    normed_ref[:PACK] = norm(mine_ref[...].astype(F32), gain_ref[...]).astype(BF16)
    normed_ref[PACK:] = norm(other_ref[...].astype(F32), gain_ref[...]).astype(BF16)
    copy.wait()
    lat_ref[...] = dot(normed_ref[...], w_ref[...].reshape(D, LAT))


def latents(rows, gain, pack):
    vmem = pl.BlockSpec(memory_space=pltpu.VMEM)
    return pl.pallas_call(
        latent_kernel,
        out_shape=(
            jax.ShapeDtypeStruct((ROWS, D), BF16),
            jax.ShapeDtypeStruct((ROWS, LAT), F32),
        ),
        in_specs=[vmem, vmem, vmem, pl.BlockSpec(memory_space=pl.ANY)],
        out_specs=(vmem, vmem),
        scratch_shapes=[pltpu.VMEM((N_DP, SLICE, LAT), BF16), pltpu.SemaphoreType.DMA],
        compiler_params=pltpu.CompilerParams(vmem_limit_bytes=ATT_VMEM),
        name="latents",
    )(*rows, gain, pack)


def weight_copies(pack_ref, qb_ref, kvb_ref, wo_ref, sems):
    sources = (
        pack_ref.at[:, QB_ROWS, 0:LAT],
        pack_ref.at[:, KVB_ROWS, 0:LAT],
        pack_ref.at[:, 0:SLICE, WO_AT : WO_AT + WO],
    )
    targets = (qb_ref, kvb_ref, wo_ref)
    copies = [pltpu.make_async_copy(a, b, sems.at[i]) for i, (a, b) in enumerate(zip(sources, targets))]
    for copy in copies:
        copy.start()
    return copies


def weight_scratch():
    return [
        pltpu.VMEM((N_DP, QR // N_DP, LAT), BF16),
        pltpu.VMEM((N_DP, KVR // N_DP, LAT), BF16),
        pltpu.VMEM((N_DP, SLICE, WO), BF16),
        pltpu.SemaphoreType.DMA((3,)),
    ]


def lanes_of(x):
    return lax.broadcasted_iota(jnp.int32, x.shape, 1)


def turn(x, tab_ref):
    return (
        x * tab_ref[0]
        + pltpu.roll(x, HEAD - ROPE // 2, 1) * tab_ref[1]
        + pltpu.roll(x, ROPE // 2, 1) * tab_ref[2]
    )


def turn_back(x, tab_ref):
    return (
        x * tab_ref[0]
        - pltpu.roll(x, HEAD - ROPE // 2, 1) * tab_ref[1]
        - pltpu.roll(x, ROPE // 2, 1) * tab_ref[2]
    )


def head_columns(h):
    return slice(HEAD * h, HEAD * (h + 1))


def probs_of(query, key, tab_ref):
    scores = jnp.where(tab_ref[3] < 0.0, -1e30, dot_nt(query, key) * SCORE_SCALE)
    weight = jnp.exp(scores - jnp.max(scores, axis=-1, keepdims=True))
    return weight / jnp.sum(weight, axis=-1, keepdims=True)


def attend_kernel(
    core_ref, mine_ref, other_ref, tab_ref, gq_ref, gkv_ref, pack_ref,
    part_ref, sq_ref, comp_ref, q_ref, kv_ref, kr_ref, mixed_ref, lat_ref,
    qb_ref, kvb_ref, wo_ref, sems,
):
    copies = weight_copies(pack_ref, qb_ref, kvb_ref, wo_ref, sems)
    zero = core_ref[0] == 0
    other = jnp.concatenate([other_ref[PACK:], other_ref[:PACK]], axis=0)
    second = jnp.where(zero, other, mine_ref[...])
    first = jnp.where(zero, mine_ref[:, :512], other[:, :512])
    latent_q = jnp.concatenate([first, second[:, :256]], axis=1)
    lat_ref[:, :QR] = latent_q[:SHARD]
    lat_ref[:, QR:] = second[:SHARD, 256:512]
    sq_ref[...] = norm(latent_q, gq_ref[...]).astype(BF16)
    comp_ref[...] = norm(second[:, 256:512], gkv_ref[...]).astype(BF16)
    rope = pltpu.roll(second[:, 512:640], NOPE, 1)
    rope = jnp.where(lanes_of(rope) < NOPE, 0.0, turn(rope, tab_ref)).astype(BF16)
    kr_ref[...] = rope
    copies[0].wait()
    query = dot(sq_ref[...], qb_ref[...].reshape(QR, LAT))
    for h in range(HEADS):
        q_ref[:, head_columns(h)] = turn(query[:, head_columns(h)], tab_ref).astype(BF16)
    copies[1].wait()
    kv_ref[...] = dot(comp_ref[...], kvb_ref[...].reshape(KVR, LAT)).astype(BF16)
    heads = []
    for h in range(HEADS):
        kv = kv_ref[:, head_columns(h)]
        key = jnp.where(lanes_of(kv) < NOPE, kv, rope)
        probs = probs_of(q_ref[:, head_columns(h)], key, tab_ref)
        heads.append(dot(probs.astype(BF16), kv))
    low = lanes_of(heads[0]) < NOPE
    tiles = [jnp.where(low, 0.0, heads[0])]
    tiles += [jnp.where(low, pltpu.roll(heads[i], NOPE, 1), heads[i + 1]) for i in (1, 3)]
    mixed_ref[...] = jnp.concatenate(tiles, axis=1).astype(BF16)
    copies[2].wait()
    part_ref[...] = dot_nt(mixed_ref[...], wo_ref[...].reshape(D, WO)).astype(BF16)


def attend(core, mine, other, tab, g_q, g_kv, pack):
    vmem = pl.BlockSpec(memory_space=pltpu.VMEM)
    widths = (D, QR, KVR, LAT, LAT, HEAD, WO)
    return pl.pallas_call(
        attend_kernel,
        out_shape=tuple(jax.ShapeDtypeStruct((ROWS, w), BF16) for w in widths)
        + (jax.ShapeDtypeStruct((SHARD, QR + KVR), F32),),
        in_specs=[pl.BlockSpec(memory_space=pltpu.SMEM)] + [vmem] * 5 + [pl.BlockSpec(memory_space=pl.ANY)],
        out_specs=(vmem,) * (len(widths) + 1),
        scratch_shapes=weight_scratch(),
        compiler_params=pltpu.CompilerParams(vmem_limit_bytes=ATT_VMEM),
        name="attend",
    )(core, mine, other, tab, g_q, g_kv, pack)


def attend_back_kernel(
    mine_ref, other_ref, tab_ref, sq_ref, comp_ref, q_ref, kv_ref, kr_ref, mixed_ref, pack_ref,
    part_ref, early_ref,
    dq_ref, dkv_ref, qb_ref, kvb_ref, wo_ref, sems,
):
    copies = weight_copies(pack_ref, qb_ref, kvb_ref, wo_ref, sems)
    d_att = jnp.concatenate([mine_ref[...], other_ref[...]], axis=0)
    wo_grad = dot_tn(d_att, mixed_ref[...]).astype(BF16)
    early_ref[:, :SLICE, :] = wo_grad.reshape(N_DP, SLICE, WO)
    copies[2].wait()
    d_mixed = dot(d_att, wo_ref[...].reshape(D, WO))
    rope = kr_ref[...]
    d_rope = jnp.zeros((ROWS, HEAD), F32)
    for h in range(HEADS):
        kv = kv_ref[:, head_columns(h)]
        low = lanes_of(kv) < NOPE
        key = jnp.where(low, kv, rope)
        query = q_ref[:, head_columns(h)]
        probs = probs_of(query, key, tab_ref)
        tile = d_mixed[:, head_columns((h + 1) // 2)]
        if h % 2 == 1:
            tile = pltpu.roll(tile, NOPE, 1)
        tile = jnp.where(low, 0.0, tile).astype(BF16)
        d_probs = dot_nt(tile, kv)
        d_scores = probs * (d_probs - jnp.sum(probs * d_probs, axis=-1, keepdims=True))
        d_scores = d_scores.astype(BF16)
        d_query = dot(d_scores, key) * SCORE_SCALE
        d_key = dot_tn(d_scores, query) * SCORE_SCALE
        d_value = dot_tn(probs.astype(BF16), tile)
        dq_ref[:, head_columns(h)] = turn_back(d_query, tab_ref).astype(BF16)
        dkv_ref[:, head_columns(h)] = jnp.where(low, d_key, d_value).astype(BF16)
        d_rope = d_rope + d_key
    d_rope = jnp.where(lanes_of(d_rope) < NOPE, 0.0, turn_back(jnp.where(lanes_of(d_rope) < NOPE, 0.0, d_rope), tab_ref))
    copies[0].wait()
    copies[1].wait()
    part_ref[:, :QR] = dot_nt(dq_ref[...], qb_ref[...].reshape(QR, LAT)).astype(BF16)
    part_ref[:, QR : QR + KVR] = dot_nt(dkv_ref[...], kvb_ref[...].reshape(KVR, LAT)).astype(BF16)
    part_ref[:, QR + KVR :] = d_rope.astype(BF16)
    qb_grad = dot_tn(sq_ref[...], dq_ref[...]).astype(BF16).reshape(N_DP, QR // N_DP, LAT)
    kvb_grad = dot_tn(comp_ref[...], dkv_ref[...]).astype(BF16).reshape(N_DP, KVR // N_DP, LAT)
    early_ref[:, QB_ROWS, :] = qb_grad[:, :, :WO]
    early_ref[:, KVB_ROWS, :] = kvb_grad[:, :, :WO]
    more = slice(A_ROWS, A_ROWS + QR // N_DP)
    early_ref[:, more, : LAT - WO] = qb_grad[:, :, WO:]
    early_ref[:, more.stop :, : LAT - WO] = kvb_grad[:, :, WO:]
    early_ref[:, A_ROWS:, LAT - WO :] = jnp.zeros((N_DP, E_ROWS - A_ROWS, 2 * WO - LAT), BF16)


def attend_back(d_attended, tab, saved, pack):
    vmem = pl.BlockSpec(memory_space=pltpu.VMEM)
    return pl.pallas_call(
        attend_back_kernel,
        out_shape=(
            jax.ShapeDtypeStruct((ROWS, QR + KVR + HEAD), BF16),
            jax.ShapeDtypeStruct((N_DP, E_ROWS, WO), BF16),
        ),
        in_specs=[vmem] * 9 + [pl.BlockSpec(memory_space=pl.ANY)],
        out_specs=(vmem,) * 2,
        scratch_shapes=[pltpu.VMEM((ROWS, LAT), BF16), pltpu.VMEM((ROWS, LAT), BF16)] + weight_scratch(),
        compiler_params=pltpu.CompilerParams(vmem_limit_bytes=ATT_VMEM),
        name="attend_back",
    )(*d_attended, tab, *saved, pack)


def normed_back_kernel(d_ref, pack_ref, out_ref, w_ref, sem):
    copy = pltpu.make_async_copy(pack_ref.at[:, 0:SLICE, 0:LAT], w_ref, sem)
    copy.start()
    copy.wait()
    out_ref[...] = dot_nt(d_ref[...], w_ref[...].reshape(D, LAT))


def normed_back(d_latent, pack):
    vmem = pl.BlockSpec(memory_space=pltpu.VMEM)
    return pl.pallas_call(
        normed_back_kernel,
        out_shape=jax.ShapeDtypeStruct((d_latent.shape[0], D), F32),
        in_specs=[vmem, pl.BlockSpec(memory_space=pl.ANY)],
        out_specs=vmem,
        scratch_shapes=[pltpu.VMEM((N_DP, SLICE, LAT), BF16), pltpu.SemaphoreType.DMA],
        compiler_params=pltpu.CompilerParams(vmem_limit_bytes=ATT_VMEM),
        name="normed_back",
    )(d_latent, pack)


def attention_packs(w_qa, w_qb, w_kva, w_kvb, w_o, gains):
    def pad(x, width, at=0):
        return jnp.pad(x, ((0, 0), (at, width - at - x.shape[1])))

    wo_t = w_o.T
    half = HEADS * VD
    latent = (w_qa[:, :512], jnp.concatenate([w_qa[:, 512:], w_kva], axis=1))
    qb = w_qb.reshape(QR // N_DP, 2, HEADS, NOPE + ROPE)
    qb = jnp.pad(qb, ((0, 0), (0, 0), (0, 0), (0, HEAD - NOPE - ROPE)))
    qb = qb.reshape(QR // N_DP, 2, LAT)
    kvb = w_kvb.reshape(KVR // N_DP, 2, LAT)
    packs = []
    for i in range(2):
        wide = jnp.concatenate([pad(latent[i], A_COLS - half), wo_t[:, half * i : half * (i + 1)]], axis=1)
        low = jnp.concatenate([qb[:, i], gains], axis=1)
        packs.append(jnp.concatenate([wide, low, pad(kvb[:, i], A_COLS)], axis=0))
    return jnp.stack(packs)


def attention_gains(pack):
    gains = pack[:, SLICE : SLICE + 3, LAT:].astype(F32)
    return dict(
        attn=gains[:, 0, :SLICE].reshape(1, D),
        ffn=gains[:, 1, :SLICE].reshape(1, D),
        q=gains[:, 2, : QR // N_DP].reshape(1, QR),
        kv=gains[:, 2, QR // N_DP : QR // N_DP + KVR // N_DP].reshape(1, KVR),
    )


def head_tables(seq_lengths):
    core, t = lax.axis_index("section"), lax.axis_index("tensor")
    at = jnp.arange(ROWS, dtype=jnp.int32)
    pack = (core + at // PACK) % 2
    row = (t + at % PACK // SHARD) % N_Z * SHARD + at % SHARD
    lengths = jnp.where(pack[:, None] == 0, seq_lengths[:1], seq_lengths[1:])
    past_end = row[:, None] >= jnp.cumsum(lengths, axis=1)
    segment = jnp.sum(past_end.astype(jnp.int32), axis=1)
    position = (row - jnp.sum(jnp.where(past_end, lengths, 0), axis=1)).astype(F32)
    frequency = 10000.0 ** (-2.0 * jnp.arange(ROPE // 2, dtype=F32) / ROPE)
    angles = position[:, None] * frequency[None, :]
    cosine, sine = jnp.cos(angles), jnp.sin(angles)
    sequence = pack * PACK + segment
    allowed = (sequence[:, None] == sequence[None, :]) & (row[None, :] <= row[:, None])

    def tile(*pieces):
        x = jnp.concatenate(pieces, axis=1)
        return jnp.pad(x, ((0, 0), (0, HEAD - x.shape[1])))

    ones, none = jnp.ones((ROWS, NOPE), F32), jnp.zeros((ROWS, NOPE), F32)
    bias = jnp.where(allowed, 0.0, -1.0).astype(F32)
    return jnp.stack(
        [tile(ones, cosine, cosine), tile(none, -sine), tile(none, jnp.zeros_like(sine), sine), bias]
    )


def ring_hop(x, by, cores=(0, 1)):
    pairs = [
        (c * N_Z + t, c * N_Z + (t + (by if c == 0 else -by)) % N_Z) for c in cores for t in range(N_Z)
    ]
    return lax.ppermute(x, ("section", "tensor"), pairs)


def ring_pieces(x):
    near = ring_hop(x, 1)
    return [x, near, ring_hop(x, -1), ring_hop(near, 1)]


def ring_sum(layer, pieces):
    def add(*terms):
        return sum(x.astype(F32) for x in terms).astype(BF16)

    pair = [(1 - layer, layer)]
    far, near, after, mine = (
        add(pieces[k], lax.ppermute(pieces[k], "section", pair)) for k in (3, 1, 2, 0)
    )
    cores = (layer,)
    near = add(near, ring_hop(far, -1, cores))
    return add(mine, ring_hop(near, -1, cores), ring_hop(after, 1, cores))


def layer_forward(own, rows, x_own, pack, gains, ffn_weights, tab):
    core = lax.axis_index("section").reshape(1)
    normed, latent = latents(rows, gains["attn"], pack)
    part, *saved, latent_own = attend(
        core, latent, to_core(latent), tab, gains["q"], gains["kv"], pack
    )
    middle = x_own + RES_SCALE * scatter_tokens(part)
    ffn_rows = gather_dp(norm(middle, gains["ffn"]).astype(BF16))
    part, gu, hidden = ffn_forward(own, ffn_rows, ffn_weights)
    return part, (x_own, middle, ffn_rows, gu, hidden, normed, latent_own, saved)


def layer_out_rows(part, saved):
    return (saved[1] + RES_SCALE * scatter_dp(part)).astype(BF16)


def layer_backward(own, grad_own, d_rows, saved, pack, gains, ffn_weights, tab, after_gather):
    core = lax.axis_index("section")
    t = lax.axis_index("tensor")
    x_own, middle, ffn_rows, gu, hidden, normed, latent_own, saved = saved
    part, ffn_grads = ffn_backward(own, d_rows, ffn_rows, gu, hidden, ffn_weights)
    d_normed_two = scatter_dp(part)
    d_middle, ffn_gain = norm_back(middle, gains["ffn"], d_normed_two)
    d_middle = d_middle + grad_own
    d_attended = gather_tokens((RES_SCALE * d_middle).astype(BF16))
    d_attended, after_gather = lax.optimization_barrier((d_attended, after_gather))
    part, early = attend_back(d_attended, tab, saved, pack)
    d_latent = scatter_tokens(part)
    d_q, q_gain = norm_back(latent_own[:, :QR], gains["q"], d_latent[:, :QR])
    d_c, kv_gain = norm_back(latent_own[:, QR:], gains["kv"], d_latent[:, QR : QR + KVR])
    d_rope = d_latent[:, QR + KVR + NOPE : QR + KVR + NOPE + ROPE]
    blank = jnp.zeros((SHARD, HEAD), F32)
    d_first = jnp.concatenate([d_q[:, :512], blank], axis=1).astype(BF16)
    d_second = jnp.concatenate([d_q[:, 512:], d_c, d_rope, blank[:, ROPE:]], axis=1).astype(BF16)
    mine = jnp.where(core == 0, d_first, d_second)
    other = to_core(jnp.where(core == 0, d_second, d_first))
    both = jnp.concatenate([mine, other], axis=0)
    part = normed_back(both, pack)
    d_normed = part[:SHARD] + to_core(part[SHARD:])
    d_block, attn_gain = norm_back(x_own, gains["attn"], d_normed)
    d_block = (d_block + d_middle).astype(BF16)
    columns = both.reshape(2 * SHARD, LAT // HEAD, HEAD).transpose(1, 0, 2)

    def piece(by):
        tile = lax.dynamic_index_in_dim(columns, (t + by) % N_Z, 0, keepdims=False)
        return jnp.concatenate([tile, columns[N_Z]], axis=1)

    rows = jnp.stack([piece(0), z_hop(piece(3), -1), z_hop(piece(2), 2), z_hop(piece(1), 1)])
    rows = rows.reshape(N_Z, 2, SHARD, 2 * HEAD).transpose(1, 0, 2, 3).reshape(ROWS, 2 * HEAD)
    down_grad = dot_tn(normed, rows).astype(BF16).reshape(N_DP, SLICE, 2 * HEAD)
    return d_block, ffn_grads, early, down_grad, (attn_gain, ffn_gain, q_gain, kv_gain), after_gather


def scatter_sum(x):
    return jnp.sum(lax.all_to_all(x, "dp", 0, 0).astype(F32), axis=0)


def late_pack(down_grad, gains):
    attn, ffn, q, kv = (g.reshape(N_DP, -1) for g in gains)
    wide = ((0, 0), (0, 2 * HEAD - SLICE))
    row = jnp.concatenate([jnp.pad(attn, wide), jnp.pad(ffn, wide), q, kv], axis=1)
    row = jnp.pad(row, ((0, 0), (0, 16 * HEAD - row.shape[1]))).reshape(N_DP, 16, HEAD)
    row = jnp.pad(row, ((0, 0), (0, 0), (0, HEAD))).astype(BF16)
    return jnp.concatenate([down_grad, row], axis=1)


def body(
    layer_input,
    cotangent,
    seq_lengths,
    g_attn,
    w_qa,
    g_q,
    w_qb,
    w_kva,
    g_kv,
    w_kvb,
    w_o,
    g_ffn,
    w_gate,
    w_up,
    w_down,
):
    core = lax.axis_index("section")
    gains = jnp.stack(
        [
            jnp.pad(g, (0, A_COLS - LAT - g.shape[0]))
            for g in (g_attn[0], g_ffn[0], jnp.concatenate([g_q[0], g_kv[0]]))
        ]
    )
    gains = jnp.pad(gains, ((0, QR // N_DP - 3), (0, 0)))
    packs = attention_packs(w_qa[0], w_qb[0], w_kva[0], w_kvb[0], w_o[0], gains)
    keep = lax.dynamic_index_in_dim(packs, core, 0, keepdims=False)
    give = lax.dynamic_index_in_dim(packs, 1 - core, 0, keepdims=False)
    attn_one, attn_two = by_core(core, keep, to_core(give))
    attn_one = lax.all_gather(attn_one, "dp")
    attn_two = lax.all_gather(attn_two, "dp")

    blocks = lax.all_to_all(ffn_pack(w_gate[0], w_up[0], w_down[0]), "dp", 0, 0)
    tab = head_tables(seq_lengths)
    blocks, cotangent, layer_input = lax.optimization_barrier((blocks, cotangent, layer_input))
    mine = ring_pieces(blocks.reshape(D, MATS))
    ffn_weights = mine + [to_core(piece) for piece in mine]

    def token_rows(x):
        packs = x.reshape(2, N_Z, SHARD, D)
        first, second = by_core(core, packs[0], packs[1])
        return from_here(first).reshape(PACK, D), from_here(second).reshape(PACK, D)

    def d_mlp_rows(grad):
        return gather_dp((RES_SCALE * grad).astype(BF16))

    cot_own = token_rows(cotangent)[0][:SHARD].astype(F32)
    d_rows_two = d_mlp_rows(cot_own)
    attn_one, d_rows_two, tab = lax.optimization_barrier((attn_one, d_rows_two, tab))
    gains_one, gains_two = attention_gains(attn_one), attention_gains(attn_two)
    own_one = (core == 0).astype(jnp.int32).reshape(1)
    own_two = 1 - own_one

    rows = token_rows(layer_input)
    x_own = rows[0][:SHARD].astype(F32)
    part, saved_one = layer_forward(own_one, rows, x_own, attn_one, gains_one, ffn_weights, tab)
    out_one = layer_out_rows(part, saved_one)
    rows_one = gather_tokens(out_one)
    part_two, saved_two = layer_forward(
        own_two, rows_one, out_one.astype(F32), attn_two, gains_two, ffn_weights, tab
    )
    in_grad_two, ffn_grads_two, early_two, down_two, dg_two, part_two = layer_backward(
        own_two, cot_own, d_rows_two, saved_two, attn_two, gains_two, ffn_weights, tab, part_two
    )
    rows_two = gather_tokens(layer_out_rows(part_two, saved_two))
    early_two = lax.psum_scatter(
        early_two.reshape(N_DP * E_ROWS, WO), "dp", scatter_dimension=0, tiled=True
    )
    grad_one = in_grad_two.astype(F32)
    d_rows_one = d_mlp_rows(grad_one)
    d_rows_one, ffn_grads_two = lax.optimization_barrier((d_rows_one, ffn_grads_two))
    in_grad_one, ffn_grads_one, early_one, down_one, dg_one, _ = layer_backward(
        own_one, grad_one, d_rows_one, saved_one, attn_one, gains_one, ffn_weights, tab, ()
    )
    early_one = lax.psum_scatter(
        early_one.reshape(N_DP * E_ROWS, WO), "dp", scatter_dimension=0, tiled=True
    )

    totals = [ring_sum(0, ffn_grads_one), ring_sum(1, ffn_grads_two)]
    total = jnp.where(core == 0, totals[0], totals[1]).reshape(N_DP, SLICE, MATS)
    gate_grad, up_grad, down_grad = ffn_unpack(lax.all_to_all(total, "dp", 0, 0))

    late = jnp.concatenate([late_pack(down_one, dg_one), late_pack(down_two, dg_two)], axis=1)
    late = scatter_sum(late)
    tiles = from_zero(jnp.stack(gather_z(late[:, :HEAD].astype(BF16)))).astype(F32)
    late = late.reshape(2, SLICE + 16, 2 * HEAD)
    tiles = tiles.reshape(N_Z, 2, SLICE + 16, HEAD)
    sums = []
    for layer, early in enumerate((early_one, early_two)):
        lat = tiles[:, layer, :SLICE].transpose(1, 0, 2).reshape(SLICE, N_Z * HEAD)
        early = early.astype(F32)
        wide = jnp.concatenate([lat, late[layer, :SLICE, HEAD:], early[:SLICE]], axis=1)
        low = jnp.concatenate([early[SLICE:A_ROWS], early[A_ROWS:, : LAT - WO]], axis=1)
        sums.append((wide, low, jnp.sum(tiles[:, layer, SLICE:], axis=0)))
    home = []
    for one, two in zip(*sums):
        keep = jnp.where(core == 0, one, two)
        give = jnp.where(core == 0, two, one)
        home.append(by_core(core, keep, to_core(give)))
    (wide_low, wide_high), (low_low, low_high), (dg_low, dg_high) = home
    qa_grad = jnp.concatenate([wide_low[:, :512], wide_high[:, :256]], axis=1)
    kva_grad = wide_high[:, 256 : 256 + KVR + ROPE]
    at = LAT + WO - HEADS * VD
    wo_grad = jnp.concatenate([wide_low[:, at:], wide_high[:, at:]], axis=1).T
    qb_rows, kvb_rows = slice(0, QR // N_DP), slice(QR // N_DP, A_ROWS - SLICE)
    heads = jnp.concatenate([low_low[qb_rows], low_high[qb_rows]], axis=1)
    heads = heads.reshape(QR // N_DP, 2 * HEADS, HEAD)[:, :, : NOPE + ROPE]
    qb_grad = heads.reshape(QR // N_DP, 2 * HEADS * (NOPE + ROPE))
    kvb_grad = jnp.concatenate([low_low[kvb_rows], low_high[kvb_rows]], axis=1)
    gains = (dg_low + dg_high).reshape(-1)

    def gain_part(at, width):
        return gains[at : at + width][None]

    layer_out = in_order(*(jnp.where(core == 0, one, two) for one, two in zip(rows_one, rows_two)))[None]
    give = jnp.where(core == 0, in_grad_two, in_grad_one)
    mine = jnp.where(core == 0, in_grad_one, in_grad_two)
    both = jnp.concatenate([mine, to_core(give)], axis=1)
    both = jnp.concatenate(gather_z(both), axis=0)
    input_grad = in_order(both[:, :D], both[:, D:])[None]
    return (
        layer_out,
        input_grad,
        gain_part(0, SLICE),
        qa_grad[None],
        gain_part(4 * HEAD, QR // N_DP),
        qb_grad[None],
        kva_grad[None],
        gain_part(4 * HEAD + QR // N_DP, KVR // N_DP),
        kvb_grad[None],
        wo_grad[None],
        gain_part(2 * HEAD, SLICE),
        gate_grad[None],
        up_grad[None],
        down_grad[None],
    )


def solution(mesh):
    in_specs = (
        P("dp", None),
        P("dp", None),
        P("dp", None),
        P("section", "dp"),
        P("section", "dp", None),
        P("section", "dp"),
        P("section", "dp", "tensor"),
        P("section", "dp", None),
        P("section", "dp"),
        P("section", "dp", "tensor"),
        P("section", "tensor", "dp"),
        P("section", "dp"),
        P("section", "dp", "tensor"),
        P("section", "dp", "tensor"),
        P("section", "tensor", "dp"),
    )
    out_specs = (
        P("section", "dp", None),
        P("section", "dp", None),
        P("section", "dp"),
        P("section", "dp", None),
        P("section", "dp"),
        P("section", "dp", "tensor"),
        P("section", "dp", None),
        P("section", "dp"),
        P("section", "dp", "tensor"),
        P("section", "tensor", "dp"),
        P("section", "dp"),
        P("section", "dp", "tensor"),
        P("section", "dp", "tensor"),
        P("section", "tensor", "dp"),
    )
    return jax.shard_map(body, mesh=mesh, in_specs=in_specs, out_specs=out_specs, check_vma=False)
```

time: 1790 us -> 698 us (0.39)
  waiting for transfers between devices: 1160 us -> 267 us
  matrix products: 290 us -> 3.34 us
  starting transfers between devices: 14.4 us -> 165 us
  blocking collectives: 181 us -> 43.9 us
  Pallas kernels: 0 us -> 88.8 us
  other arithmetic: 81.6 us -> 60.1 us
    reduce_scatter x8 -> x2, waiting for transfers between devices: 451 us -> 0.01 us  [the longest x1 0.01 us: body(): lax.psum_scatter(early_one.reshape(N_DP * E_ROWS, WO), 'dp', scatter_dime...]
    psum x11 -> x0, waiting for transfers between devices: 401 us -> none  [the longest x3 122 us: layer_backward(): lax.psum(product_right(d_gate, w_gate) + product_right(d_up, w_up), 'tens...]
    all_gather x7 -> x2, waiting for transfers between devices: 295 us -> 9.73 us  [the longest x1 9.73 us: body(): attn_one = lax.all_gather(attn_one, 'dp')]
    dot_general x87 -> x2, matrix products: 284 us -> 3.34 us  [dot_tn(): lax.dot_general(a, b, (((0,), (0,)), ((), ())), preferred_element_type=F32)]
    all_to_all x0 -> x9, waiting for transfers between devices: none -> 164 us  [the longest x4 63.7 us: gather_dp(): lax.all_to_all(copies, 'dp', 0, 0).reshape(N_DP * x.shape[0], x.shape[1])]
    unnamed x2 -> x0, blocking collectives: 119 us -> none
    ppermute x4 -> x76, starting transfers between devices: 12.5 us -> 117 us  [the longest x36 41.4 us: z_hop(): return lax.ppermute(x, 'tensor', [(i, (i + by) % N_Z) for i in range(N_Z)])]
    pallas_call x0 -> x14, Pallas kernels: none -> 88.8 us  [the longest x2 28.3 us: ffn_backward(): pl.pallas_call(ffn_backward_kernel, out_shape=(jax.ShapeDtypeStruct((TOKE...]
  transfers between devices with their start and end apart: 30 -> 89, of which waited for: 26 -> 39; matrix products, arithmetic and copies ran while one was open for 11% -> 11% of each run, Pallas kernels for 0% -> 5%
where the time goes in v1:
time: 698 us; the launch traced here: 689 us
  waiting for transfers between devices  267 us (38%)
  starting transfers between devices  165 us (24%)
  Pallas kernels  88.8 us (13%)
  other arithmetic  60.1 us (9%)
  local copies, waits for them, and re-layouts  43.9 us (6%)
  blocking collectives  43.9 us (6%)
  between operations  16.3 us (2%)
    ppermute x9, waiting for transfers between devices, ring_hop(): return lax.ppermute(x, ('section', 'tensor'), pairs)  63.9 us
    all_to_all x4, waiting for transfers between devices, gather_dp(): lax.all_to_all(copies, 'dp', 0, 0).reshape(N_DP * x.shape[0], x.shape[1])  63.7 us
    all_to_all x2, blocking collectives, scatter_dp(): pieces = lax.all_to_all(part.reshape(N_DP, SHARD, D), 'dp', 0, 0)  43.9 us
    ppermute x36, starting transfers between devices, z_hop(): return lax.ppermute(x, 'tensor', [(i, (i + by) % N_Z) for i in range(N_Z)])  41.4 us
    ppermute x23, starting transfers between devices, to_core(): return lax.ppermute(x, 'section', [(0, 1), (1, 0)])  35.9 us
    all_to_all x1, waiting for transfers between devices, body(): blocks = lax.all_to_all(ffn_pack(w_gate[0], w_up[0], w_down[0]), 'dp', 0, 0)  33.5 us
    pallas_call x2, Pallas kernels, ffn_backward(): pl.pallas_call(ffn_backward_kernel, out_shape=(jax.ShapeDtypeStruct((TOKE...  28.3 us
    all_to_all x2, waiting for transfers between devices, scatter_dp(): pieces = lax.all_to_all(part.reshape(N_DP, SHARD, D), 'dp', 0, 0)  26.9 us
  transfers between devices with their start and end apart: 89, of which 39 were waited for; matrix products, arithmetic and copies ran while one was open for 11% of the time, Pallas kernels for 5%

profile of v1, /device:TPU:1, one launch (start us, length us, event | category | flops | bytes accessed | tf_op | source)
XLA Modules:
  0.0 689.1 jit_solution(11441723002064479660)
XLA Ops:
  23.3 7.0 %all-to-all-start = ((bf16[16,160,384]{2,1,0:T(8,128)(2,1)}), bf16[16,160,384]{2,1,0:T(8,128)(2,1)}, u32[]{:S(2)}, u32[]{:S(2)}) async-start(bf16[16,160,384]{2,1,0:T(8,128)(2,1)} %ffn_pack.1), calls=%async_computation | async-start | bytes 3932160 | tf_op jit(solution)/shard_map/all_to_all | solution.py:696
  31.2 33.5 %all-to-all-done = bf16[16,160,384]{2,1,0:T(8,128)(2,1)} async-done(((bf16[16,160,384]{2,1,0:T(8,128)(2,1)}), bf16[16,160,384]{2,1,0:T(8,128)(2,1)}, u32[]{:S(2)}, u32[]{:S(2)}) %all-to-all-start) | async-done | bytes 1966112 | tf_op jit(solution)/shard_map/all_to_all | solution.py:696
  75.6 24.5 %collective-permute-done.6.refs_1_ = bf16[2560,384]{1,0:T(8,128)(2,1)} collective-permute-done((bf16[2560,384]{1,0:T(8,128)(2,1)}, bf16[2560,384]{1,0:T(8,128)(2,1)}, u32[]{:S(2)}, u32[]{:S(2)}) %collective-permute-start.6) | collective-permute-done | bytes 1966112 | tf_op jit(solution)/shard_map/ppermute | solution.py:577
  104.6 9.7 %all-gather.5.cloned.1.call-done = bf16[3584,896]{1,0:T(8,128)(2,1)} async-done(((bf16[224,896]{1,0:T(8,128)(2,1)}), bf16[3584,896]{1,0:T(8,128)(2,1)}) %all-gather.5.cloned.1.call-update) | async-done | bytes 6422544 | tf_op jit(solution)/shard_map/all_gather | solution.py:693
  146.4 25.2 %all-to-all-done.2 = bf16[16,16,2560]{2,1,0:T(8,128)(2,1)S(1)} async-done(((bf16[16,16,2560]{2,1,0:T(8,128)(2,1)}), bf16[16,16,2560]{2,1,0:T(8,128)(2,1)S(1)}, u32[]{:S(2)}, u32[]{:S(2)}) %all-to-all-start.2) | async-done | bytes 1310752 | tf_op jit(solution)/shard_map/all_to_all | solution.py:92
  172.7 10.1 %ffn_forward.2 = (bf16[256,2560]{1,0:T(8,128)(2,1)}, f32[256,1024]{1,0:T(8,128)}, bf16[256,512]{1,0:T(8,128)(2,1)}) custom-call(s32[1]{0:T(128)} %bitcast.33.own_ref, bf16[256,2560]{1,0:T(8,128)(2,1)} %bitcast.216, bf16[2560,384]{1,0:T(8,128)(2,1)} %bitcast.35.refs_0_, bf16[2560,384]{1,0:T(8,128)(2,1)} %collective-permute-done.6.refs_1_, ...), custom_call_target="tpu_custom_call" | custom-call | tf_op jit(solution)/shard_map/ffn_forward/pallas_call | solution.py:168
  182.8 23.0 %all_to_all.55 = bf16[16,16,2560]{2,1,0:T(8,128)(2,1)S(1)} all-to-all(bf16[16,16,2560]{2,1,0:T(8,128)(2,1)} %bitcast.234), channel_id=1, replica_groups=mesh['section'=2,'tensor'=4,'dp'=16] {'dp'}, dimensions={0} | all-to-all | bytes 2621440 | tf_op jit(solution)/shard_map/all_to_all | solution.py:96
  213.3 7.2 %collective-permute-start.16 = (bf16[64,2560]{1,0:T(8,128)(2,1)S(1)}, bf16[64,2560]{1,0:T(8,128)(2,1)S(1)}, u32[]{:S(2)}, u32[]{:S(2)}) collective-permute-start(bf16[64,2560]{1,0:T(8,128)(2,1)S(1)} %pad_maximum_fusion.7.mine_ref), channel_id=1, source_target_pairs={{0,64},{64,0},{1,65},{65,1},{2,66},{66,2},{3,67},{67,3},{4,68},{68... | collective-permute-start | bytes 983048 | tf_op jit(solution)/shard_map/ppermute | solution.py:45
  248.7 17.5 %all-to-all-done.4 = bf16[16,16,2560]{2,1,0:T(8,128)(2,1)} async-done(((bf16[16,16,2560]{2,1,0:T(8,128)(2,1)}), bf16[16,16,2560]{2,1,0:T(8,128)(2,1)}, u32[]{:S(2)}, u32[]{:S(2)}) %all-to-all-start.4) | async-done | bytes 1310752 | tf_op jit(solution)/shard_map/all_to_all | solution.py:92
  266.3 10.1 %ffn_forward.3 = (bf16[256,2560]{1,0:T(8,128)(2,1)}, f32[256,1024]{1,0:T(8,128)}, bf16[256,512]{1,0:T(8,128)(2,1)}) custom-call(s32[1]{0:T(128)S(6)} %sub.58.own_ref, bf16[256,2560]{1,0:T(8,128)(2,1)} %bitcast.38.n_ref, bf16[2560,384]{1,0:T(8,128)(2,1)} %bitcast.35.refs_0_, bf16[2560,384]{1,0:T(8,128)(2,1)} %collective-permute-done.6.refs_1_, ...), custom_call_target="tpu_custom_call" | custom-call | tf_op jit(solution)/shard_map/ffn_forward/pallas_call | solution.py:168
  276.4 14.2 %ffn_backward.2 = (bf16[256,2560]{1,0:T(8,128)(2,1)}, bf16[2560,384]{1,0:T(8,128)(2,1)}, bf16[2560,384]{1,0:T(8,128)(2,1)}, bf16[2560,384]{1,0:T(8,128)(2,1)}, bf16[2560,384]{1,0:T(8,128)(2,1)}) custom-call(s32[1]{0:T(128)S(6)} %sub.58.own_ref, bf16[256,2560]{1,0:T(8,128)(2,1)} %bitcast.220, bf16[256,2560]{1,0:T(8,128)(2,1)} %bitcast.38.n_ref, ...), custom_call_target="tpu_custom_call" | custom-call | tf_op jit(solution)/shard_map/ffn_backward/pallas_call | solution.py:210
  290.6 20.9 %all_to_all.56 = bf16[16,16,2560]{2,1,0:T(8,128)(2,1)S(1)} all-to-all(bf16[16,16,2560]{2,1,0:T(8,128)(2,1)} %bitcast.233), channel_id=1, replica_groups=mesh['section'=2,'tensor'=4,'dp'=16] {'dp'}, dimensions={0} | all-to-all | bytes 2621440 | tf_op jit(solution)/shard_map/all_to_all | solution.py:96
  332.9 5.9 attend_back.2
  363.1 19.9 %all-to-all-done.7 = bf16[16,16,2560]{2,1,0:T(8,128)(2,1)} async-done(((bf16[16,16,2560]{2,1,0:T(8,128)(2,1)}), bf16[16,16,2560]{2,1,0:T(8,128)(2,1)}, u32[]{:S(2)}, u32[]{:S(2)}) %all-to-all-start.7) | async-done | bytes 1310752 | tf_op jit(solution)/shard_map/all_to_all | solution.py:92
  383.0 14.1 %ffn_backward.3 = (bf16[256,2560]{1,0:T(8,128)(2,1)}, bf16[2560,384]{1,0:T(8,128)(2,1)}, bf16[2560,384]{1,0:T(8,128)(2,1)}, bf16[2560,384]{1,0:T(8,128)(2,1)}, bf16[2560,384]{1,0:T(8,128)(2,1)}) custom-call(s32[1]{0:T(128)} %bitcast.33.own_ref, bf16[256,2560]{1,0:T(8,128)(2,1)} %bitcast.46.dm_ref, bf16[256,2560]{1,0:T(8,128)(2,1)} %bitcast.217, ...), custom_call_target="tpu_custom_call" | custom-call | tf_op jit(solution)/shard_map/ffn_backward/pallas_call | solution.py:210
  408.8 10.7 %all-to-all-done.8 = bf16[16,16,2560]{2,1,0:T(8,128)(2,1)} async-done(((bf16[16,16,2560]{2,1,0:T(8,128)(2,1)}), bf16[16,16,2560]{2,1,0:T(8,128)(2,1)}, u32[]{:S(2)}, u32[]{:S(2)}) %all-to-all-start.8) | async-done | bytes 1310752 | tf_op jit(solution)/shard_map/all_to_all | solution.py:96
  429.1 16.2 %all-to-all-done.6 = bf16[16,16,2560]{2,1,0:T(8,128)(2,1)} async-done(((bf16[16,16,2560]{2,1,0:T(8,128)(2,1)}), bf16[16,16,2560]{2,1,0:T(8,128)(2,1)}, u32[]{:S(2)}, u32[]{:S(2)}) %all-to-all-start.6) | async-done | bytes 1310752 | tf_op jit(solution)/shard_map/all_to_all | solution.py:96
  454.0 5.9 attend_back.3
  523.3 7.4 %collective-permute-start.62 = (bf16[2560,384]{1,0:T(8,128)(2,1)}, bf16[2560,384]{1,0:T(8,128)(2,1)}, u32[]{:S(2)}, u32[]{:S(2)}) collective-permute-start(bf16[2560,384]{1,0:T(8,128)(2,1)} %get-tuple-element.121), channel_id=1, source_target_pairs={{64,0},{65,1},{66,2},{67,3},{68,4},{69,5},{70,6},{71,7},{72,8},{73... | collective-permute-start | bytes 5898248 | tf_op jit(solution)/shard_map/ppermute | solution.py:591
  540.2 22.0 %all-to-all-done.9 = bf16[16,352,256]{2,1,0:T(8,128)(2,1)} async-done(((bf16[16,352,256]{2,1,0:T(8,128)(2,1)}), bf16[16,352,256]{2,1,0:T(8,128)(2,1)}, u32[]{:S(2)}, u32[]{:S(2)}) %all-to-all-start.9) | async-done | bytes 2883616 | tf_op jit(solution)/shard_map/all_to_all | solution.py:652
  587.4 31.8 %collective-permute-done.75 = bf16[2560,384]{1,0:T(8,128)(2,1)S(1)} collective-permute-done((bf16[2560,384]{1,0:T(8,128)(2,1)S(1)}, bf16[2560,384]{1,0:T(8,128)(2,1)S(1)}, u32[]{:S(2)}, u32[]{:S(2)}) %collective-permute-start.75) | collective-permute-done | bytes 1966112 | tf_op jit(solution)/shard_map/ppermute | solution.py:577
  624.7 6.2 fusion.6
  630.8 7.5 %all-to-all-start.10 = ((bf16[16,160,384]{2,1,0:T(8,128)(2,1)}), bf16[16,160,384]{2,1,0:T(8,128)(2,1)S(1)}, u32[]{:S(2)}, u32[]{:S(2)}) async-start(bf16[16,160,384]{2,1,0:T(8,128)(2,1)} %bitcast.90), calls=%async_computation.12 | async-start | bytes 3932160 | tf_op jit(solution)/shard_map/all_to_all | solution.py:744
  648.3 18.2 %all-to-all-done.10.in_ref = bf16[16,160,384]{2,1,0:T(8,128)(2,1)S(1)} async-done(((bf16[16,160,384]{2,1,0:T(8,128)(2,1)}), bf16[16,160,384]{2,1,0:T(8,128)(2,1)S(1)}, u32[]{:S(2)}, u32[]{:S(2)}) %all-to-all-start.10) | async-done | bytes 1966112 | tf_op jit(solution)/shard_map/all_to_all | solution.py:744
  (583 shorter events, 304.0 us)
Async XLA Ops:
  7.2 107.1 %all-gather.5.cloned.1.call-start = ((), (), s32[]{:S(2)}) async-start(), calls=%async_computation.15 | async-start | bytes 6823936 | tf_op jit(solution)/shard_map/all_gather | solution.py:693
  17.4 203.1 %all-gather.7.cloned.1.call-start = ((), (), s32[]{:S(2)}) async-start(), calls=%async_computation.16 | async-start | bytes 6823936 | tf_op jit(solution)/shard_map/all_gather | solution.py:694
  23.3 41.5 %all-to-all-start = ((bf16[16,160,384]{2,1,0:T(8,128)(2,1)}), bf16[16,160,384]{2,1,0:T(8,128)(2,1)}, u32[]{:S(2)}, u32[]{:S(2)}) async-start(bf16[16,160,384]{2,1,0:T(8,128)(2,1)} %ffn_pack.1), calls=%async_computation | async-start | bytes 3932160 | tf_op jit(solution)/shard_map/all_to_all | solution.py:696
  64.8 35.3 %collective-permute-start.6 = (bf16[2560,384]{1,0:T(8,128)(2,1)}, bf16[2560,384]{1,0:T(8,128)(2,1)}, u32[]{:S(2)}, u32[]{:S(2)}) collective-permute-start(bf16[2560,384]{1,0:T(8,128)(2,1)} %bitcast.35.refs_0_), channel_id=1, source_target_pairs={{0,16},{16,32},{32,48},{48,0},{64,112},{80,64},{96,80},{112,96},{1... | collective-permute-start | bytes 5898248 | tf_op jit(solution)/shard_map/ppermute | solution.py:577
  69.3 35.3 %all-to-all-start.1 = ((bf16[16,16,2560]{2,1,0:T(8,128)(2,1)}), bf16[16,16,2560]{2,1,0:T(8,128)(2,1)S(1)}, u32[]{:S(2)}, u32[]{:S(2)}) async-start(bf16[16,16,2560]{2,1,0:T(8,128)(2,1)} %broadcast_in_dim.79), calls=%async_computation.1 | async-start | bytes 2621440 | tf_op jit(solution)/shard_map/all_to_all | solution.py:92
  75.2 55.4 %collective-permute-start.7 = (bf16[2560,384]{1,0:T(8,128)(2,1)}, bf16[2560,384]{1,0:T(8,128)(2,1)}, u32[]{:S(2)}, u32[]{:S(2)}) collective-permute-start(bf16[2560,384]{1,0:T(8,128)(2,1)} %bitcast.35.refs_0_), channel_id=1, source_target_pairs={{0,48},{16,0},{32,16},{48,32},{64,80},{80,96},{96,112},{112,64},{1... | collective-permute-start | bytes 5898248 | tf_op jit(solution)/shard_map/ppermute | solution.py:577
  100.1 33.9 %collective-permute-start.8 = (bf16[2560,384]{1,0:T(8,128)(2,1)}, bf16[2560,384]{1,0:T(8,128)(2,1)}, u32[]{:S(2)}, u32[]{:S(2)}) collective-permute-start(bf16[2560,384]{1,0:T(8,128)(2,1)} %collective-permute-done.6.refs_1_), channel_id=1, source_target_pairs={{0,16},{16,32},{32,48},{48,0},{64,112},{80,64},{96,80},{112,96},{1... | collective-permute-start | bytes 5898248 | tf_op jit(solution)/shard_map/ppermute | solution.py:577
  141.0 30.6 %all-to-all-start.2 = ((bf16[16,16,2560]{2,1,0:T(8,128)(2,1)}), bf16[16,16,2560]{2,1,0:T(8,128)(2,1)S(1)}, u32[]{:S(2)}, u32[]{:S(2)}) async-start(bf16[16,16,2560]{2,1,0:T(8,128)(2,1)} %broadcast_in_dim.147), calls=%async_computation.2 | async-start | bytes 2621440 | tf_op jit(solution)/shard_map/all_to_all | solution.py:92
  401.5 241.2 %reduce-scatter.5.cloned.1.call-start = ((), (), s32[]{:S(2)}) async-start(), calls=%async_computation.14 | async-start | bytes 3760128 | tf_op jit(solution)/shard_map/reduce_scatter | solution.py:729
  424.0 220.3 %reduce-scatter.3.cloned.1.call-start = ((), (), s32[]{:S(2)}) async-start(), calls=%async_computation.13 | async-start | bytes 3760128 | tf_op jit(solution)/shard_map/reduce_scatter | solution.py:738
  460.8 29.9 %collective-permute-start.64 = (bf16[2560,384]{1,0:T(8,128)(2,1)}, bf16[2560,384]{1,0:T(8,128)(2,1)}, u32[]{:S(2)}, u32[]{:S(2)}) collective-permute-start(bf16[2560,384]{1,0:T(8,128)(2,1)} %get-tuple-element.123), channel_id=1, source_target_pairs={{64,0},{65,1},{66,2},{67,3},{68,4},{69,5},{70,6},{71,7},{72,8},{73... | collective-permute-start | bytes 5898248 | tf_op jit(solution)/shard_map/ppermute | solution.py:591
  464.5 32.6 %collective-permute-start.67 = (bf16[2560,384]{1,0:T(8,128)(2,1)}, bf16[2560,384]{1,0:T(8,128)(2,1)}, u32[]{:S(2)}, u32[]{:S(2)}) collective-permute-start(bf16[2560,384]{1,0:T(8,128)(2,1)} %get-tuple-element.124), channel_id=1, source_target_pairs={{64,0},{65,1},{66,2},{67,3},{68,4},{69,5},{70,6},{71,7},{72,8},{73... | collective-permute-start | bytes 5898248 | tf_op jit(solution)/shard_map/ppermute | solution.py:591
  482.5 51.6 %collective-permute-start.63 = (bf16[2560,384]{1,0:T(8,128)(2,1)}, bf16[2560,384]{1,0:T(8,128)(2,1)}, u32[]{:S(2)}, u32[]{:S(2)}) collective-permute-start(bf16[2560,384]{1,0:T(8,128)(2,1)} %get-tuple-element.122), channel_id=1, source_target_pairs={{64,0},{65,1},{66,2},{67,3},{68,4},{69,5},{70,6},{71,7},{72,8},{73... | collective-permute-start | bytes 5898248 | tf_op jit(solution)/shard_map/ppermute | solution.py:591
  487.8 30.5 %collective-permute-start.74 = (bf16[2560,384]{1,0:T(8,128)(2,1)}, bf16[2560,384]{1,0:T(8,128)(2,1)}, u32[]{:S(2)}, u32[]{:S(2)}) collective-permute-start(bf16[2560,384]{1,0:T(8,128)(2,1)} %get-tuple-element.128), channel_id=1, source_target_pairs={{0,64},{1,65},{2,66},{3,67},{4,68},{5,69},{6,70},{7,71},{8,72},{9,... | collective-permute-start | bytes 5898248 | tf_op jit(solution)/shard_map/ppermute | solution.py:591
  497.2 38.3 %collective-permute-start.65 = (bf16[2560,384]{1,0:T(8,128)(2,1)}, bf16[2560,384]{1,0:T(8,128)(2,1)}, u32[]{:S(2)}, u32[]{:S(2)}) collective-permute-start(bf16[2560,384]{1,0:T(8,128)(2,1)} %add_convert_fusion.9), channel_id=1, source_target_pairs={{0,48},{16,0},{32,16},{48,32},{1,49},{17,1},{33,17},{49,33},{2,50}... | collective-permute-start | bytes 5898248 | tf_op jit(solution)/shard_map/ppermute | solution.py:577
  511.7 50.5 %all-to-all-start.9 = ((bf16[16,352,256]{2,1,0:T(8,128)(2,1)}), bf16[16,352,256]{2,1,0:T(8,128)(2,1)}, u32[]{:S(2)}, u32[]{:S(2)}) async-start(bf16[16,352,256]{2,1,0:T(8,128)(2,1)} %fusion.5), calls=%async_computation.9 | async-start | bytes 5767168 | tf_op jit(solution)/shard_map/all_to_all | solution.py:652
  523.3 52.0 %collective-permute-start.62 = (bf16[2560,384]{1,0:T(8,128)(2,1)}, bf16[2560,384]{1,0:T(8,128)(2,1)}, u32[]{:S(2)}, u32[]{:S(2)}) collective-permute-start(bf16[2560,384]{1,0:T(8,128)(2,1)} %get-tuple-element.121), channel_id=1, source_target_pairs={{64,0},{65,1},{66,2},{67,3},{68,4},{69,5},{70,6},{71,7},{72,8},{73... | collective-permute-start | bytes 5898248 | tf_op jit(solution)/shard_map/ppermute | solution.py:591
  530.8 39.6 %collective-permute-start.70 = (bf16[2560,384]{1,0:T(8,128)(2,1)}, bf16[2560,384]{1,0:T(8,128)(2,1)}, u32[]{:S(2)}, u32[]{:S(2)}) collective-permute-start(bf16[2560,384]{1,0:T(8,128)(2,1)} %get-tuple-element.126), channel_id=1, source_target_pairs={{0,64},{1,65},{2,66},{3,67},{4,68},{5,69},{6,70},{7,71},{8,72},{9,... | collective-permute-start | bytes 5898248 | tf_op jit(solution)/shard_map/ppermute | solution.py:591
  532.1 38.3 %collective-permute-start.72 = (bf16[2560,384]{1,0:T(8,128)(2,1)}, bf16[2560,384]{1,0:T(8,128)(2,1)}, u32[]{:S(2)}, u32[]{:S(2)}) collective-permute-start(bf16[2560,384]{1,0:T(8,128)(2,1)} %add_convert_fusion.3), channel_id=1, source_target_pairs={{64,80},{80,96},{96,112},{112,64},{65,81},{81,97},{97,113},{113,65... | collective-permute-start | bytes 5898248 | tf_op jit(solution)/shard_map/ppermute | solution.py:577
  534.1 53.3 %collective-permute-start.69 = (bf16[2560,384]{1,0:T(8,128)(2,1)S(1)}, bf16[2560,384]{1,0:T(8,128)(2,1)}, u32[]{:S(2)}, u32[]{:S(2)}) collective-permute-start(bf16[2560,384]{1,0:T(8,128)(2,1)S(1)} %copy-done.29), channel_id=1, source_target_pairs={{0,64},{1,65},{2,66},{3,67},{4,68},{5,69},{6,70},{7,71},{8,72},{9,... | collective-permute-start | bytes 5898248 | tf_op jit(solution)/shard_map/ppermute | solution.py:591
  576.2 43.0 %collective-permute-start.75 = (bf16[2560,384]{1,0:T(8,128)(2,1)S(1)}, bf16[2560,384]{1,0:T(8,128)(2,1)S(1)}, u32[]{:S(2)}, u32[]{:S(2)}) collective-permute-start(bf16[2560,384]{1,0:T(8,128)(2,1)S(1)} %copy-done.32), channel_id=1, source_target_pairs={{64,112},{80,64},{96,80},{112,96},{65,113},{81,65},{97,81},{113,97... | collective-permute-start | bytes 5898248 | tf_op jit(solution)/shard_map/ppermute | solution.py:577
  579.4 39.8 %collective-permute-start.66 = (bf16[2560,384]{1,0:T(8,128)(2,1)S(1)}, bf16[2560,384]{1,0:T(8,128)(2,1)S(1)}, u32[]{:S(2)}, u32[]{:S(2)}) collective-permute-start(bf16[2560,384]{1,0:T(8,128)(2,1)S(1)} %copy-done.33), channel_id=1, source_target_pairs={{0,48},{16,0},{32,16},{48,32},{1,49},{17,1},{33,17},{49,33},{2,50}... | collective-permute-start | bytes 5898248 | tf_op jit(solution)/shard_map/ppermute | solution.py:577
  580.2 44.4 %collective-permute-start.73 = (bf16[2560,384]{1,0:T(8,128)(2,1)S(1)}, bf16[2560,384]{1,0:T(8,128)(2,1)S(1)}, u32[]{:S(2)}, u32[]{:S(2)}) collective-permute-start(bf16[2560,384]{1,0:T(8,128)(2,1)S(1)} %add_convert_fusion.2), channel_id=1, source_target_pairs={{64,80},{80,96},{96,112},{112,64},{65,81},{81,97},{97,113},{113,65... | collective-permute-start | bytes 5898248 | tf_op jit(solution)/shard_map/ppermute | solution.py:577
  630.8 35.6 %all-to-all-start.10 = ((bf16[16,160,384]{2,1,0:T(8,128)(2,1)}), bf16[16,160,384]{2,1,0:T(8,128)(2,1)S(1)}, u32[]{:S(2)}, u32[]{:S(2)}) async-start(bf16[16,160,384]{2,1,0:T(8,128)(2,1)} %bitcast.90), calls=%async_computation.12 | async-start | bytes 3932160 | tf_op jit(solution)/shard_map/all_to_all | solution.py:744
  (141 other events, 1397.1 us)
Sparse Core Ops, SparseCore 0:
  17.5 96.7 all-gather.4
  117.1 73.5 all-gather.6
  405.7 84.4 reduce-scatter.4
  493.5 108.6 reduce-scatter.2

commit v2 on v1

--- a/solution.py
+++ b/solution.py
@@ -114,11 +114,7 @@
 MATS = 3 * LANES
 TOKENS = N_DP * SHARD
 FF_VMEM = 56 * 1024 * 1024
-FF_SCRATCH = [
-    pltpu.VMEM((N_Z, D, MATS), BF16),
-    pltpu.VMEM((TOKENS, D), F32),
-    pltpu.SemaphoreType.DMA((N_Z,)),
-]
+FF_SCRATCH = [pltpu.VMEM((N_Z, D, MATS), BF16), pltpu.SemaphoreType.DMA((N_Z,))]
 
 
 def ffn_copies(own_ref, mine, other, w_ref, sems):
@@ -138,24 +134,22 @@
     return copies
 
 
+def down_pair(w_ref, z):
+    return jnp.concatenate([w_ref[z, :, 2 * LANES :], w_ref[z + 1, :, 2 * LANES :]], axis=1)
+
+
 def ffn_forward_kernel(own_ref, n_ref, *refs):
     mine, other = refs[:N_Z], refs[N_Z : 2 * N_Z]
-    part_ref, gu_ref, hid_ref, w_ref, acc_ref, sems = refs[2 * N_Z :]
+    part_ref, gu_ref, hid_ref, w_ref, sems = refs[2 * N_Z :]
     copies = ffn_copies(own_ref, mine, other, w_ref, sems)
     for z in range(N_Z):
         copies[z].wait()
         gu = dot(n_ref[...], w_ref[z, :, : 2 * LANES])
         gu_ref[:, 2 * LANES * z : 2 * LANES * (z + 1)] = gu
         gate, up = gu[:, :LANES], gu[:, LANES:]
-        hidden = (gate * jax.nn.sigmoid(gate) * up).astype(BF16)
-        hid_ref[:, LANES * z : LANES * (z + 1)] = hidden
-        out = dot_nt(hidden, w_ref[z, :, 2 * LANES :])
-        if z == 0:
-            acc_ref[...] = out
-        elif z < N_Z - 1:
-            acc_ref[...] += out
-        else:
-            part_ref[...] = (acc_ref[...] + out).astype(BF16)
+        hid_ref[:, LANES * z : LANES * (z + 1)] = (gate * jax.nn.sigmoid(gate) * up).astype(BF16)
+    out = dot_nt(hid_ref[:, : 2 * LANES], down_pair(w_ref, 0))
+    part_ref[...] = (out + dot_nt(hid_ref[:, 2 * LANES :], down_pair(w_ref, 2))).astype(BF16)
 
 
 def ffn_specs(arrays):
@@ -180,44 +174,105 @@
     )(own, rows, *weights)
 
 
-def ffn_backward_kernel(own_ref, dm_ref, n_ref, gu_ref, hid_ref, *refs):
-    mine, other, part_ref = refs[:N_Z], refs[N_Z : 2 * N_Z], refs[2 * N_Z]
-    grads = refs[2 * N_Z + 1 : 3 * N_Z + 1]
-    w_ref, acc_ref, sems = refs[3 * N_Z + 1 :]
+HALF_ROWS = SLICE // 2
+
+
+def ffn_backward_kernel(own_ref, dm_ref, gu_ref, *refs):
+    mine, other = refs[:N_Z], refs[N_Z : 2 * N_Z]
+    part_ref, dgu_ref, w_ref, sems = refs[2 * N_Z :]
     copies = ffn_copies(own_ref, mine, other, w_ref, sems)
+    out = None
+    for z in range(0, N_Z, 2):
+        copies[z].wait()
+        copies[z + 1].wait()
+        d_hidden = dot(dm_ref[...], down_pair(w_ref, z))
+        for k in range(2):
+            columns = slice(2 * LANES * (z + k), 2 * LANES * (z + k) + LANES)
+            more = slice(columns.stop, columns.stop + LANES)
+            gate, up = gu_ref[:, columns], gu_ref[:, more]
+            d_h = d_hidden[:, LANES * k : LANES * (k + 1)]
+            s = jax.nn.sigmoid(gate)
+            dgu_ref[:, columns] = (d_h * up * (s + gate * s * (1.0 - s))).astype(BF16)
+            dgu_ref[:, more] = (d_h * (gate * s)).astype(BF16)
     for z in range(N_Z):
-        hidden = hid_ref[:, LANES * z : LANES * (z + 1)]
-        grads[z][:, 2 * LANES :] = dot_tn(dm_ref[...], hidden).astype(BF16)
-        copies[z].wait()
-        d_hidden = dot(dm_ref[...], w_ref[z, :, 2 * LANES :])
-        gate = gu_ref[:, 2 * LANES * z : 2 * LANES * z + LANES]
-        up = gu_ref[:, 2 * LANES * z + LANES : 2 * LANES * (z + 1)]
-        s = jax.nn.sigmoid(gate)
-        d_gate = d_hidden * up * (s + gate * s * (1.0 - s))
-        d_up = d_hidden * (gate * s)
-        d_gu = jnp.concatenate([d_gate.astype(BF16), d_up.astype(BF16)], axis=1)
-        grads[z][:, : 2 * LANES] = dot_tn(n_ref[...], d_gu).astype(BF16)
-        out = dot_nt(d_gu, w_ref[z, :, : 2 * LANES])
-        if z == 0:
-            acc_ref[...] = out
-        elif z < N_Z - 1:
-            acc_ref[...] += out
-        else:
-            part_ref[...] = (acc_ref[...] + out).astype(BF16)
-
-
-def ffn_backward(own, d_rows, rows, gu, hidden, weights):
-    out = pl.pallas_call(
+        term = dot_nt(dgu_ref[:, 2 * LANES * z : 2 * LANES * (z + 1)], w_ref[z, :, : 2 * LANES])
+        out = term if z == 0 else out + term
+    part_ref[...] = out.astype(BF16)
+
+
+def ffn_backward(own, d_rows, gu, weights):
+    return pl.pallas_call(
         ffn_backward_kernel,
-        out_shape=(jax.ShapeDtypeStruct((TOKENS, D), BF16),)
-        + tuple(jax.ShapeDtypeStruct((D, MATS), BF16) for _ in range(N_Z)),
-        in_specs=ffn_specs(4),
-        out_specs=(pl.BlockSpec(memory_space=pltpu.VMEM),) * (N_Z + 1),
+        out_shape=(
+            jax.ShapeDtypeStruct((TOKENS, D), BF16),
+            jax.ShapeDtypeStruct((TOKENS, 2 * LANES * N_Z), BF16),
+        ),
+        in_specs=ffn_specs(2),
+        out_specs=(pl.BlockSpec(memory_space=pltpu.VMEM),) * 2,
         scratch_shapes=FF_SCRATCH,
         compiler_params=pltpu.CompilerParams(vmem_limit_bytes=FF_VMEM),
         name="ffn_backward",
-    )(own, d_rows, rows, gu, hidden, *weights)
-    return out[0], out[1:]
+    )(own, d_rows, gu, *weights)
+
+
+HALF_ROWS = SLICE // 2
+
+
+def ffn_gradients_kernel(own_ref, dm_ref, n_ref, dgu_ref, hid_ref, *refs):
+    outs, grad_ref, out_sems = refs[: 2 * N_Z], refs[2 * N_Z], refs[2 * N_Z + 1]
+    core = own_ref[1]
+
+    def store(z, columns, grad):
+        grad_ref[z, :, :, :, columns] = grad.reshape(N_DP, 2, HALF_ROWS, grad.shape[1])
+
+    def send(z, keep_at, give_at):
+        return [
+            pltpu.make_async_copy(grad_ref.at[z, :, core], outs[keep_at], out_sems.at[keep_at]),
+            pltpu.make_async_copy(
+                grad_ref.at[z, :, 1 - core], outs[N_Z + give_at], out_sems.at[N_Z + give_at]
+            ),
+        ]
+
+    for z in (2, 0):
+        hidden = hid_ref[:, LANES * z : LANES * (z + 2)]
+        grad = dot_tn(dm_ref[...], hidden).astype(BF16)
+        store(z, slice(2 * LANES, MATS), grad[:, :LANES])
+        store(z + 1, slice(2 * LANES, MATS), grad[:, LANES:])
+        for k in range(2):
+            d_gu = dgu_ref[:, 2 * LANES * (z + k) : 2 * LANES * (z + k + 1)]
+            store(z + k, slice(0, 2 * LANES), dot_tn(n_ref[...], d_gu).astype(BF16))
+            if z + k in (0, N_Z - 1):
+                for copy in send(z + k, z + k, z + k):
+                    copy.start()
+            else:
+                for owner in (1, 0):
+                    keep_at = z + k if owner == 1 else 3 - z - k
+
+                    @pl.when(own_ref[0] == owner)
+                    def _(at=z + k, keep_at=keep_at):
+                        for copy in send(at, keep_at, 3 - keep_at):
+                            copy.start()
+
+    for z in range(N_Z):
+        for copy in send(z, z, z):
+            copy.wait()
+
+
+def ffn_gradients(own, d_rows, rows, d_gu, hidden):
+    vmem = pl.BlockSpec(memory_space=pltpu.VMEM)
+    return pl.pallas_call(
+        ffn_gradients_kernel,
+        out_shape=tuple(jax.ShapeDtypeStruct((N_DP, HALF_ROWS, MATS), BF16) for _ in range(2 * N_Z)),
+        in_specs=[pl.BlockSpec(memory_space=pltpu.SMEM)] + [vmem] * 4,
+        out_specs=(pl.BlockSpec(memory_space=pl.ANY),) * (2 * N_Z),
+        scratch_shapes=[
+            pltpu.VMEM((N_Z, N_DP, 2, HALF_ROWS, MATS), BF16),
+            pltpu.SemaphoreType.DMA((2 * N_Z,)),
+        ],
+        compiler_params=pltpu.CompilerParams(vmem_limit_bytes=FF_VMEM),
+        cost_estimate=pl.CostEstimate(flops=2 * TOKENS * D * MATS * N_Z, bytes_accessed=1 << 24, transcendentals=0),
+        name="ffn_gradients",
+    )(own, d_rows, rows, d_gu, hidden)
 
 
 FF = N_DP * FF_PART
@@ -225,15 +280,10 @@
 FF_PADDED = (FF - FF_PART) // LANES * LANES + WINDOW
 
 
-def identity(n):
-    at = lax.broadcasted_iota(jnp.int32, (n, n), 0)
-    return jnp.where(at == lax.broadcasted_iota(jnp.int32, (n, n), 1), 1.0, 0.0).astype(BF16)
-
-
 def ffn_pack_kernel(gate_ref, up_ref, down_ref, out_ref, wide_ref):
     wide_ref[0, :, :FF] = gate_ref[...].astype(F32)
     wide_ref[1, :, :FF] = up_ref[...].astype(F32)
-    wide_ref[2, :, :FF] = dot_nt(identity(SLICE), down_ref[...])
+    wide_ref[2, :, :FF] = down_ref[...].astype(F32)
     valid = lax.broadcasted_iota(jnp.int32, (SLICE, LANES), 1) < FF_PART
     for p in range(N_DP):
         at = FF_PART * p // LANES * LANES
@@ -256,36 +306,43 @@
     )(w_gate, w_up, w_down)
 
 
-def ffn_unpack_kernel(in_ref, gate_ref, up_ref, down_ref, wide_ref):
+def ffn_unpack_kernel(core_ref, one, one_got, two, two_got, gate_ref, up_ref, down_ref, wide_ref):
+    first = core_ref[0] == 0
     wide_ref[...] = jnp.zeros(wide_ref.shape, F32)
-    valid = lax.broadcasted_iota(jnp.int32, (SLICE, LANES), 1) < FF_PART
+    valid = lax.broadcasted_iota(jnp.int32, (HALF_ROWS, LANES), 1) < FF_PART
     for p in range(N_DP):
         at = FF_PART * p // LANES * LANES
         by = FF_PART * p - at
         for m in range(3):
-            block = in_ref[p, :, LANES * m : LANES * (m + 1)].astype(F32)
-            block = jnp.where(valid, block, 0.0)
-            window = jnp.concatenate([block, jnp.zeros_like(block)], axis=1)
-            if by > 0:
-                window = pltpu.roll(window, by, 1)
-            wide_ref[m, :, at : at + WINDOW] += window
+            columns = slice(LANES * m, LANES * (m + 1))
+            low = jnp.where(first, one[p, :, columns].astype(F32), two_got[p, :, columns].astype(F32))
+            high = jnp.where(first, one_got[p, :, columns].astype(F32), two[p, :, columns].astype(F32))
+            for half, block in enumerate((low, high)):
+                block = jnp.where(valid, block, 0.0)
+                window = jnp.concatenate([block, jnp.zeros_like(block)], axis=1)
+                if by > 0:
+                    window = pltpu.roll(window, by, 1)
+                wide_ref[m, HALF_ROWS * half : HALF_ROWS * (half + 1), at : at + WINDOW] += window
     gate_ref[...] = wide_ref[0, :, :FF]
     up_ref[...] = wide_ref[1, :, :FF]
-    down_ref[...] = dot_tn(wide_ref[2, :, :FF].astype(BF16), identity(SLICE))
-
-
-def ffn_unpack(blocks):
+    down_ref[...] = wide_ref[2, :, :FF]
+
+
+def ffn_unpack(core, *blocks):
+    vmem = pl.BlockSpec(memory_space=pltpu.VMEM)
     return pl.pallas_call(
         ffn_unpack_kernel,
         out_shape=(
             jax.ShapeDtypeStruct((SLICE, FF), F32),
             jax.ShapeDtypeStruct((SLICE, FF), F32),
-            jax.ShapeDtypeStruct((FF, SLICE), F32),
+            jax.ShapeDtypeStruct((SLICE, FF), F32),
         ),
+        in_specs=[pl.BlockSpec(memory_space=pltpu.SMEM)] + [vmem] * 4,
+        out_specs=(vmem,) * 3,
         scratch_shapes=[pltpu.VMEM((3, SLICE, FF_PADDED), F32)],
         compiler_params=pltpu.CompilerParams(vmem_limit_bytes=FF_VMEM),
         name="ffn_unpack",
-    )(blocks)
+    )(core, *blocks)
 
 
 A_ROWS = SLICE + QR // N_DP + KVR // N_DP
@@ -432,16 +489,20 @@
 
 
 def attend_back_kernel(
-    mine_ref, other_ref, tab_ref, sq_ref, comp_ref, q_ref, kv_ref, kr_ref, mixed_ref, pack_ref,
-    part_ref, early_ref,
-    dq_ref, dkv_ref, qb_ref, kvb_ref, wo_ref, sems,
+    mine_ref, other_ref, tab_hbm, q_hbm, kv_hbm, kr_hbm, pack_ref,
+    part_ref, dq_ref, dkv_ref,
+    tab_ref, q_ref, kv_ref, kr_ref, in_sems, qb_ref, kvb_ref, wo_ref, sems,
 ):
+    pairs = ((kv_hbm, kv_ref), (kr_hbm, kr_ref), (q_hbm, q_ref), (tab_hbm, tab_ref))
+    inputs = [pltpu.make_async_copy(a, b, in_sems.at[i]) for i, (a, b) in enumerate(pairs)]
+    for copy in inputs:
+        copy.start()
     copies = weight_copies(pack_ref, qb_ref, kvb_ref, wo_ref, sems)
     d_att = jnp.concatenate([mine_ref[...], other_ref[...]], axis=0)
-    wo_grad = dot_tn(d_att, mixed_ref[...]).astype(BF16)
-    early_ref[:, :SLICE, :] = wo_grad.reshape(N_DP, SLICE, WO)
     copies[2].wait()
     d_mixed = dot(d_att, wo_ref[...].reshape(D, WO))
+    for copy in inputs:
+        copy.wait()
     rope = kr_ref[...]
     d_rope = jnp.zeros((ROWS, HEAD), F32)
     for h in range(HEADS):
@@ -469,30 +530,128 @@
     part_ref[:, :QR] = dot_nt(dq_ref[...], qb_ref[...].reshape(QR, LAT)).astype(BF16)
     part_ref[:, QR : QR + KVR] = dot_nt(dkv_ref[...], kvb_ref[...].reshape(KVR, LAT)).astype(BF16)
     part_ref[:, QR + KVR :] = d_rope.astype(BF16)
+
+
+def attend_back(d_attended, tab, saved, pack):
+    vmem = pl.BlockSpec(memory_space=pltpu.VMEM)
+    return pl.pallas_call(
+        attend_back_kernel,
+        out_shape=(
+            jax.ShapeDtypeStruct((ROWS, QR + KVR + HEAD), BF16),
+            jax.ShapeDtypeStruct((ROWS, LAT), BF16),
+            jax.ShapeDtypeStruct((ROWS, LAT), BF16),
+        ),
+        in_specs=[vmem] * 2 + [pl.BlockSpec(memory_space=pl.ANY)] * 5,
+        out_specs=(vmem,) * 3,
+        scratch_shapes=[
+            pltpu.VMEM((4, ROWS, HEAD), F32),
+            pltpu.VMEM((ROWS, LAT), BF16),
+            pltpu.VMEM((ROWS, LAT), BF16),
+            pltpu.VMEM((ROWS, HEAD), BF16),
+            pltpu.SemaphoreType.DMA((4,)),
+        ]
+        + weight_scratch(),
+        compiler_params=pltpu.CompilerParams(vmem_limit_bytes=ATT_VMEM),
+        name="attend_back",
+    )(*d_attended, tab, *saved[2:5], pack)
+
+
+def attend_gradients_kernel(
+    mine_ref, other_ref, dq_ref, dkv_ref, sq_hbm, comp_hbm, mixed_hbm,
+    early_ref,
+    sq_ref, comp_ref, mixed_ref, sems,
+):
+    pairs = ((mixed_hbm, mixed_ref), (sq_hbm, sq_ref), (comp_hbm, comp_ref))
+    copies = [pltpu.make_async_copy(a, b, sems.at[i]) for i, (a, b) in enumerate(pairs)]
+    for copy in copies:
+        copy.start()
+    d_att = jnp.concatenate([mine_ref[...], other_ref[...]], axis=0)
+    copies[0].wait()
+    wo_grad = dot_tn(d_att, mixed_ref[...]).astype(BF16)
+    early_ref[:, :SLICE, :] = wo_grad.reshape(N_DP, SLICE, WO)
+    copies[1].wait()
     qb_grad = dot_tn(sq_ref[...], dq_ref[...]).astype(BF16).reshape(N_DP, QR // N_DP, LAT)
+    copies[2].wait()
     kvb_grad = dot_tn(comp_ref[...], dkv_ref[...]).astype(BF16).reshape(N_DP, KVR // N_DP, LAT)
     early_ref[:, QB_ROWS, :] = qb_grad[:, :, :WO]
     early_ref[:, KVB_ROWS, :] = kvb_grad[:, :, :WO]
     more = slice(A_ROWS, A_ROWS + QR // N_DP)
     early_ref[:, more, : LAT - WO] = qb_grad[:, :, WO:]
-    early_ref[:, more.stop :, : LAT - WO] = kvb_grad[:, :, WO:]
-    early_ref[:, A_ROWS:, LAT - WO :] = jnp.zeros((N_DP, E_ROWS - A_ROWS, 2 * WO - LAT), BF16)
-
-
-def attend_back(d_attended, tab, saved, pack):
+    early_ref[:, more.stop : E_ROWS, : LAT - WO] = kvb_grad[:, :, WO:]
+    early_ref[:, A_ROWS:E_ROWS, LAT - WO :] = jnp.zeros((N_DP, E_ROWS - A_ROWS, 2 * WO - LAT), BF16)
+    if early_ref.shape[1] > E_ROWS:
+        rest = early_ref.shape[1] - E_ROWS
+        early_ref[:, E_ROWS:, 2 * HEAD :] = jnp.zeros((N_DP, rest, WO - 2 * HEAD), BF16)
+        early_ref[:, E_ROWS:, : 2 * HEAD] = jnp.zeros((N_DP, rest, 2 * HEAD), BF16)
+
+
+def attend_gradients(d_attended, saved, d_query, d_key_value, rows):
     vmem = pl.BlockSpec(memory_space=pltpu.VMEM)
     return pl.pallas_call(
-        attend_back_kernel,
-        out_shape=(
-            jax.ShapeDtypeStruct((ROWS, QR + KVR + HEAD), BF16),
-            jax.ShapeDtypeStruct((N_DP, E_ROWS, WO), BF16),
-        ),
-        in_specs=[vmem] * 9 + [pl.BlockSpec(memory_space=pl.ANY)],
-        out_specs=(vmem,) * 2,
-        scratch_shapes=[pltpu.VMEM((ROWS, LAT), BF16), pltpu.VMEM((ROWS, LAT), BF16)] + weight_scratch(),
+        attend_gradients_kernel,
+        out_shape=jax.ShapeDtypeStruct((N_DP, rows, WO), BF16),
+        in_specs=[vmem] * 4 + [pl.BlockSpec(memory_space=pl.ANY)] * 3,
+        out_specs=vmem,
+        scratch_shapes=[
+            pltpu.VMEM((ROWS, QR), BF16),
+            pltpu.VMEM((ROWS, KVR), BF16),
+            pltpu.VMEM((ROWS, WO), BF16),
+            pltpu.SemaphoreType.DMA((3,)),
+        ],
         compiler_params=pltpu.CompilerParams(vmem_limit_bytes=ATT_VMEM),
-        name="attend_back",
-    )(*d_attended, tab, *saved, pack)
+        name="attend_gradients",
+    )(*d_attended, d_query, d_key_value, saved[0], saved[1], saved[5])
+
+
+L_ROWS = SLICE + 16
+
+
+def late_kernel(rows_ref, gains_ref, normed_hbm, *refs):
+    packs = len(refs) == 6
+    out_ref, late_ref, normed_ref, sem, out_sem = refs[1:] if packs else (refs[0], refs[0], *refs[1:], None)
+    copy = pltpu.make_async_copy(normed_hbm, normed_ref, sem)
+    copy.start()
+    late_ref[:, SLICE:, :HEAD] = gains_ref[...]
+    late_ref[:, SLICE:, HEAD:] = jnp.zeros(gains_ref.shape, BF16)
+    copy.wait()
+    grad = dot_tn(normed_ref[...], rows_ref[...]).astype(BF16)
+    late_ref[:, :SLICE, :] = grad.reshape(N_DP, SLICE, 2 * HEAD)
+    if packs:
+        copy = pltpu.make_async_copy(late_ref, out_ref.at[:, E_ROWS:, : 2 * HEAD], out_sem)
+        copy.start()
+        copy.wait()
+
+
+def late_pack(normed, rows, gains, packs=None):
+    attn, q, kv, ffn = (g.reshape(N_DP, -1) for g in gains)
+    wide = ((0, 0), (0, 2 * HEAD - SLICE))
+    row = jnp.concatenate([jnp.pad(attn, wide), jnp.pad(ffn, wide), q, kv], axis=1)
+    row = jnp.pad(row, ((0, 0), (0, 16 * HEAD - row.shape[1]))).reshape(N_DP, 16, HEAD).astype(BF16)
+    vmem = pl.BlockSpec(memory_space=pltpu.VMEM)
+    hbm = pl.BlockSpec(memory_space=pl.ANY)
+    shape = (N_DP, L_ROWS, 2 * HEAD)
+    scratch = [pltpu.VMEM((ROWS, D), BF16), pltpu.SemaphoreType.DMA]
+    params = pltpu.CompilerParams(vmem_limit_bytes=ATT_VMEM)
+    if packs is None:
+        return pl.pallas_call(
+            late_kernel,
+            out_shape=jax.ShapeDtypeStruct(shape, BF16),
+            in_specs=[vmem, vmem, hbm],
+            out_specs=vmem,
+            scratch_shapes=scratch,
+            compiler_params=params,
+            name="late",
+        )(rows, row, normed)
+    return pl.pallas_call(
+        late_kernel,
+        out_shape=jax.ShapeDtypeStruct(packs.shape, BF16),
+        in_specs=[vmem, vmem, hbm, hbm],
+        out_specs=hbm,
+        scratch_shapes=[pltpu.VMEM(shape, BF16)] + scratch + [pltpu.SemaphoreType.DMA],
+        input_output_aliases={3: 0},
+        compiler_params=params,
+        name="late_in_packs",
+    )(rows, row, normed, packs)
 
 
 def normed_back_kernel(d_ref, pack_ref, out_ref, w_ref, sem):
@@ -515,23 +674,133 @@
     )(d_latent, pack)
 
 
-def attention_packs(w_qa, w_qb, w_kva, w_kvb, w_o, gains):
-    def pad(x, width, at=0):
-        return jnp.pad(x, ((0, 0), (at, width - at - x.shape[1])))
-
-    wo_t = w_o.T
+def home_kernel(
+    core_ref, tiles_ref, tiles_got_ref, rope_ref, rope_got_ref, early_ref, early_got_ref,
+    qa_ref, kva_ref, qb_ref, kvb_ref, wo_ref, gain_ref, heads_ref,
+):
+    first = core_ref[0] == 0
+
+    def halves(keep, got):
+        keep, got = keep.astype(F32), got.astype(F32)
+        return jnp.where(first, keep, got), jnp.where(first, got, keep)
+
+    wide = slice(0, SLICE)
+    gains = jnp.zeros(gain_ref.shape, F32)
+    for z in range(N_Z):
+        low, high = halves(tiles_ref[z], tiles_got_ref[z])
+        gains = gains + low[SLICE:] + high[SLICE:]
+        qa_ref[:, HEAD * z : HEAD * (z + 1)] = low[wide]
+        if z < 2:
+            qa_ref[:, HEAD * (z + 4) : HEAD * (z + 5)] = high[wide]
+        else:
+            kva_ref[:, HEAD * (z - 2) : HEAD * (z - 1)] = high[wide]
+    gain_ref[...] = gains
+    _, high = halves(rope_ref[...], rope_got_ref[...])
+    kva_ref[:, KVR:] = high[:, :ROPE]
+    low, high = halves(early_ref[wide], early_got_ref[wide])
+    at = WO - HEADS * VD
+    wo_ref[...] = jnp.concatenate([low[:, at:], high[:, at:]], axis=1)
+    heads_ref[...] = jnp.zeros(heads_ref.shape, F32)
+    valid = lax.broadcasted_iota(jnp.int32, (QR // N_DP, HEAD), 1) < NOPE + ROPE
+    more = A_ROWS - SLICE
+    for j in range(HEADS):
+        rows = QB_ROWS if j < 3 else slice(QB_ROWS.start + more, QB_ROWS.stop + more)
+        columns = slice(HEAD * (j % 3), HEAD * (j % 3 + 1))
+        for k, tile in enumerate(halves(early_ref[rows, columns], early_got_ref[rows, columns])):
+            start = (NOPE + ROPE) * (HEADS * k + j)
+            at = start // HEAD * HEAD
+            tile = jnp.where(valid, tile, 0.0)
+            window = jnp.concatenate([tile, jnp.zeros_like(tile)], axis=1)
+            if start > at:
+                window = pltpu.roll(window, start - at, 1)
+            heads_ref[:, at : at + 2 * HEAD] += window
+        rows = KVB_ROWS if j < 3 else slice(KVB_ROWS.start + more, KVB_ROWS.stop + more)
+        for k, tile in enumerate(halves(early_ref[rows, columns], early_got_ref[rows, columns])):
+            kvb_ref[:, HEAD * (HEADS * k + j) : HEAD * (HEADS * k + j + 1)] = tile
+    qb_ref[...] = heads_ref[:, : 2 * HEADS * (NOPE + ROPE)]
+
+
+def home(core, *pieces):
+    vmem = pl.BlockSpec(memory_space=pltpu.VMEM)
+    shapes = (
+        (SLICE, QR),
+        (SLICE, KVR + ROPE),
+        (QR // N_DP, 2 * HEADS * (NOPE + ROPE)),
+        (KVR // N_DP, 2 * LAT),
+        (SLICE, 2 * HEADS * VD),
+        (16, HEAD),
+    )
+    return pl.pallas_call(
+        home_kernel,
+        out_shape=tuple(jax.ShapeDtypeStruct(x, F32) for x in shapes),
+        in_specs=[pl.BlockSpec(memory_space=pltpu.SMEM)] + [vmem] * len(pieces),
+        out_specs=(vmem,) * len(shapes),
+        scratch_shapes=[pltpu.VMEM((QR // N_DP, 1152), F32)],
+        compiler_params=pltpu.CompilerParams(vmem_limit_bytes=ATT_VMEM),
+        name="home",
+    )(core, *pieces)
+
+
+def attention_pack_kernel(
+    core_ref, qa_ref, qb_ref, kva_ref, kvb_ref, wo_ref, ga_ref, gf_ref, gq_ref, gk_ref,
+    keep_ref, give_ref, heads_ref,
+):
     half = HEADS * VD
-    latent = (w_qa[:, :512], jnp.concatenate([w_qa[:, 512:], w_kva], axis=1))
-    qb = w_qb.reshape(QR // N_DP, 2, HEADS, NOPE + ROPE)
-    qb = jnp.pad(qb, ((0, 0), (0, 0), (0, 0), (0, HEAD - NOPE - ROPE)))
-    qb = qb.reshape(QR // N_DP, 2, LAT)
-    kvb = w_kvb.reshape(KVR // N_DP, 2, LAT)
-    packs = []
-    for i in range(2):
-        wide = jnp.concatenate([pad(latent[i], A_COLS - half), wo_t[:, half * i : half * (i + 1)]], axis=1)
-        low = jnp.concatenate([qb[:, i], gains], axis=1)
-        packs.append(jnp.concatenate([wide, low, pad(kvb[:, i], A_COLS)], axis=0))
-    return jnp.stack(packs)
+    first = core_ref[0] == 0
+
+    def put(rows, columns, zero, one):
+        keep_ref[rows, columns] = jnp.where(first, zero, one).astype(BF16)
+        give_ref[rows, columns] = jnp.where(first, one, zero).astype(BF16)
+
+    def blank(rows, columns):
+        zero = jnp.zeros((rows.stop - rows.start, columns.stop - columns.start), BF16)
+        keep_ref[rows, columns] = zero
+        give_ref[rows, columns] = zero
+
+    wide = slice(0, SLICE)
+    qa = qa_ref[...].astype(F32)
+    put(wide, slice(0, 256), qa[:, :256], qa[:, 512:])
+    put(wide, slice(256, 512), qa[:, 256:512], kva_ref[:, :256].astype(F32))
+    wo_t = wo_ref[...].astype(F32)
+    tail = jnp.zeros((SLICE, WO), F32)
+    rope = jnp.concatenate([kva_ref[:, 256:].astype(F32), jnp.zeros((SLICE, WO - ROPE), F32)], axis=1)
+    low = jnp.concatenate([tail[:, : WO - half], wo_t[:, :half]], axis=1)
+    high = jnp.concatenate([tail[:, : WO - half], wo_t[:, half:]], axis=1)
+    put(wide, slice(WO_AT, A_COLS), low, high + rope)
+    heads_ref[:, : 2 * HEADS * (NOPE + ROPE)] = qb_ref[...].astype(F32)
+    rows = QB_ROWS.stop - QB_ROWS.start
+    valid = lax.broadcasted_iota(jnp.int32, (rows, HEAD), 1) < NOPE + ROPE
+    tiles = []
+    for j in range(2 * HEADS):
+        at = (NOPE + ROPE) * j // HEAD * HEAD
+        by = (NOPE + ROPE) * j - at
+        window = heads_ref[:, at : at + 2 * HEAD]
+        if by > 0:
+            window = pltpu.roll(window, 2 * HEAD - by, 1)
+        tiles.append(jnp.where(valid, window[:, :HEAD], 0.0))
+    for j in range(HEADS):
+        put(QB_ROWS, slice(HEAD * j, HEAD * (j + 1)), tiles[j], tiles[HEADS + j])
+    gain_rows = [jnp.concatenate([g[...].astype(F32), jnp.zeros((1, 256 - SLICE), F32)], axis=1) for g in (ga_ref, gf_ref)]
+    last = [gq_ref[...].astype(F32), gk_ref[...].astype(F32), jnp.zeros((1, 256 - 64), F32)]
+    gain_rows.append(jnp.concatenate(last, axis=1))
+    gains = jnp.concatenate(gain_rows + [jnp.zeros((rows - 3, 256), F32)], axis=0)
+    put(QB_ROWS, slice(LAT, A_COLS), gains, gains)
+    kvb = kvb_ref[...].astype(F32)
+    put(KVB_ROWS, slice(0, LAT), kvb[:, :LAT], kvb[:, LAT:])
+    blank(KVB_ROWS, slice(LAT, A_COLS))
+
+
+def attention_packs(core, *weights):
+    vmem = pl.BlockSpec(memory_space=pltpu.VMEM)
+    return pl.pallas_call(
+        attention_pack_kernel,
+        out_shape=(jax.ShapeDtypeStruct((A_ROWS, A_COLS), BF16),) * 2,
+        in_specs=[pl.BlockSpec(memory_space=pltpu.SMEM)] + [vmem] * len(weights),
+        out_specs=(vmem, vmem),
+        scratch_shapes=[pltpu.VMEM((QR // N_DP, 1152), F32)],
+        compiler_params=pltpu.CompilerParams(vmem_limit_bytes=ATT_VMEM),
+        name="attention_pack",
+    )(core, *weights)
 
 
 def attention_gains(pack):
@@ -570,59 +839,69 @@
     )
 
 
-def ring_hop(x, by, cores=(0, 1)):
+def ring_hop(x, by):
     pairs = [
-        (c * N_Z + t, c * N_Z + (t + (by if c == 0 else -by)) % N_Z) for c in cores for t in range(N_Z)
+        (c * N_Z + t, c * N_Z + (t + (by if c == 0 else -by)) % N_Z) for c in range(2) for t in range(N_Z)
     ]
     return lax.ppermute(x, ("section", "tensor"), pairs)
 
 
-def ring_pieces(x):
-    near = ring_hop(x, 1)
-    return [x, near, ring_hop(x, -1), ring_hop(near, 1)]
-
-
-def ring_sum(layer, pieces):
-    def add(*terms):
-        return sum(x.astype(F32) for x in terms).astype(BF16)
-
-    pair = [(1 - layer, layer)]
-    far, near, after, mine = (
-        add(pieces[k], lax.ppermute(pieces[k], "section", pair)) for k in (3, 1, 2, 0)
-    )
-    cores = (layer,)
-    near = add(near, ring_hop(far, -1, cores))
-    return add(mine, ring_hop(near, -1, cores), ring_hop(after, 1, cores))
-
-
-def layer_forward(own, rows, x_own, pack, gains, ffn_weights, tab):
+def add(*terms):
+    return sum(x.astype(F32) for x in terms).astype(BF16)
+
+
+def ring_pairs(pieces):
+    got = [to_core(x) for x in pieces[N_Z:]]
+    return add(pieces[3], got[3]), add(pieces[2], got[2]), (pieces[1], got[1]), (pieces[0], got[0])
+
+
+def ring_first(pairs):
+    far, after, near, mine = pairs
+    return ring_hop(far, -1), ring_hop(after, 1), near, mine
+
+
+def ring_last(first):
+    far, after, near, mine = first
+    return add(*mine, after, ring_hop(add(*near, far), -1))
+
+
+tie = lax.optimization_barrier
+
+
+def attention_forward(rows, x_own, pack, gains, tab, other=()):
     core = lax.axis_index("section").reshape(1)
     normed, latent = latents(rows, gains["attn"], pack)
+    latent, other = tie((latent, other))
     part, *saved, latent_own = attend(
         core, latent, to_core(latent), tab, gains["q"], gains["kv"], pack
     )
     middle = x_own + RES_SCALE * scatter_tokens(part)
+    return middle, (normed, latent_own, saved), other
+
+
+def layer_forward(own, x_own, middle, saved, gains, ffn_weights, far=None):
     ffn_rows = gather_dp(norm(middle, gains["ffn"]).astype(BF16))
+    if far is not None:
+        ffn_rows, far = tie((ffn_rows, far))
+        ffn_weights = ffn_weights[:3] + [far] + ffn_weights[3:] + [to_core(far)]
     part, gu, hidden = ffn_forward(own, ffn_rows, ffn_weights)
-    return part, (x_own, middle, ffn_rows, gu, hidden, normed, latent_own, saved)
+    return part, (x_own, middle, ffn_rows, gu, hidden) + saved, ffn_weights
 
 
 def layer_out_rows(part, saved):
-    return (saved[1] + RES_SCALE * scatter_dp(part)).astype(BF16)
-
-
-def layer_backward(own, grad_own, d_rows, saved, pack, gains, ffn_weights, tab, after_gather):
+    return (saved[1] + RES_SCALE * part).astype(BF16)
+
+
+def middle_backward(grad_own, d_normed_two, saved, gains):
+    d_middle, ffn_gain = norm_back(saved[1], gains["ffn"], d_normed_two)
+    return d_middle + grad_own, ffn_gain
+
+
+def attention_backward(part, d_middle, saved, pack, gains, also=()):
     core = lax.axis_index("section")
     t = lax.axis_index("tensor")
-    x_own, middle, ffn_rows, gu, hidden, normed, latent_own, saved = saved
-    part, ffn_grads = ffn_backward(own, d_rows, ffn_rows, gu, hidden, ffn_weights)
-    d_normed_two = scatter_dp(part)
-    d_middle, ffn_gain = norm_back(middle, gains["ffn"], d_normed_two)
-    d_middle = d_middle + grad_own
-    d_attended = gather_tokens((RES_SCALE * d_middle).astype(BF16))
-    d_attended, after_gather = lax.optimization_barrier((d_attended, after_gather))
-    part, early = attend_back(d_attended, tab, saved, pack)
-    d_latent = scatter_tokens(part)
+    x_own, _, _, _, _, _, latent_own, _ = saved
+    d_latent, also = tie((scatter_tokens(part), also))
     d_q, q_gain = norm_back(latent_own[:, :QR], gains["q"], d_latent[:, :QR])
     d_c, kv_gain = norm_back(latent_own[:, QR:], gains["kv"], d_latent[:, QR : QR + KVR])
     d_rope = d_latent[:, QR + KVR + NOPE : QR + KVR + NOPE + ROPE]
@@ -644,21 +923,11 @@
 
     rows = jnp.stack([piece(0), z_hop(piece(3), -1), z_hop(piece(2), 2), z_hop(piece(1), 1)])
     rows = rows.reshape(N_Z, 2, SHARD, 2 * HEAD).transpose(1, 0, 2, 3).reshape(ROWS, 2 * HEAD)
-    down_grad = dot_tn(normed, rows).astype(BF16).reshape(N_DP, SLICE, 2 * HEAD)
-    return d_block, ffn_grads, early, down_grad, (attn_gain, ffn_gain, q_gain, kv_gain), after_gather
+    return d_block, rows, (attn_gain, q_gain, kv_gain), also
 
 
 def scatter_sum(x):
     return jnp.sum(lax.all_to_all(x, "dp", 0, 0).astype(F32), axis=0)
-
-
-def late_pack(down_grad, gains):
-    attn, ffn, q, kv = (g.reshape(N_DP, -1) for g in gains)
-    wide = ((0, 0), (0, 2 * HEAD - SLICE))
-    row = jnp.concatenate([jnp.pad(attn, wide), jnp.pad(ffn, wide), q, kv], axis=1)
-    row = jnp.pad(row, ((0, 0), (0, 16 * HEAD - row.shape[1]))).reshape(N_DP, 16, HEAD)
-    row = jnp.pad(row, ((0, 0), (0, 0), (0, HEAD))).astype(BF16)
-    return jnp.concatenate([down_grad, row], axis=1)
 
 
 def body(
@@ -679,25 +948,18 @@
     w_down,
 ):
     core = lax.axis_index("section")
-    gains = jnp.stack(
-        [
-            jnp.pad(g, (0, A_COLS - LAT - g.shape[0]))
-            for g in (g_attn[0], g_ffn[0], jnp.concatenate([g_q[0], g_kv[0]]))
-        ]
-    )
-    gains = jnp.pad(gains, ((0, QR // N_DP - 3), (0, 0)))
-    packs = attention_packs(w_qa[0], w_qb[0], w_kva[0], w_kvb[0], w_o[0], gains)
-    keep = lax.dynamic_index_in_dim(packs, core, 0, keepdims=False)
-    give = lax.dynamic_index_in_dim(packs, 1 - core, 0, keepdims=False)
+    keep, give = attention_packs(
+        core.reshape(1), w_qa[0], w_qb[0], w_kva[0], w_kvb[0], w_o[0].T, g_attn, g_ffn, g_q, g_kv
+    )
     attn_one, attn_two = by_core(core, keep, to_core(give))
     attn_one = lax.all_gather(attn_one, "dp")
     attn_two = lax.all_gather(attn_two, "dp")
 
-    blocks = lax.all_to_all(ffn_pack(w_gate[0], w_up[0], w_down[0]), "dp", 0, 0)
+    blocks = lax.all_to_all(ffn_pack(w_gate[0], w_up[0], w_down[0].T), "dp", 0, 0)
     tab = head_tables(seq_lengths)
     blocks, cotangent, layer_input = lax.optimization_barrier((blocks, cotangent, layer_input))
-    mine = ring_pieces(blocks.reshape(D, MATS))
-    ffn_weights = mine + [to_core(piece) for piece in mine]
+    weights = blocks.reshape(D, MATS)
+    near, after = ring_hop(weights, 1), ring_hop(weights, -1)
 
     def token_rows(x):
         packs = x.reshape(2, N_Z, SHARD, D)
@@ -707,70 +969,99 @@
     def d_mlp_rows(grad):
         return gather_dp((RES_SCALE * grad).astype(BF16))
 
+    def d_attended_rows(d_middle):
+        return gather_tokens((RES_SCALE * d_middle).astype(BF16))
+
     cot_own = token_rows(cotangent)[0][:SHARD].astype(F32)
-    d_rows_two = d_mlp_rows(cot_own)
-    attn_one, d_rows_two, tab = lax.optimization_barrier((attn_one, d_rows_two, tab))
+    attn_one, tab = tie((attn_one, tab))
     gains_one, gains_two = attention_gains(attn_one), attention_gains(attn_two)
-    own_one = (core == 0).astype(jnp.int32).reshape(1)
-    own_two = 1 - own_one
+    own_one = jnp.stack([(core == 0).astype(jnp.int32), core])
+    own_two = jnp.stack([(core == 1).astype(jnp.int32), core])
 
     rows = token_rows(layer_input)
     x_own = rows[0][:SHARD].astype(F32)
-    part, saved_one = layer_forward(own_one, rows, x_own, attn_one, gains_one, ffn_weights, tab)
-    out_one = layer_out_rows(part, saved_one)
+    middle, saved, (near, after) = attention_forward(
+        rows, x_own, attn_one, gains_one, tab, (near, after)
+    )
+    mine = [weights, near, after]
+    ffn_weights = mine + [to_core(piece) for piece in mine]
+    middle, near, cot_rows = tie((middle, near, (RES_SCALE * cot_own).astype(BF16)))
+    d_rows_two = lax.all_gather(cot_rows, "dp").reshape(TOKENS, D)
+    part, saved_one, ffn_weights = layer_forward(
+        own_one, x_own, middle, saved, gains_one, ffn_weights, ring_hop(near, 1)
+    )
+    out_one = layer_out_rows(scatter_dp(part), saved_one)
     rows_one = gather_tokens(out_one)
-    part_two, saved_two = layer_forward(
-        own_two, rows_one, out_one.astype(F32), attn_two, gains_two, ffn_weights, tab
-    )
-    in_grad_two, ffn_grads_two, early_two, down_two, dg_two, part_two = layer_backward(
-        own_two, cot_own, d_rows_two, saved_two, attn_two, gains_two, ffn_weights, tab, part_two
+    x_own = out_one.astype(F32)
+    middle, saved, _ = attention_forward(rows_one, x_own, attn_two, gains_two, tab)
+    part_two, saved_two, _ = layer_forward(own_two, x_own, middle, saved, gains_two, ffn_weights)
+
+    ffn_rows, gu, hidden = saved_two[2:5]
+    part, d_gu = ffn_backward(own_two, d_rows_two, gu, ffn_weights)
+    grads_two = ffn_gradients(own_two, d_rows_two, ffn_rows, d_gu, hidden)
+    d_normed_two = scatter_dp(part)
+    ring_two = ring_pairs(grads_two)
+    d_middle, ffn_gain_two = middle_backward(cot_own, d_normed_two, saved_two, gains_two)
+    d_attended = d_attended_rows(d_middle)
+    part, d_query, d_key_value = attend_back(d_attended, tab, saved_two[-1], attn_two)
+    packs_two = attend_gradients(d_attended, saved_two[-1], d_query, d_key_value, E_ROWS + L_ROWS)
+    in_grad_two, rows, dg_two, part_two = attention_backward(
+        part, d_middle, saved_two, attn_two, gains_two, scatter_dp(part_two)
+    )
+    packs_two = late_pack(saved_two[5], rows, (*dg_two, ffn_gain_two), packs_two).reshape(-1, WO)
+    in_grad_two, ring_two = tie((in_grad_two, ring_two))
+    ring_two = ring_first(ring_two)
+
+    grad_one = in_grad_two.astype(F32)
+    d_rows, packs_two = tie((d_mlp_rows(grad_one), packs_two))
+    packs_two = lax.psum_scatter(packs_two, "dp", scatter_dimension=0, tiled=True)
+    ffn_rows, gu, hidden = saved_one[2:5]
+    part, d_gu = ffn_backward(own_one, d_rows, gu, ffn_weights)
+    grads_one = ffn_gradients(own_one, d_rows, ffn_rows, d_gu, hidden)
+    d_normed_two = scatter_dp(part)
+    total_two = ring_last(ring_two)
+    d_normed_two, total_two = tie((d_normed_two, total_two))
+    d_middle, ffn_gain_one = middle_backward(grad_one, d_normed_two, saved_one, gains_one)
+    d_attended = d_attended_rows(d_middle)
+    part, d_query, d_key_value = attend_back(d_attended, tab, saved_one[-1], attn_one)
+    early_one = attend_gradients(d_attended, saved_one[-1], d_query, d_key_value, E_ROWS)
+    part, early_one = tie((part, early_one))
+    early_one = scatter_sum(early_one)
+    home_two = lax.all_to_all(total_two, "dp", 0, 0)
+    part, home_two = tie((part, home_two))
+    in_grad_one, rows, dg_one, grads_one = attention_backward(
+        part, d_middle, saved_one, attn_one, gains_one, grads_one
+    )
+    rows, pairs = tie((rows, ring_pairs(grads_one)))
+    total_one = ring_last(ring_first(pairs))
+    in_grad_one, dg_one, early_one, part_two, packs_two = tie(
+        (in_grad_one, dg_one, early_one, part_two, packs_two)
     )
     rows_two = gather_tokens(layer_out_rows(part_two, saved_two))
-    early_two = lax.psum_scatter(
-        early_two.reshape(N_DP * E_ROWS, WO), "dp", scatter_dimension=0, tiled=True
-    )
-    grad_one = in_grad_two.astype(F32)
-    d_rows_one = d_mlp_rows(grad_one)
-    d_rows_one, ffn_grads_two = lax.optimization_barrier((d_rows_one, ffn_grads_two))
-    in_grad_one, ffn_grads_one, early_one, down_one, dg_one, _ = layer_backward(
-        own_one, grad_one, d_rows_one, saved_one, attn_one, gains_one, ffn_weights, tab, ()
-    )
-    early_one = lax.psum_scatter(
-        early_one.reshape(N_DP * E_ROWS, WO), "dp", scatter_dimension=0, tiled=True
-    )
-
-    totals = [ring_sum(0, ffn_grads_one), ring_sum(1, ffn_grads_two)]
-    total = jnp.where(core == 0, totals[0], totals[1]).reshape(N_DP, SLICE, MATS)
-    gate_grad, up_grad, down_grad = ffn_unpack(lax.all_to_all(total, "dp", 0, 0))
-
-    late = jnp.concatenate([late_pack(down_one, dg_one), late_pack(down_two, dg_two)], axis=1)
-    late = scatter_sum(late)
-    tiles = from_zero(jnp.stack(gather_z(late[:, :HEAD].astype(BF16)))).astype(F32)
-    late = late.reshape(2, SLICE + 16, 2 * HEAD)
-    tiles = tiles.reshape(N_Z, 2, SLICE + 16, HEAD)
-    sums = []
-    for layer, early in enumerate((early_one, early_two)):
-        lat = tiles[:, layer, :SLICE].transpose(1, 0, 2).reshape(SLICE, N_Z * HEAD)
-        early = early.astype(F32)
-        wide = jnp.concatenate([lat, late[layer, :SLICE, HEAD:], early[:SLICE]], axis=1)
-        low = jnp.concatenate([early[SLICE:A_ROWS], early[A_ROWS:, : LAT - WO]], axis=1)
-        sums.append((wide, low, jnp.sum(tiles[:, layer, SLICE:], axis=0)))
-    home = []
-    for one, two in zip(*sums):
-        keep = jnp.where(core == 0, one, two)
+    late_one = scatter_sum(late_pack(saved_one[5], rows, (*dg_one, ffn_gain_one)))
+
+    total_one, late_one = tie((total_one, late_one))
+    home_one = lax.all_to_all(total_one, "dp", 0, 0)
+    got_one = lax.ppermute(home_one, "section", [(1, 0)])
+    got_two = lax.ppermute(home_two, "section", [(0, 1)])
+    gate_grad, up_grad, down_grad = ffn_unpack(core.reshape(1), home_one, got_one, home_two, got_two)
+
+    packs_two = packs_two.astype(F32)
+    early_two, late_two = packs_two[:E_ROWS], packs_two[E_ROWS:, : 2 * HEAD]
+
+    def homeward(one, two):
         give = jnp.where(core == 0, two, one)
-        home.append(by_core(core, keep, to_core(give)))
-    (wide_low, wide_high), (low_low, low_high), (dg_low, dg_high) = home
-    qa_grad = jnp.concatenate([wide_low[:, :512], wide_high[:, :256]], axis=1)
-    kva_grad = wide_high[:, 256 : 256 + KVR + ROPE]
-    at = LAT + WO - HEADS * VD
-    wo_grad = jnp.concatenate([wide_low[:, at:], wide_high[:, at:]], axis=1).T
-    qb_rows, kvb_rows = slice(0, QR // N_DP), slice(QR // N_DP, A_ROWS - SLICE)
-    heads = jnp.concatenate([low_low[qb_rows], low_high[qb_rows]], axis=1)
-    heads = heads.reshape(QR // N_DP, 2 * HEADS, HEAD)[:, :, : NOPE + ROPE]
-    qb_grad = heads.reshape(QR // N_DP, 2 * HEADS * (NOPE + ROPE))
-    kvb_grad = jnp.concatenate([low_low[kvb_rows], low_high[kvb_rows]], axis=1)
-    gains = (dg_low + dg_high).reshape(-1)
+        return jnp.where(core == 0, one, two), to_core(give)
+
+    tiles = jnp.concatenate([late_one[:, :HEAD], late_two[:, :HEAD]], axis=0).astype(BF16)
+    tiles = from_zero(jnp.stack(gather_z(tiles))).reshape(N_Z, 2, SLICE + 16, HEAD)
+    qa_grad, kva_grad, qb_grad, kvb_grad, wo_grad, gains = home(
+        core.reshape(1),
+        *homeward(tiles[:, 0], tiles[:, 1]),
+        *homeward(late_one[:SLICE, HEAD:], late_two[:SLICE, HEAD:]),
+        *homeward(early_one, early_two),
+    )
+    gains = gains.reshape(-1)
 
     def gain_part(at, width):
         return gains[at : at + width][None]
@@ -791,11 +1082,11 @@
         kva_grad[None],
         gain_part(4 * HEAD + QR // N_DP, KVR // N_DP),
         kvb_grad[None],
-        wo_grad[None],
+        wo_grad.T[None],
         gain_part(2 * HEAD, SLICE),
         gate_grad[None],
         up_grad[None],
-        down_grad[None],
+        down_grad.T[None],
     )
 
 

time: 698 us -> 653 us (0.936)
  waiting for transfers between devices: 267 us -> 226 us
  blocking collectives: 43.9 us -> 26.7 us
  Pallas kernels: 88.8 us -> 101 us
    ppermute x9, waiting for transfers between devices: 63.9 us -> 13.8 us  [ring_hop(): return lax.ppermute(x, ('section', 'tensor'), pairs)]
    pallas_call x0 -> x8, Pallas kernels: none -> 27.2 us  [the longest x2 12.7 us: ffn_gradients(): pl.pallas_call(ffn_gradients_kernel, out_shape=tuple((jax.ShapeDtypeStruc...]
    all_gather x1, waiting for transfers between devices: 9.73 us -> 34.2 us  [body(): attn_one = lax.all_gather(attn_one, 'dp')]
    all_to_all x2 -> x1, blocking collectives: 43.9 us -> 26.7 us  [scatter_dp(): pieces = lax.all_to_all(part.reshape(N_DP, SHARD, D), 'dp', 0, 0)]
    all_to_all x4 -> x3, waiting for transfers between devices: 63.7 us -> 46.6 us  [gather_dp(): lax.all_to_all(copies, 'dp', 0, 0).reshape(N_DP * x.shape[0], x.shape[1])]
    ppermute x8 -> x2, starting transfers between devices: 22.8 us -> 6.51 us  [the longest x1 5.22 us: body(): got_one = lax.ppermute(home_one, 'section', [(1, 0)])]
    ppermute x36, waiting for transfers between devices: 19.7 us -> 32 us  [z_hop(): return lax.ppermute(x, 'tensor', [(i, (i + by) % N_Z) for i in range(N_Z)])]
    pallas_call x2, Pallas kernels: 28.3 us -> 16.6 us  [ffn_backward(): pl.pallas_call(ffn_backward_kernel, out_shape=(jax.ShapeDtypeStruct((TOKE...]
  transfers between devices with their start and end apart: 89 -> 93, of which waited for: 39 -> 41; matrix products, arithmetic and copies ran while one was open for 11% -> 12% of each run, Pallas kernels for 5% -> 13%
where the time goes in v2:
time: 653 us; the launch traced here: 642 us
  waiting for transfers between devices  226 us (35%)
  starting transfers between devices  169 us (26%)
  Pallas kernels  101 us (15%)
  other arithmetic  63.9 us (10%)
  local copies, waits for them, and re-layouts  39.6 us (6%)
  blocking collectives  26.7 us (4%)
  between operations  16.1 us (2%)
    all_to_all x3, waiting for transfers between devices, gather_dp(): lax.all_to_all(copies, 'dp', 0, 0).reshape(N_DP * x.shape[0], x.shape[1])  46.6 us
    ppermute x36, starting transfers between devices, z_hop(): return lax.ppermute(x, 'tensor', [(i, (i + by) % N_Z) for i in range(N_Z)])  46 us
    ppermute x31, starting transfers between devices, to_core(): return lax.ppermute(x, 'section', [(0, 1), (1, 0)])  39.6 us
    all_gather x1, waiting for transfers between devices, body(): attn_one = lax.all_gather(attn_one, 'dp')  34.2 us
    all_to_all x1, waiting for transfers between devices, body(): lax.all_to_all(ffn_pack(w_gate[0], w_up[0], w_down[0].T), 'dp', 0, 0)  33 us
    ppermute x36, waiting for transfers between devices, z_hop(): return lax.ppermute(x, 'tensor', [(i, (i + by) % N_Z) for i in range(N_Z)])  32 us
    all_to_all x1, blocking collectives, scatter_dp(): pieces = lax.all_to_all(part.reshape(N_DP, SHARD, D), 'dp', 0, 0)  26.7 us
    all_to_all x3, waiting for transfers between devices, scatter_dp(): pieces = lax.all_to_all(part.reshape(N_DP, SHARD, D), 'dp', 0, 0)  24.6 us
  transfers between devices with their start and end apart: 93, of which 41 were waited for; matrix products, arithmetic and copies ran while one was open for 12% of the time, Pallas kernels for 13%

profile of v2, /device:TPU:1, one launch (start us, length us, event | category | flops | bytes accessed | tf_op | source)
XLA Modules:
  0.0 642.1 jit_solution(1797680579858172098)
XLA Ops:
  22.2 7.0 %all-to-all-start = ((bf16[16,160,384]{2,1,0:T(8,128)(2,1)}), bf16[16,160,384]{2,1,0:T(8,128)(2,1)}, u32[]{:S(2)}, u32[]{:S(2)}) async-start(bf16[16,160,384]{2,1,0:T(8,128)(2,1)} %ffn_pack.1), calls=%async_computation | async-start | bytes 3932160 | tf_op jit(solution)/shard_map/all_to_all | solution.py:958
  30.4 33.0 %all-to-all-done = bf16[16,160,384]{2,1,0:T(8,128)(2,1)} async-done(((bf16[16,160,384]{2,1,0:T(8,128)(2,1)}), bf16[16,160,384]{2,1,0:T(8,128)(2,1)}, u32[]{:S(2)}, u32[]{:S(2)}) %all-to-all-start) | async-done | bytes 1966112 | tf_op jit(solution)/shard_map/all_to_all | solution.py:958
  68.5 34.2 %all-gather.7.cloned.1.call-done = bf16[3584,896]{1,0:T(8,128)(2,1)} async-done(((bf16[224,896]{1,0:T(8,128)(2,1)}), bf16[3584,896]{1,0:T(8,128)(2,1)}) %all-gather.7.cloned.1.call-update) | async-done | bytes 6422544 | tf_op jit(solution)/shard_map/all_gather | solution.py:955
  137.8 28.7 %all-to-all-done.1 = bf16[16,16,2560]{2,1,0:T(8,128)(2,1)} async-done(((bf16[16,16,2560]{2,1,0:T(8,128)(2,1)}), bf16[16,16,2560]{2,1,0:T(8,128)(2,1)}, u32[]{:S(2)}, u32[]{:S(2)}) %all-to-all-start.1) | async-done | bytes 1310752 | tf_op jit(solution)/shard_map/all_to_all | solution.py:92
  170.8 8.2 %ffn_forward.2 = (bf16[256,2560]{1,0:T(8,128)(2,1)}, f32[256,1024]{1,0:T(8,128)}, bf16[256,512]{1,0:T(8,128)(2,1)}) custom-call(s32[2]{0:T(128)} %pad_add_fusion.own_ref, bf16[256,2560]{1,0:T(8,128)(2,1)} %bitcast.26.n_ref, bf16[2560,384]{1,0:T(8,128)(2,1)} %bitcast.22.refs_0_, bf16[2560,384]{1,0:T(8,128)(2,1)} %collective-permute-done.1.refs_1_, ...), custom_call_target="tpu_custom_call" | custom-call | tf_op jit(solution)/shard_map/ffn_forward/pallas_call | solution.py:162
  179.0 26.7 %all_to_all.60 = bf16[16,16,2560]{2,1,0:T(8,128)(2,1)S(1)} all-to-all(bf16[16,16,2560]{2,1,0:T(8,128)(2,1)} %bitcast.197), channel_id=1, replica_groups=mesh['section'=2,'tensor'=4,'dp'=16] {'dp'}, dimensions={0} | all-to-all | bytes 2621440 | tf_op jit(solution)/shard_map/all_to_all | solution.py:96
  251.8 17.9 %all-to-all-done.3 = bf16[16,16,2560]{2,1,0:T(8,128)(2,1)} async-done(((bf16[16,16,2560]{2,1,0:T(8,128)(2,1)}), bf16[16,16,2560]{2,1,0:T(8,128)(2,1)}, u32[]{:S(2)}, u32[]{:S(2)}) %all-to-all-start.3) | async-done | bytes 1310752 | tf_op jit(solution)/shard_map/all_to_all | solution.py:92
  269.7 8.1 %ffn_forward.3 = (bf16[256,2560]{1,0:T(8,128)(2,1)}, f32[256,1024]{1,0:T(8,128)}, bf16[256,512]{1,0:T(8,128)(2,1)}) custom-call(s32[2]{0:T(128)} %pad_add_fusion.1.own_ref, bf16[256,2560]{1,0:T(8,128)(2,1)} %bitcast.31.n_ref, bf16[2560,384]{1,0:T(8,128)(2,1)} %bitcast.22.refs_0_, bf16[2560,384]{1,0:T(8,128)(2,1)} %collective-permute-done.1.refs_1_, ...), custom_call_target="tpu_custom_call" | custom-call | tf_op jit(solution)/shard_map/ffn_forward/pallas_call | solution.py:162
  277.8 8.3 %ffn_backward.2 = (bf16[256,2560]{1,0:T(8,128)(2,1)}, bf16[256,1024]{1,0:T(8,128)(2,1)}) custom-call(s32[2]{0:T(128)} %pad_add_fusion.1.own_ref, bf16[256,2560]{1,0:T(8,128)(2,1)} %all-gather.11.cloned.1.call-done.dm_ref, f32[256,1024]{1,0:T(8,128)} %get-tuple-element.154.gu_ref, bf16[2560,384]{1,0:T(8,128)(2,1)} %bitcast.22.refs_0_, ...), custom_call_target="tpu_custom_call" | custom-call | tf_op jit(solution)/shard_map/ffn_backward/pallas_call | solution.py:204
  293.2 13.8 %all-to-all-done.4 = bf16[16,16,2560]{2,1,0:T(8,128)(2,1)} async-done(((bf16[16,16,2560]{2,1,0:T(8,128)(2,1)}), bf16[16,16,2560]{2,1,0:T(8,128)(2,1)}, u32[]{:S(2)}, u32[]{:S(2)}) %all-to-all-start.4) | async-done | bytes 1310752 | tf_op jit(solution)/shard_map/all_to_all | solution.py:96
  338.2 6.3 ffn_gradients.2
  369.5 6.7 %all-to-all-start.6 = ((bf16[16,16,2560]{2,1,0:T(8,128)(2,1)}), bf16[16,16,2560]{2,1,0:T(8,128)(2,1)}, u32[]{:S(2)}, u32[]{:S(2)}) async-start(bf16[16,16,2560]{2,1,0:T(8,128)(2,1)} %broadcast_in_dim.142), calls=%async_computation.6 | async-start | bytes 2621440 | tf_op jit(solution)/shard_map/all_to_all | solution.py:92
  402.7 8.3 %ffn_backward.3 = (bf16[256,2560]{1,0:T(8,128)(2,1)}, bf16[256,1024]{1,0:T(8,128)(2,1)}) custom-call(s32[2]{0:T(128)} %pad_add_fusion.own_ref, bf16[256,2560]{1,0:T(8,128)(2,1)} %bitcast.35.dm_ref, f32[256,1024]{1,0:T(8,128)} %get-tuple-element.180.gu_ref, bf16[2560,384]{1,0:T(8,128)(2,1)} %bitcast.22.refs_0_, ...), custom_call_target="tpu_custom_call" | custom-call | tf_op jit(solution)/shard_map/ffn_backward/pallas_call | solution.py:204
  411.0 6.5 %all-to-all-start.7 = ((bf16[16,16,2560]{2,1,0:T(8,128)(2,1)}), bf16[16,16,2560]{2,1,0:T(8,128)(2,1)S(1)}, u32[]{:S(2)}, u32[]{:S(2)}) async-start(bf16[16,16,2560]{2,1,0:T(8,128)(2,1)} %bitcast.195), calls=%async_computation.7 | async-start | bytes 2621440 | tf_op jit(solution)/shard_map/all_to_all | solution.py:96
  427.6 9.9 %all-to-all-done.7 = bf16[16,16,2560]{2,1,0:T(8,128)(2,1)S(1)} async-done(((bf16[16,16,2560]{2,1,0:T(8,128)(2,1)}), bf16[16,16,2560]{2,1,0:T(8,128)(2,1)S(1)}, u32[]{:S(2)}, u32[]{:S(2)}) %all-to-all-start.7) | async-done | bytes 1310752 | tf_op jit(solution)/shard_map/all_to_all | solution.py:96
  438.3 7.1 %all-to-all-start.8 = ((bf16[16,80,384]{2,1,0:T(8,128)(2,1)}), bf16[16,80,384]{2,1,0:T(8,128)(2,1)}, u32[]{:S(2)}, u32[]{:S(2)}) async-start(bf16[16,80,384]{2,1,0:T(8,128)(2,1)} %add_convert_fusion.4), calls=%async_computation.8 | async-start | bytes 1966080 | tf_op jit(solution)/shard_map/all_to_all | solution.py:1030
  460.8 6.2 attend_back.3
  475.8 6.4 ffn_gradients.3
  485.1 6.9 %all-to-all-start.9 = ((bf16[16,288,384]{2,1,0:T(8,128)(2,1)}), bf16[16,288,384]{2,1,0:T(8,128)(2,1)}, u32[]{:S(2)}, u32[]{:S(2)}) async-start(bf16[16,288,384]{2,1,0:T(8,128)(2,1)} %attend_gradients.3), calls=%async_computation.9 | async-start | bytes 7077888 | tf_op jit(solution)/shard_map/all_to_all | solution.py:930
  529.1 20.0 %all-to-all-done.9 = bf16[16,288,384]{2,1,0:T(8,128)(2,1)} async-done(((bf16[16,288,384]{2,1,0:T(8,128)(2,1)}), bf16[16,288,384]{2,1,0:T(8,128)(2,1)}, u32[]{:S(2)}, u32[]{:S(2)}) %all-to-all-start.9) | async-done | bytes 3538976 | tf_op jit(solution)/shard_map/all_to_all | solution.py:930
  563.3 8.0 %all-to-all-start.10 = ((bf16[16,176,256]{2,1,0:T(8,128)(2,1)}), bf16[16,176,256]{2,1,0:T(8,128)(2,1)S(1)}, u32[]{:S(2)}, u32[]{:S(2)}) async-start(bf16[16,176,256]{2,1,0:T(8,128)(2,1)} %late.1), calls=%async_computation.10 | async-start | bytes 2883584 | tf_op jit(solution)/shard_map/all_to_all | solution.py:930
  585.6 6.5 %collective-permute-start.55 = (bf16[64,2560]{1,0:T(8,128)(2,1)S(1)}, bf16[64,2560]{1,0:T(8,128)(2,1)S(1)}, u32[]{:S(2)}, u32[]{:S(2)}) collective-permute-start(bf16[64,2560]{1,0:T(8,128)(2,1)S(1)} %get-tuple-element.306), channel_id=1, source_target_pairs={{0,64},{64,0},{1,65},{65,1},{2,66},{66,2},{3,67},{67,3},{4,68},{68... | collective-permute-start | bytes 983048 | tf_op jit(solution)/shard_map/ppermute | solution.py:45
  599.2 6.9 %all-to-all-start.11 = ((bf16[16,80,384]{2,1,0:T(8,128)(2,1)}), bf16[16,80,384]{2,1,0:T(8,128)(2,1)S(1)}, u32[]{:S(2)}, u32[]{:S(2)}) async-start(bf16[16,80,384]{2,1,0:T(8,128)(2,1)} %add_convert_fusion), calls=%async_computation.11 | async-start | bytes 1966080 | tf_op jit(solution)/shard_map/all_to_all | solution.py:1044
  608.8 11.4 %all-to-all-done.11.one = bf16[16,80,384]{2,1,0:T(8,128)(2,1)S(1)} async-done(((bf16[16,80,384]{2,1,0:T(8,128)(2,1)}), bf16[16,80,384]{2,1,0:T(8,128)(2,1)S(1)}, u32[]{:S(2)}, u32[]{:S(2)}) %all-to-all-start.11) | async-done | bytes 983072 | tf_op jit(solution)/shard_map/all_to_all | solution.py:1044
  (598 shorter events, 323.0 us)
Async XLA Ops:
  7.2 95.5 %all-gather.7.cloned.1.call-start = ((), (), s32[]{:S(2)}) async-start(), calls=%async_computation.13 | async-start | bytes 6823936 | tf_op jit(solution)/shard_map/all_gather | solution.py:955
  22.2 41.2 %all-to-all-start = ((bf16[16,160,384]{2,1,0:T(8,128)(2,1)}), bf16[16,160,384]{2,1,0:T(8,128)(2,1)}, u32[]{:S(2)}, u32[]{:S(2)}) async-start(bf16[16,160,384]{2,1,0:T(8,128)(2,1)} %ffn_pack.1), calls=%async_computation | async-start | bytes 3932160 | tf_op jit(solution)/shard_map/all_to_all | solution.py:958
  29.3 187.2 %all-gather.9.cloned.1.call-start = ((), (), s32[]{:S(2)}) async-start(), calls=%async_computation.14 | async-start | bytes 6823936 | tf_op jit(solution)/shard_map/all_gather | solution.py:956
  63.5 42.9 %collective-permute-start.2 = (bf16[2560,384]{1,0:T(8,128)(2,1)}, bf16[2560,384]{1,0:T(8,128)(2,1)}, u32[]{:S(2)}, u32[]{:S(2)}) collective-permute-start(bf16[2560,384]{1,0:T(8,128)(2,1)} %bitcast.22.refs_0_), channel_id=1, source_target_pairs={{0,48},{16,0},{32,16},{48,32},{64,80},{80,96},{96,112},{112,64},{1... | collective-permute-start | bytes 5898248 | tf_op jit(solution)/shard_map/ppermute | solution.py:846
  65.1 45.0 %collective-permute-start.1 = (bf16[2560,384]{1,0:T(8,128)(2,1)}, bf16[2560,384]{1,0:T(8,128)(2,1)}, u32[]{:S(2)}, u32[]{:S(2)}) collective-permute-start(bf16[2560,384]{1,0:T(8,128)(2,1)} %bitcast.22.refs_0_), channel_id=1, source_target_pairs={{0,16},{16,32},{32,48},{48,0},{64,112},{80,64},{96,80},{112,96},{1... | collective-permute-start | bytes 5898248 | tf_op jit(solution)/shard_map/ppermute | solution.py:846
  128.2 38.3 %collective-permute-start.8 = (bf16[2560,384]{1,0:T(8,128)(2,1)}, bf16[2560,384]{1,0:T(8,128)(2,1)S(1)}, u32[]{:S(2)}, u32[]{:S(2)}) collective-permute-start(bf16[2560,384]{1,0:T(8,128)(2,1)} %collective-permute-done.1.refs_1_), channel_id=1, source_target_pairs={{0,16},{16,32},{32,48},{48,0},{64,112},{80,64},{96,80},{112,96},{1... | collective-permute-start | bytes 5898248 | tf_op jit(solution)/shard_map/ppermute | solution.py:846
  132.7 33.8 %all-to-all-start.1 = ((bf16[16,16,2560]{2,1,0:T(8,128)(2,1)}), bf16[16,16,2560]{2,1,0:T(8,128)(2,1)}, u32[]{:S(2)}, u32[]{:S(2)}) async-start(bf16[16,16,2560]{2,1,0:T(8,128)(2,1)} %broadcast_in_dim.140), calls=%async_computation.1 | async-start | bytes 2621440 | tf_op jit(solution)/shard_map/all_to_all | solution.py:92
  137.1 140.7 %all-gather.11.cloned.1.call-start = ((), (), s32[]{:S(2)}) async-start(), calls=%async_computation.15 | async-start | bytes 1392640 | tf_op jit(solution)/shard_map/all_gather | solution.py:989
  137.1 30.6 %collective-permute-start.9 = (bf16[2560,384]{1,0:T(8,128)(2,1)}, bf16[2560,384]{1,0:T(8,128)(2,1)}, u32[]{:S(2)}, u32[]{:S(2)}) collective-permute-start(bf16[2560,384]{1,0:T(8,128)(2,1)} %bitcast.22.refs_0_), channel_id=1, source_target_pairs={{0,64},{64,0},{1,65},{65,1},{2,66},{66,2},{3,67},{67,3},{4,68},{68... | collective-permute-start | bytes 5898248 | tf_op jit(solution)/shard_map/ppermute | solution.py:45
  137.2 30.5 %collective-permute-start.10 = (bf16[2560,384]{1,0:T(8,128)(2,1)}, bf16[2560,384]{1,0:T(8,128)(2,1)}, u32[]{:S(2)}, u32[]{:S(2)}) collective-permute-start(bf16[2560,384]{1,0:T(8,128)(2,1)} %collective-permute-done.1.refs_1_), channel_id=1, source_target_pairs={{0,64},{64,0},{1,65},{65,1},{2,66},{66,2},{3,67},{67,3},{4,68},{68... | collective-permute-start | bytes 5898248 | tf_op jit(solution)/shard_map/ppermute | solution.py:45
  137.7 30.0 %collective-permute-start.11 = (bf16[2560,384]{1,0:T(8,128)(2,1)}, bf16[2560,384]{1,0:T(8,128)(2,1)}, u32[]{:S(2)}, u32[]{:S(2)}) collective-permute-start(bf16[2560,384]{1,0:T(8,128)(2,1)} %collective-permute-done.2.refs_2_), channel_id=1, source_target_pairs={{0,64},{64,0},{1,65},{65,1},{2,66},{66,2},{3,67},{67,3},{4,68},{68... | collective-permute-start | bytes 5898248 | tf_op jit(solution)/shard_map/ppermute | solution.py:45
  324.6 25.5 %all-to-all-start.5 = ((bf16[16,16,2560]{2,1,0:T(8,128)(2,1)}), bf16[16,16,2560]{2,1,0:T(8,128)(2,1)}, u32[]{:S(2)}, u32[]{:S(2)}) async-start(bf16[16,16,2560]{2,1,0:T(8,128)(2,1)} %bitcast.194), calls=%async_computation.5 | async-start | bytes 2621440 | tf_op jit(solution)/shard_map/all_to_all | solution.py:96
  369.5 28.6 %all-to-all-start.6 = ((bf16[16,16,2560]{2,1,0:T(8,128)(2,1)}), bf16[16,16,2560]{2,1,0:T(8,128)(2,1)}, u32[]{:S(2)}, u32[]{:S(2)}) async-start(bf16[16,16,2560]{2,1,0:T(8,128)(2,1)} %broadcast_in_dim.142), calls=%async_computation.6 | async-start | bytes 2621440 | tf_op jit(solution)/shard_map/all_to_all | solution.py:92
  376.2 178.7 %reduce-scatter.4.cloned.1.call-start = ((), (), s32[]{:S(2)}) async-start(), calls=%async_computation.16 | async-start | bytes 6057984
  411.0 26.4 %all-to-all-start.7 = ((bf16[16,16,2560]{2,1,0:T(8,128)(2,1)}), bf16[16,16,2560]{2,1,0:T(8,128)(2,1)S(1)}, u32[]{:S(2)}, u32[]{:S(2)}) async-start(bf16[16,16,2560]{2,1,0:T(8,128)(2,1)} %bitcast.195), calls=%async_computation.7 | async-start | bytes 2621440 | tf_op jit(solution)/shard_map/all_to_all | solution.py:96
  438.3 32.8 %all-to-all-start.8 = ((bf16[16,80,384]{2,1,0:T(8,128)(2,1)}), bf16[16,80,384]{2,1,0:T(8,128)(2,1)}, u32[]{:S(2)}, u32[]{:S(2)}) async-start(bf16[16,80,384]{2,1,0:T(8,128)(2,1)} %add_convert_fusion.4), calls=%async_computation.8 | async-start | bytes 1966080 | tf_op jit(solution)/shard_map/all_to_all | solution.py:1030
  482.3 23.6 %collective-permute-start.63 = (bf16[16,80,384]{2,1,0:T(8,128)(2,1)}, bf16[16,80,384]{2,1,0:T(8,128)(2,1)}, u32[]{:S(2)}, u32[]{:S(2)}) collective-permute-start(bf16[16,80,384]{2,1,0:T(8,128)(2,1)} %get-tuple-element.218), channel_id=1, source_target_pairs={{0,64},{64,0},{1,65},{65,1},{2,66},{66,2},{3,67},{67,3},{4,68},{68... | collective-permute-start | bytes 2949128 | tf_op jit(solution)/shard_map/ppermute | solution.py:45
  484.4 24.2 %collective-permute-start.64 = (bf16[16,80,384]{2,1,0:T(8,128)(2,1)}, bf16[16,80,384]{2,1,0:T(8,128)(2,1)}, u32[]{:S(2)}, u32[]{:S(2)}) collective-permute-start(bf16[16,80,384]{2,1,0:T(8,128)(2,1)} %get-tuple-element.220), channel_id=1, source_target_pairs={{0,64},{64,0},{1,65},{65,1},{2,66},{66,2},{3,67},{67,3},{4,68},{68... | collective-permute-start | bytes 2949128 | tf_op jit(solution)/shard_map/ppermute | solution.py:45
  485.1 64.0 %all-to-all-start.9 = ((bf16[16,288,384]{2,1,0:T(8,128)(2,1)}), bf16[16,288,384]{2,1,0:T(8,128)(2,1)}, u32[]{:S(2)}, u32[]{:S(2)}) async-start(bf16[16,288,384]{2,1,0:T(8,128)(2,1)} %attend_gradients.3), calls=%async_computation.9 | async-start | bytes 7077888 | tf_op jit(solution)/shard_map/all_to_all | solution.py:930
  519.1 110.2 %collective-permute-start.77 = (bf16[16,80,384]{2,1,0:T(8,128)(2,1)}, bf16[16,80,384]{2,1,0:T(8,128)(2,1)}, u32[]{:S(2)}, u32[]{:S(2)}) collective-permute-start(bf16[16,80,384]{2,1,0:T(8,128)(2,1)} %all-to-all-done.8.two), channel_id=1, source_target_pairs={{0,64},{1,65},{2,66},{3,67},{4,68},{5,69},{6,70},{7,71},{8,72},{9,... | collective-permute-start | bytes 2949128 | tf_op jit(solution)/shard_map/ppermute | solution.py:1046
  520.6 31.3 %collective-permute-start.67 = (bf16[16,80,384]{2,1,0:T(8,128)(2,1)}, bf16[16,80,384]{2,1,0:T(8,128)(2,1)}, u32[]{:S(2)}, u32[]{:S(2)}) collective-permute-start(bf16[16,80,384]{2,1,0:T(8,128)(2,1)} %add_convert_fusion.2), channel_id=1, source_target_pairs={{0,16},{16,32},{32,48},{48,0},{64,112},{80,64},{96,80},{112,96},{1... | collective-permute-start | bytes 2949128 | tf_op jit(solution)/shard_map/ppermute | solution.py:846
  556.7 26.2 %collective-permute-start.52 = (bf16[16,2560]{1,0:T(8,128)(2,1)}, bf16[16,2560]{1,0:T(8,128)(2,1)}, u32[]{:S(2)}, u32[]{:S(2)}) collective-permute-start(bf16[16,2560]{1,0:T(8,128)(2,1)} %add_convert_fusion.8), channel_id=1, source_target_pairs={{0,48},{16,0},{32,16},{48,32},{1,49},{17,1},{33,17},{49,33},{2,50}... | collective-permute-start | bytes 245768 | tf_op jit(solution)/shard_map/ppermute | solution.py:49
  563.3 32.0 %all-to-all-start.10 = ((bf16[16,176,256]{2,1,0:T(8,128)(2,1)}), bf16[16,176,256]{2,1,0:T(8,128)(2,1)S(1)}, u32[]{:S(2)}, u32[]{:S(2)}) async-start(bf16[16,176,256]{2,1,0:T(8,128)(2,1)} %late.1), calls=%async_computation.10 | async-start | bytes 2883584 | tf_op jit(solution)/shard_map/all_to_all | solution.py:930
  576.8 49.6 %collective-permute-start.75 = (f32[288,384]{1,0:T(8,128)}, f32[288,384]{1,0:T(8,128)S(1)}, u32[]{:S(2)}, u32[]{:S(2)}) collective-permute-start(f32[288,384]{1,0:T(8,128)} %get-tuple-element.282), channel_id=1, source_target_pairs={{0,64},{64,0},{1,65},{65,1},{2,66},{66,2},{3,67},{67,3},{4,68},{68... | collective-permute-start | bytes 1327112 | tf_op jit(solution)/shard_map/ppermute | solution.py:45
  (169 other events, 1653.3 us)
Sparse Core Ops, SparseCore 0:
  18.6 84.0 all-gather.6
  105.4 75.5 all-gather.8
  232.6 44.6 all-gather.10
  398.3 97.6 reduce-scatter.3

commit v3 on v2

--- a/solution.py
+++ b/solution.py
@@ -308,6 +308,7 @@
 
 def ffn_unpack_kernel(core_ref, one, one_got, two, two_got, gate_ref, up_ref, down_ref, wide_ref):
     first = core_ref[0] == 0
+    rows = slice(0, HALF_ROWS)
     wide_ref[...] = jnp.zeros(wide_ref.shape, F32)
     valid = lax.broadcasted_iota(jnp.int32, (HALF_ROWS, LANES), 1) < FF_PART
     for p in range(N_DP):
@@ -315,8 +316,8 @@
         by = FF_PART * p - at
         for m in range(3):
             columns = slice(LANES * m, LANES * (m + 1))
-            low = jnp.where(first, one[p, :, columns].astype(F32), two_got[p, :, columns].astype(F32))
-            high = jnp.where(first, one_got[p, :, columns].astype(F32), two[p, :, columns].astype(F32))
+            low = jnp.where(first, one[p, rows, columns].astype(F32), two_got[p, :, columns].astype(F32))
+            high = jnp.where(first, one_got[p, rows, columns].astype(F32), two[p, :, columns].astype(F32))
             for half, block in enumerate((low, high)):
                 block = jnp.where(valid, block, 0.0)
                 window = jnp.concatenate([block, jnp.zeros_like(block)], axis=1)
@@ -558,8 +559,8 @@
 
 def attend_gradients_kernel(
     mine_ref, other_ref, dq_ref, dkv_ref, sq_hbm, comp_hbm, mixed_hbm,
-    early_ref,
-    sq_ref, comp_ref, mixed_ref, sems,
+    out_ref,
+    early_ref, sq_ref, comp_ref, mixed_ref, sems,
 ):
     pairs = ((mixed_hbm, mixed_ref), (sq_hbm, sq_ref), (comp_hbm, comp_ref))
     copies = [pltpu.make_async_copy(a, b, sems.at[i]) for i, (a, b) in enumerate(pairs)]
@@ -577,79 +578,154 @@
     early_ref[:, KVB_ROWS, :] = kvb_grad[:, :, :WO]
     more = slice(A_ROWS, A_ROWS + QR // N_DP)
     early_ref[:, more, : LAT - WO] = qb_grad[:, :, WO:]
-    early_ref[:, more.stop : E_ROWS, : LAT - WO] = kvb_grad[:, :, WO:]
-    early_ref[:, A_ROWS:E_ROWS, LAT - WO :] = jnp.zeros((N_DP, E_ROWS - A_ROWS, 2 * WO - LAT), BF16)
-    if early_ref.shape[1] > E_ROWS:
-        rest = early_ref.shape[1] - E_ROWS
-        early_ref[:, E_ROWS:, 2 * HEAD :] = jnp.zeros((N_DP, rest, WO - 2 * HEAD), BF16)
-        early_ref[:, E_ROWS:, : 2 * HEAD] = jnp.zeros((N_DP, rest, 2 * HEAD), BF16)
-
-
-def attend_gradients(d_attended, saved, d_query, d_key_value, rows):
+    early_ref[:, more.stop :, : LAT - WO] = kvb_grad[:, :, WO:]
+    early_ref[:, A_ROWS:, LAT - WO :] = jnp.zeros((N_DP, E_ROWS - A_ROWS, 2 * WO - LAT), BF16)
+    copy = pltpu.make_async_copy(early_ref, out_ref.at[:, :E_ROWS], sems.at[3])
+    copy.start()
+    copy.wait()
+
+
+def attend_gradients(d_attended, saved, d_query, d_key_value):
     vmem = pl.BlockSpec(memory_space=pltpu.VMEM)
+    hbm = pl.BlockSpec(memory_space=pl.ANY)
     return pl.pallas_call(
         attend_gradients_kernel,
-        out_shape=jax.ShapeDtypeStruct((N_DP, rows, WO), BF16),
-        in_specs=[vmem] * 4 + [pl.BlockSpec(memory_space=pl.ANY)] * 3,
+        out_shape=jax.ShapeDtypeStruct((N_DP, E_ROWS + L_ROWS, WO), BF16),
+        in_specs=[vmem] * 4 + [hbm] * 3,
+        out_specs=hbm,
+        scratch_shapes=[
+            pltpu.VMEM((N_DP, E_ROWS, WO), BF16),
+            pltpu.VMEM((ROWS, QR), BF16),
+            pltpu.VMEM((ROWS, KVR), BF16),
+            pltpu.VMEM((ROWS, WO), BF16),
+            pltpu.SemaphoreType.DMA((4,)),
+        ],
+        compiler_params=pltpu.CompilerParams(vmem_limit_bytes=ATT_VMEM),
+        name="attend_gradients",
+    )(*d_attended, d_query, d_key_value, saved[0], saved[1], saved[5])
+
+
+def low_gradients_kernel(
+    dq_ref, dkv_ref, columns_ref, sq_hbm, comp_hbm, out_ref, sq_ref, comp_ref, sems
+):
+    copies = [
+        pltpu.make_async_copy(sq_hbm, sq_ref, sems.at[0]),
+        pltpu.make_async_copy(comp_hbm, comp_ref, sems.at[1]),
+    ]
+    for copy in copies:
+        copy.start()
+    copies[0].wait()
+    grad = dot_tn(sq_ref[...], dq_ref[...]).astype(BF16)
+    out_ref[:, : QR // N_DP, :] = grad.reshape(N_DP, QR // N_DP, LAT)
+    copies[1].wait()
+    grad = dot_tn(comp_ref[...], dkv_ref[...]).astype(BF16)
+    out_ref[:, QR // N_DP : LOW_ROWS, :] = grad.reshape(N_DP, KVR // N_DP, LAT)
+    out_ref[:, LOW_ROWS:, :SLICE] = columns_ref[...]
+    out_ref[:, LOW_ROWS:, SLICE:] = jnp.zeros((N_DP, SHARD, LAT - SLICE), BF16)
+
+
+LOW_ROWS = A_ROWS - SLICE
+
+
+def low_gradients(saved, d_query, d_key_value, columns):
+    vmem = pl.BlockSpec(memory_space=pltpu.VMEM)
+    hbm = pl.BlockSpec(memory_space=pl.ANY)
+    return pl.pallas_call(
+        low_gradients_kernel,
+        out_shape=jax.ShapeDtypeStruct((N_DP, LOW_ROWS + SHARD, LAT), BF16),
+        in_specs=[vmem, vmem, vmem, hbm, hbm],
         out_specs=vmem,
         scratch_shapes=[
             pltpu.VMEM((ROWS, QR), BF16),
             pltpu.VMEM((ROWS, KVR), BF16),
-            pltpu.VMEM((ROWS, WO), BF16),
-            pltpu.SemaphoreType.DMA((3,)),
+            pltpu.SemaphoreType.DMA((2,)),
         ],
         compiler_params=pltpu.CompilerParams(vmem_limit_bytes=ATT_VMEM),
-        name="attend_gradients",
-    )(*d_attended, d_query, d_key_value, saved[0], saved[1], saved[5])
+        name="low_gradients",
+    )(d_query, d_key_value, columns, saved[0], saved[1])
+
+
+def wo_gradient_kernel(mine_ref, other_ref, mixed_hbm, out_ref, mixed_ref, sem):
+    copy = pltpu.make_async_copy(mixed_hbm, mixed_ref, sem)
+    copy.start()
+    copy.wait()
+    total = None
+    for i in range(2 * N_Z):
+        d_ref = mine_ref if i < N_Z else other_ref
+        d_att = d_ref[TOKENS * (i % N_Z) : TOKENS * (i % N_Z + 1)]
+        mixed = mixed_ref[:, SHARD * i : SHARD * (i + 1), :].reshape(TOKENS, WO)
+        term = dot_tn(d_att, mixed)
+        total = term if total is None else total + term
+    out_ref[...] = total
+
+
+def wo_gradient(d_attended, mixed):
+    vmem = pl.BlockSpec(memory_space=pltpu.VMEM)
+    return pl.pallas_call(
+        wo_gradient_kernel,
+        out_shape=jax.ShapeDtypeStruct((SLICE, WO), F32),
+        in_specs=[vmem, vmem, pl.BlockSpec(memory_space=pl.ANY)],
+        out_specs=vmem,
+        scratch_shapes=[pltpu.VMEM((N_DP, ROWS, WO), BF16), pltpu.SemaphoreType.DMA],
+        compiler_params=pltpu.CompilerParams(vmem_limit_bytes=ATT_VMEM),
+        name="wo_gradient",
+    )(*d_attended, mixed)
+
+
+LAT_ALL = QR + KVR + HEAD
+
+
+def latent_gradient_kernel(rows_ref, normed_ref, out_ref):
+    rows = rows_ref[...].reshape(TOKENS, LAT_ALL)
+    out_ref[...] = dot_tn(normed_ref[...].reshape(TOKENS, SLICE), rows).astype(BF16)
+
+
+def latent_gradient(rows, normed):
+    return pl.pallas_call(
+        latent_gradient_kernel,
+        out_shape=jax.ShapeDtypeStruct((SLICE, LAT_ALL), BF16),
+        compiler_params=pltpu.CompilerParams(vmem_limit_bytes=ATT_VMEM),
+        name="latent_gradient",
+    )(rows, normed)
 
 
 L_ROWS = SLICE + 16
 
 
-def late_kernel(rows_ref, gains_ref, normed_hbm, *refs):
-    packs = len(refs) == 6
-    out_ref, late_ref, normed_ref, sem, out_sem = refs[1:] if packs else (refs[0], refs[0], *refs[1:], None)
+def late_kernel(rows_ref, gains_ref, normed_hbm, packs_ref, out_ref, late_ref, normed_ref, sem, out_sem):
     copy = pltpu.make_async_copy(normed_hbm, normed_ref, sem)
     copy.start()
     late_ref[:, SLICE:, :HEAD] = gains_ref[...]
-    late_ref[:, SLICE:, HEAD:] = jnp.zeros(gains_ref.shape, BF16)
+    late_ref[:, SLICE:, HEAD : 2 * HEAD] = jnp.zeros(gains_ref.shape, BF16)
+    late_ref[:, :, 2 * HEAD :] = jnp.zeros((N_DP, L_ROWS, WO - 2 * HEAD), BF16)
     copy.wait()
     grad = dot_tn(normed_ref[...], rows_ref[...]).astype(BF16)
-    late_ref[:, :SLICE, :] = grad.reshape(N_DP, SLICE, 2 * HEAD)
-    if packs:
-        copy = pltpu.make_async_copy(late_ref, out_ref.at[:, E_ROWS:, : 2 * HEAD], out_sem)
-        copy.start()
-        copy.wait()
-
-
-def late_pack(normed, rows, gains, packs=None):
+    late_ref[:, :SLICE, : 2 * HEAD] = grad.reshape(N_DP, SLICE, 2 * HEAD)
+    copy = pltpu.make_async_copy(late_ref, out_ref.at[:, E_ROWS:], out_sem)
+    copy.start()
+    copy.wait()
+
+
+def late_pack(normed, rows, gains, packs):
     attn, q, kv, ffn = (g.reshape(N_DP, -1) for g in gains)
     wide = ((0, 0), (0, 2 * HEAD - SLICE))
     row = jnp.concatenate([jnp.pad(attn, wide), jnp.pad(ffn, wide), q, kv], axis=1)
     row = jnp.pad(row, ((0, 0), (0, 16 * HEAD - row.shape[1]))).reshape(N_DP, 16, HEAD).astype(BF16)
     vmem = pl.BlockSpec(memory_space=pltpu.VMEM)
     hbm = pl.BlockSpec(memory_space=pl.ANY)
-    shape = (N_DP, L_ROWS, 2 * HEAD)
-    scratch = [pltpu.VMEM((ROWS, D), BF16), pltpu.SemaphoreType.DMA]
-    params = pltpu.CompilerParams(vmem_limit_bytes=ATT_VMEM)
-    if packs is None:
-        return pl.pallas_call(
-            late_kernel,
-            out_shape=jax.ShapeDtypeStruct(shape, BF16),
-            in_specs=[vmem, vmem, hbm],
-            out_specs=vmem,
-            scratch_shapes=scratch,
-            compiler_params=params,
-            name="late",
-        )(rows, row, normed)
     return pl.pallas_call(
         late_kernel,
         out_shape=jax.ShapeDtypeStruct(packs.shape, BF16),
         in_specs=[vmem, vmem, hbm, hbm],
         out_specs=hbm,
-        scratch_shapes=[pltpu.VMEM(shape, BF16)] + scratch + [pltpu.SemaphoreType.DMA],
+        scratch_shapes=[
+            pltpu.VMEM((N_DP, L_ROWS, WO), BF16),
+            pltpu.VMEM((ROWS, D), BF16),
+            pltpu.SemaphoreType.DMA,
+            pltpu.SemaphoreType.DMA,
+        ],
         input_output_aliases={3: 0},
-        compiler_params=params,
+        compiler_params=pltpu.CompilerParams(vmem_limit_bytes=ATT_VMEM),
         name="late_in_packs",
     )(rows, row, normed, packs)
 
@@ -675,48 +751,55 @@
 
 
 def home_kernel(
-    core_ref, tiles_ref, tiles_got_ref, rope_ref, rope_got_ref, early_ref, early_got_ref,
+    core_ref, lat_ref, wo1_ref, wo1_got_ref, low_ref, low_got_ref,
+    tiles_ref, tiles_got_ref, packs_ref, packs_got_ref,
     qa_ref, kva_ref, qb_ref, kvb_ref, wo_ref, gain_ref, heads_ref,
 ):
     first = core_ref[0] == 0
 
-    def halves(keep, got):
-        keep, got = keep.astype(F32), got.astype(F32)
-        return jnp.where(first, keep, got), jnp.where(first, got, keep)
+    def pick(one, two):
+        return jnp.where(first, one.astype(F32), two.astype(F32))
 
     wide = slice(0, SLICE)
     gains = jnp.zeros(gain_ref.shape, F32)
     for z in range(N_Z):
-        low, high = halves(tiles_ref[z], tiles_got_ref[z])
-        gains = gains + low[SLICE:] + high[SLICE:]
-        qa_ref[:, HEAD * z : HEAD * (z + 1)] = low[wide]
+        low, high = tiles_got_ref[z], tiles_ref[z]
+        gains = gains + low[SLICE:].astype(F32) + high[SLICE:].astype(F32)
+        columns = slice(HEAD * z, HEAD * (z + 1))
+        qa_ref[:, columns] = pick(lat_ref[wide, columns], low[wide])
+        columns = slice(HEAD * (z + 4), HEAD * (z + 5))
+        both = pick(lat_ref[wide, columns], high[wide])
         if z < 2:
-            qa_ref[:, HEAD * (z + 4) : HEAD * (z + 5)] = high[wide]
+            qa_ref[:, columns] = both
         else:
-            kva_ref[:, HEAD * (z - 2) : HEAD * (z - 1)] = high[wide]
+            kva_ref[:, HEAD * (z - 2) : HEAD * (z - 1)] = both
     gain_ref[...] = gains
-    _, high = halves(rope_ref[...], rope_got_ref[...])
-    kva_ref[:, KVR:] = high[:, :ROPE]
-    low, high = halves(early_ref[wide], early_got_ref[wide])
+    rope = pick(lat_ref[wide, QR + KVR :], packs_ref[E_ROWS : E_ROWS + SLICE, HEAD : 2 * HEAD])
+    kva_ref[:, KVR:] = rope[:, :ROPE]
     at = WO - HEADS * VD
+    low, high = pick(wo1_ref[...], packs_got_ref[wide]), pick(wo1_got_ref[...], packs_ref[wide])
     wo_ref[...] = jnp.concatenate([low[:, at:], high[:, at:]], axis=1)
     heads_ref[...] = jnp.zeros(heads_ref.shape, F32)
+    qb_rows, kvb_rows = slice(0, QR // N_DP), slice(QR // N_DP, A_ROWS - SLICE)
     valid = lax.broadcasted_iota(jnp.int32, (QR // N_DP, HEAD), 1) < NOPE + ROPE
-    more = A_ROWS - SLICE
     for j in range(HEADS):
-        rows = QB_ROWS if j < 3 else slice(QB_ROWS.start + more, QB_ROWS.stop + more)
-        columns = slice(HEAD * (j % 3), HEAD * (j % 3 + 1))
-        for k, tile in enumerate(halves(early_ref[rows, columns], early_got_ref[rows, columns])):
-            start = (NOPE + ROPE) * (HEADS * k + j)
-            at = start // HEAD * HEAD
-            tile = jnp.where(valid, tile, 0.0)
-            window = jnp.concatenate([tile, jnp.zeros_like(tile)], axis=1)
-            if start > at:
-                window = pltpu.roll(window, start - at, 1)
-            heads_ref[:, at : at + 2 * HEAD] += window
-        rows = KVB_ROWS if j < 3 else slice(KVB_ROWS.start + more, KVB_ROWS.stop + more)
-        for k, tile in enumerate(halves(early_ref[rows, columns], early_got_ref[rows, columns])):
-            kvb_ref[:, HEAD * (HEADS * k + j) : HEAD * (HEADS * k + j + 1)] = tile
+        start = SLICE if j < 3 else A_ROWS
+        columns, packed = slice(HEAD * j, HEAD * (j + 1)), slice(HEAD * (j % 3), HEAD * (j % 3 + 1))
+        for rows in (qb_rows, kvb_rows):
+            at_rows = slice(start + rows.start, start + rows.stop)
+            low = pick(low_ref[rows, columns], packs_got_ref[at_rows, packed])
+            high = pick(low_got_ref[rows, columns], packs_ref[at_rows, packed])
+            for k, tile in enumerate((low, high)):
+                if rows == kvb_rows:
+                    kvb_ref[:, HEAD * (HEADS * k + j) : HEAD * (HEADS * k + j + 1)] = tile
+                    continue
+                begin = (NOPE + ROPE) * (HEADS * k + j)
+                at = begin // HEAD * HEAD
+                tile = jnp.where(valid, tile, 0.0)
+                window = jnp.concatenate([tile, jnp.zeros_like(tile)], axis=1)
+                if begin > at:
+                    window = pltpu.roll(window, begin - at, 1)
+                heads_ref[:, at : at + 2 * HEAD] += window
     qb_ref[...] = heads_ref[:, : 2 * HEADS * (NOPE + ROPE)]
 
 
@@ -868,15 +951,13 @@
 tie = lax.optimization_barrier
 
 
-def attention_forward(rows, x_own, pack, gains, tab, other=()):
+def attention_forward(normed, latent, x_own, pack, gains, tab):
     core = lax.axis_index("section").reshape(1)
-    normed, latent = latents(rows, gains["attn"], pack)
-    latent, other = tie((latent, other))
     part, *saved, latent_own = attend(
         core, latent, to_core(latent), tab, gains["q"], gains["kv"], pack
     )
     middle = x_own + RES_SCALE * scatter_tokens(part)
-    return middle, (normed, latent_own, saved), other
+    return middle, (normed, latent_own, saved)
 
 
 def layer_forward(own, x_own, middle, saved, gains, ffn_weights, far=None):
@@ -923,7 +1004,7 @@
 
     rows = jnp.stack([piece(0), z_hop(piece(3), -1), z_hop(piece(2), 2), z_hop(piece(1), 1)])
     rows = rows.reshape(N_Z, 2, SHARD, 2 * HEAD).transpose(1, 0, 2, 3).reshape(ROWS, 2 * HEAD)
-    return d_block, rows, (attn_gain, q_gain, kv_gain), also
+    return d_block, rows, jnp.concatenate([d_q, d_c, d_rope, blank[:, ROPE:]], axis=1), (attn_gain, q_gain, kv_gain), also
 
 
 def scatter_sum(x):
@@ -948,14 +1029,15 @@
     w_down,
 ):
     core = lax.axis_index("section")
+    blocks = ffn_pack(w_gate[0], w_up[0], w_down[0].T)
+    blocks, w_qa = tie((blocks, w_qa))
     keep, give = attention_packs(
         core.reshape(1), w_qa[0], w_qb[0], w_kva[0], w_kvb[0], w_o[0].T, g_attn, g_ffn, g_q, g_kv
     )
     attn_one, attn_two = by_core(core, keep, to_core(give))
     attn_one = lax.all_gather(attn_one, "dp")
-    attn_two = lax.all_gather(attn_two, "dp")
-
-    blocks = lax.all_to_all(ffn_pack(w_gate[0], w_up[0], w_down[0].T), "dp", 0, 0)
+
+    blocks = lax.all_to_all(blocks, "dp", 0, 0)
     tab = head_tables(seq_lengths)
     blocks, cotangent, layer_input = lax.optimization_barrier((blocks, cotangent, layer_input))
     weights = blocks.reshape(D, MATS)
@@ -973,39 +1055,52 @@
         return gather_tokens((RES_SCALE * d_middle).astype(BF16))
 
     cot_own = token_rows(cotangent)[0][:SHARD].astype(F32)
-    attn_one, tab = tie((attn_one, tab))
-    gains_one, gains_two = attention_gains(attn_one), attention_gains(attn_two)
+    attn_one, tab, near, after = tie((attn_one, tab, near, after))
+    gains_one = attention_gains(attn_one)
     own_one = jnp.stack([(core == 0).astype(jnp.int32), core])
     own_two = jnp.stack([(core == 1).astype(jnp.int32), core])
 
     rows = token_rows(layer_input)
     x_own = rows[0][:SHARD].astype(F32)
-    middle, saved, (near, after) = attention_forward(
-        rows, x_own, attn_one, gains_one, tab, (near, after)
-    )
+    normed, latent = latents(rows, gains_one["attn"], attn_one)
+    wide = (A_COLS, A_COLS, D - 2 * A_COLS)
+    shared = jnp.concatenate([(RES_SCALE * cot_own).astype(BF16), normed[:SHARD]], axis=0)
+    shared = [shared[:, :A_COLS], shared[:, A_COLS : 2 * A_COLS], shared[:, 2 * A_COLS :]]
+    shared[2] = jnp.pad(shared[2], ((0, 0), (0, A_COLS - wide[2])))
+    attn_two = lax.all_gather(jnp.concatenate([attn_two] + shared, axis=0), "dp")
+    shared = [
+        attn_two[:, A_ROWS + 2 * SHARD * i : A_ROWS + 2 * SHARD * (i + 1), : wide[i]] for i in range(3)
+    ]
+    shared = jnp.concatenate(shared, axis=2)
+    d_rows_two = shared[:, :SHARD].reshape(TOKENS, D)
+    normed_one = lax.dynamic_slice_in_dim(shared[:, SHARD:], lax.axis_index("dp") * SLICE, SLICE, 2)
+    gains_two = attention_gains(attn_two)
+    middle, saved = attention_forward(normed, latent, x_own, attn_one, gains_one, tab)
     mine = [weights, near, after]
     ffn_weights = mine + [to_core(piece) for piece in mine]
-    middle, near, cot_rows = tie((middle, near, (RES_SCALE * cot_own).astype(BF16)))
-    d_rows_two = lax.all_gather(cot_rows, "dp").reshape(TOKENS, D)
     part, saved_one, ffn_weights = layer_forward(
         own_one, x_own, middle, saved, gains_one, ffn_weights, ring_hop(near, 1)
     )
     out_one = layer_out_rows(scatter_dp(part), saved_one)
     rows_one = gather_tokens(out_one)
     x_own = out_one.astype(F32)
-    middle, saved, _ = attention_forward(rows_one, x_own, attn_two, gains_two, tab)
+    normed, latent = latents(rows_one, gains_two["attn"], attn_two)
+    middle, saved = attention_forward(normed, latent, x_own, attn_two, gains_two, tab)
     part_two, saved_two, _ = layer_forward(own_two, x_own, middle, saved, gains_two, ffn_weights)
+
+    mixed_one = lax.all_gather(saved_one[-1][5], "dp")
 
     ffn_rows, gu, hidden = saved_two[2:5]
     part, d_gu = ffn_backward(own_two, d_rows_two, gu, ffn_weights)
     grads_two = ffn_gradients(own_two, d_rows_two, ffn_rows, d_gu, hidden)
     d_normed_two = scatter_dp(part)
+    d_normed_two, mixed_one = tie((d_normed_two, mixed_one))
     ring_two = ring_pairs(grads_two)
     d_middle, ffn_gain_two = middle_backward(cot_own, d_normed_two, saved_two, gains_two)
     d_attended = d_attended_rows(d_middle)
     part, d_query, d_key_value = attend_back(d_attended, tab, saved_two[-1], attn_two)
-    packs_two = attend_gradients(d_attended, saved_two[-1], d_query, d_key_value, E_ROWS + L_ROWS)
-    in_grad_two, rows, dg_two, part_two = attention_backward(
+    packs_two = attend_gradients(d_attended, saved_two[-1], d_query, d_key_value)
+    in_grad_two, rows, _, dg_two, part_two = attention_backward(
         part, d_middle, saved_two, attn_two, gains_two, scatter_dp(part_two)
     )
     packs_two = late_pack(saved_two[5], rows, (*dg_two, ffn_gain_two), packs_two).reshape(-1, WO)
@@ -1020,51 +1115,68 @@
     grads_one = ffn_gradients(own_one, d_rows, ffn_rows, d_gu, hidden)
     d_normed_two = scatter_dp(part)
     total_two = ring_last(ring_two)
-    d_normed_two, total_two = tie((d_normed_two, total_two))
+    rows_two = gather_tokens(layer_out_rows(part_two, saved_two))
+    d_normed_two, total_two, rows_two = tie((d_normed_two, total_two, rows_two))
     d_middle, ffn_gain_one = middle_backward(grad_one, d_normed_two, saved_one, gains_one)
-    d_attended = d_attended_rows(d_middle)
+    d_att_own = (RES_SCALE * d_middle).astype(BF16)
+    columns = d_att_own.reshape(SHARD, N_DP, SLICE).transpose(1, 0, 2)
+    home_two = lax.all_to_all(total_two, "dp", 0, 0)
+    d_attended, grads_one, columns, home_two = tie(
+        (gather_tokens(d_att_own), grads_one, columns, home_two)
+    )
     part, d_query, d_key_value = attend_back(d_attended, tab, saved_one[-1], attn_one)
-    early_one = attend_gradients(d_attended, saved_one[-1], d_query, d_key_value, E_ROWS)
-    part, early_one = tie((part, early_one))
-    early_one = scatter_sum(early_one)
-    home_two = lax.all_to_all(total_two, "dp", 0, 0)
-    part, home_two = tie((part, home_two))
-    in_grad_one, rows, dg_one, grads_one = attention_backward(
-        part, d_middle, saved_one, attn_one, gains_one, grads_one
-    )
-    rows, pairs = tie((rows, ring_pairs(grads_one)))
-    total_one = ring_last(ring_first(pairs))
-    in_grad_one, dg_one, early_one, part_two, packs_two = tie(
-        (in_grad_one, dg_one, early_one, part_two, packs_two)
-    )
-    rows_two = gather_tokens(layer_out_rows(part_two, saved_two))
-    late_one = scatter_sum(late_pack(saved_one[5], rows, (*dg_one, ffn_gain_one)))
-
-    total_one, late_one = tie((total_one, late_one))
-    home_one = lax.all_to_all(total_one, "dp", 0, 0)
+    low_one = low_gradients(saved_one[-1], d_query, d_key_value, columns)
+    part, low_one = tie((part, low_one))
+    low_one = lax.all_to_all(low_one, "dp", 0, 0)
+    in_grad_one, _, d_lat_own, dg_one, pairs = attention_backward(
+        part, d_middle, saved_one, attn_one, gains_one, ring_pairs(grads_one)
+    )
+    d_lat = jnp.broadcast_to(d_lat_own.astype(BF16)[None], (N_DP, SHARD, LAT_ALL))
+    d_lat, low_one, first = tie((d_lat, low_one, ring_first(pairs)))
+    columns = gather_tokens(low_one[:, LOW_ROWS:, :SLICE].reshape(TOKENS, SLICE))
+    wo_one = wo_gradient(columns, mixed_one)
+    low_one = jnp.sum(low_one[:, :LOW_ROWS].astype(F32), axis=0)
+    d_lat = lax.all_to_all(d_lat, "dp", 0, 0)
+    lat_one = latent_gradient(d_lat, normed_one)
+    total_one, lat_one, in_grad_one = tie((ring_last(first), lat_one, in_grad_one))
+
+    total_one = total_one.reshape(N_DP, HALF_ROWS, MATS)
+    attn, q, kv = dg_one
+    dg_one = jnp.concatenate([attn, ffn_gain_one, q, kv]).astype(BF16).reshape(-1, HEAD)
+    dg_one = add(dg_one, to_core(dg_one))
+    dg_one = sum(x.astype(F32) for x in gather_z(dg_one)).reshape(-1)
+    row = [dg_one[:D], dg_one[D : 2 * D], dg_one[2 * D : 2 * D + QR], dg_one[2 * D + QR :]]
+    row = jnp.concatenate([x.reshape(N_DP, -1) for x in row], axis=1).astype(BF16)
+    row = jnp.pad(row[:, None], ((0, 0), (0, 15), (0, 0)))
+    home_one = lax.all_to_all(jnp.concatenate([total_one, row], axis=1), "dp", 0, 0)
+    dg_one = jnp.sum(home_one[:, HALF_ROWS].astype(F32), axis=0)
     got_one = lax.ppermute(home_one, "section", [(1, 0)])
     got_two = lax.ppermute(home_two, "section", [(0, 1)])
     gate_grad, up_grad, down_grad = ffn_unpack(core.reshape(1), home_one, got_one, home_two, got_two)
 
-    packs_two = packs_two.astype(F32)
-    early_two, late_two = packs_two[:E_ROWS], packs_two[E_ROWS:, : 2 * HEAD]
-
-    def homeward(one, two):
-        give = jnp.where(core == 0, two, one)
-        return jnp.where(core == 0, one, two), to_core(give)
-
-    tiles = jnp.concatenate([late_one[:, :HEAD], late_two[:, :HEAD]], axis=0).astype(BF16)
-    tiles = from_zero(jnp.stack(gather_z(tiles))).reshape(N_Z, 2, SLICE + 16, HEAD)
+    def from_other(x, layer):
+        return lax.ppermute(x, "section", [(1 - layer, layer)])
+
+    lat_one = add(lat_one, from_other(lat_one, 0))
+    lat_one = sum(x.astype(F32) for x in gather_z(lat_one))
+    packs_two, lat_one = tie((packs_two, lat_one))
+    tiles = from_zero(jnp.stack(gather_z(packs_two[E_ROWS:, :HEAD])))
     qa_grad, kva_grad, qb_grad, kvb_grad, wo_grad, gains = home(
         core.reshape(1),
-        *homeward(tiles[:, 0], tiles[:, 1]),
-        *homeward(late_one[:SLICE, HEAD:], late_two[:SLICE, HEAD:]),
-        *homeward(early_one, early_two),
+        lat_one,
+        wo_one,
+        from_other(wo_one, 0),
+        low_one,
+        from_other(low_one, 0),
+        tiles,
+        from_other(tiles, 1),
+        packs_two,
+        from_other(packs_two, 1),
     )
     gains = gains.reshape(-1)
 
-    def gain_part(at, width):
-        return gains[at : at + width][None]
+    def gain_part(one, two, width):
+        return jnp.where(core == 0, dg_one[one : one + width], gains[two : two + width])[None]
 
     layer_out = in_order(*(jnp.where(core == 0, one, two) for one, two in zip(rows_one, rows_two)))[None]
     give = jnp.where(core == 0, in_grad_two, in_grad_one)
@@ -1075,15 +1187,15 @@
     return (
         layer_out,
         input_grad,
-        gain_part(0, SLICE),
+        gain_part(0, 0, SLICE),
         qa_grad[None],
-        gain_part(4 * HEAD, QR // N_DP),
+        gain_part(2 * SLICE, 4 * HEAD, QR // N_DP),
         qb_grad[None],
         kva_grad[None],
-        gain_part(4 * HEAD + QR // N_DP, KVR // N_DP),
+        gain_part(2 * SLICE + QR // N_DP, 4 * HEAD + QR // N_DP, KVR // N_DP),
         kvb_grad[None],
         wo_grad.T[None],
-        gain_part(2 * HEAD, SLICE),
+        gain_part(SLICE, 2 * HEAD, SLICE),
         gate_grad[None],
         up_grad[None],
         down_grad.T[None],

time: 653 us -> 622 us (0.953)
  waiting for transfers between devices: 226 us -> 162 us
  starting transfers between devices: 169 us -> 197 us
  other arithmetic: 63.9 us -> 71 us
    all_gather x1, waiting for transfers between devices: 34.2 us -> 0.01 us  [body(): attn_one = lax.all_gather(attn_one, 'dp')]
    all_to_all x4, waiting for transfers between devices: 64.5 us -> 33.9 us  [the longest x1 31.1 us: body(): blocks = lax.all_to_all(blocks, 'dp', 0, 0)]
    ppermute x9, waiting for transfers between devices: 13.8 us -> 42.5 us  [ring_hop(): return lax.ppermute(x, ('section', 'tensor'), pairs)]
    ppermute x0 -> x5, starting transfers between devices: none -> 17.8 us  [from_other(): return lax.ppermute(x, 'section', [(1 - layer, layer)])]
    ppermute x36 -> x42, starting transfers between devices: 46 us -> 62.4 us  [z_hop(): return lax.ppermute(x, 'tensor', [(i, (i + by) % N_Z) for i in range(N_Z)])]
    all_to_all x3, waiting for transfers between devices: 24.6 us -> 12 us  [scatter_dp(): pieces = lax.all_to_all(part.reshape(N_DP, SHARD, D), 'dp', 0, 0)]
    all_to_all x3, waiting for transfers between devices: 46.6 us -> 34.7 us  [gather_dp(): lax.all_to_all(copies, 'dp', 0, 0).reshape(N_DP * x.shape[0], x.shape[1])]
    unnamed x221 -> x179, local copies, waits for them, and re-layouts: 21 us -> 10.5 us
  transfers between devices with their start and end apart: 93 -> 103, of which waited for: 41 -> 35; matrix products, arithmetic and copies ran while one was open for 12% -> 15% of each run, Pallas kernels for 13% -> 14%
where the time goes in v3:
time: 622 us; the launch traced here: 612 us
  starting transfers between devices  197 us (32%)
  waiting for transfers between devices  162 us (26%)
  Pallas kernels  97.8 us (16%)
  other arithmetic  71 us (11%)
  local copies, waits for them, and re-layouts  39.1 us (6%)
  blocking collectives  29 us (5%)
  between operations  16.3 us (3%)
    ppermute x42, starting transfers between devices, z_hop(): return lax.ppermute(x, 'tensor', [(i, (i + by) % N_Z) for i in range(N_Z)])  62.4 us
    ppermute x30, starting transfers between devices, to_core(): return lax.ppermute(x, 'section', [(0, 1), (1, 0)])  48.7 us
    ppermute x9, waiting for transfers between devices, ring_hop(): return lax.ppermute(x, ('section', 'tensor'), pairs)  42.5 us
    all_to_all x3, waiting for transfers between devices, gather_dp(): lax.all_to_all(copies, 'dp', 0, 0).reshape(N_DP * x.shape[0], x.shape[1])  34.7 us
    all_to_all x1, waiting for transfers between devices, body(): blocks = lax.all_to_all(blocks, 'dp', 0, 0)  31.1 us
    all_to_all x1, blocking collectives, scatter_dp(): pieces = lax.all_to_all(part.reshape(N_DP, SHARD, D), 'dp', 0, 0)  29 us
    ppermute x42, waiting for transfers between devices, z_hop(): return lax.ppermute(x, 'tensor', [(i, (i + by) % N_Z) for i in range(N_Z)])  28.3 us
    convert_element_type x10, other arithmetic, add(): return sum((x.astype(F32) for x in terms)).astype(BF16)  21.9 us
  transfers between devices with their start and end apart: 103, of which 35 were waited for; matrix products, arithmetic and copies ran while one was open for 15% of the time, Pallas kernels for 14%

profile of v3, /device:TPU:1, one launch (start us, length us, event | category | flops | bytes accessed | tf_op | source)
XLA Modules:
  0.0 611.9 jit_solution(751332888053321694)
XLA Ops:
  15.5 6.8 %all-to-all-start = ((bf16[16,160,384]{2,1,0:T(8,128)(2,1)}), bf16[16,160,384]{2,1,0:T(8,128)(2,1)S(1)}, u32[]{:S(2)}, u32[]{:S(2)}) async-start(bf16[16,160,384]{2,1,0:T(8,128)(2,1)} %ffn_pack.1), calls=%async_computation | async-start | bytes 3932160 | tf_op jit(solution)/shard_map/all_to_all | solution.py:1040
  23.6 31.1 %all-to-all-done = bf16[16,160,384]{2,1,0:T(8,128)(2,1)S(1)} async-done(((bf16[16,160,384]{2,1,0:T(8,128)(2,1)}), bf16[16,160,384]{2,1,0:T(8,128)(2,1)S(1)}, u32[]{:S(2)}, u32[]{:S(2)}) %all-to-all-start) | async-done | bytes 1966112 | tf_op jit(solution)/shard_map/all_to_all | solution.py:1040
  61.8 33.4 %collective-permute-done.2.refs_2_ = bf16[2560,384]{1,0:T(8,128)(2,1)S(1)} collective-permute-done((bf16[2560,384]{1,0:T(8,128)(2,1)S(1)}, bf16[2560,384]{1,0:T(8,128)(2,1)S(1)}, u32[]{:S(2)}, u32[]{:S(2)}) %collective-permute-start.2) | collective-permute-done | bytes 1966112 | tf_op jit(solution)/shard_map/ppermute | solution.py:929
  137.7 18.6 %all-to-all-done.1 = bf16[16,16,2560]{2,1,0:T(8,128)(2,1)} async-done(((bf16[16,16,2560]{2,1,0:T(8,128)(2,1)}), bf16[16,16,2560]{2,1,0:T(8,128)(2,1)}, u32[]{:S(2)}, u32[]{:S(2)}) %all-to-all-start.1) | async-done | bytes 1310752 | tf_op jit(solution)/shard_map/all_to_all | solution.py:92
  156.3 8.1 %collective-permute-start.12 = (bf16[2560,384]{1,0:T(8,128)(2,1)}, bf16[2560,384]{1,0:T(8,128)(2,1)}, u32[]{:S(2)}, u32[]{:S(2)}) collective-permute-start(bf16[2560,384]{1,0:T(8,128)(2,1)} %collective-permute-done.8.refs_3_), channel_id=1, source_target_pairs={{0,64},{64,0},{1,65},{65,1},{2,66},{66,2},{3,67},{67,3},{4,68},{68... | collective-permute-start | bytes 5898248 | tf_op jit(solution)/shard_map/ppermute | solution.py:45
  168.3 8.2 %ffn_forward.2 = (bf16[256,2560]{1,0:T(8,128)(2,1)}, f32[256,1024]{1,0:T(8,128)}, bf16[256,512]{1,0:T(8,128)(2,1)}) custom-call(s32[2]{0:T(128)} %pad_add_fusion.own_ref, bf16[256,2560]{1,0:T(8,128)(2,1)} %bitcast.24.n_ref, bf16[2560,384]{1,0:T(8,128)(2,1)} %bitcast.166, bf16[2560,384]{1,0:T(8,128)(2,1)} %collective-permute-done.1.refs_1_, ...), custom_call_target="tpu_custom_call" | custom-call | tf_op jit(solution)/shard_map/ffn_forward/pallas_call | solution.py:162
  176.5 29.0 %all_to_all.60 = bf16[16,16,2560]{2,1,0:T(8,128)(2,1)S(1)} all-to-all(bf16[16,16,2560]{2,1,0:T(8,128)(2,1)} %bitcast.178), channel_id=1, replica_groups=mesh['section'=2,'tensor'=4,'dp'=16] {'dp'}, dimensions={0} | all-to-all | bytes 2621440 | tf_op jit(solution)/shard_map/all_to_all | solution.py:96
  253.2 14.5 %all-to-all-done.3 = bf16[16,16,2560]{2,1,0:T(8,128)(2,1)S(1)} async-done(((bf16[16,16,2560]{2,1,0:T(8,128)(2,1)}), bf16[16,16,2560]{2,1,0:T(8,128)(2,1)S(1)}, u32[]{:S(2)}, u32[]{:S(2)}) %all-to-all-start.3) | async-done | bytes 1310752 | tf_op jit(solution)/shard_map/all_to_all | solution.py:92
  268.7 8.1 %ffn_forward.3 = (bf16[256,2560]{1,0:T(8,128)(2,1)}, f32[256,1024]{1,0:T(8,128)}, bf16[256,512]{1,0:T(8,128)(2,1)}) custom-call(s32[2]{0:T(128)} %pad_add_fusion.1.own_ref, bf16[256,2560]{1,0:T(8,128)(2,1)} %bitcast.170, bf16[2560,384]{1,0:T(8,128)(2,1)} %bitcast.167, bf16[2560,384]{1,0:T(8,128)(2,1)} %collective-permute-done.1.refs_1_, ...), custom_call_target="tpu_custom_call" | custom-call | tf_op jit(solution)/shard_map/ffn_forward/pallas_call | solution.py:162
  276.8 8.4 %ffn_backward.2 = (bf16[256,2560]{1,0:T(8,128)(2,1)}, bf16[256,1024]{1,0:T(8,128)(2,1)}) custom-call(s32[2]{0:T(128)} %pad_add_fusion.1.own_ref, bf16[256,2560]{1,0:T(8,128)(2,1)} %bitcast.172, f32[256,1024]{1,0:T(8,128)} %get-tuple-element.159.gu_ref, bf16[2560,384]{1,0:T(8,128)(2,1)} %bitcast.168, bf16[2560,384]{1,0:T(8,128)(2,1)} %collective-permute-done.1.refs_1_, ...), custom_call_target="tpu_custom_call" | custom-call | tf_op jit(solution)/shard_map/ffn_backward/pallas_call | solution.py:204
  298.7 7.3 %all-to-all-done.4 = bf16[16,16,2560]{2,1,0:T(8,128)(2,1)S(1)} async-done(((bf16[16,16,2560]{2,1,0:T(8,128)(2,1)}), bf16[16,16,2560]{2,1,0:T(8,128)(2,1)S(1)}, u32[]{:S(2)}, u32[]{:S(2)}) %all-to-all-start.4) | async-done | bytes 1310752 | tf_op jit(solution)/shard_map/all_to_all | solution.py:96
  318.9 5.5 collective-permute-start.25
  330.2 6.1 %attend_back.2 = (bf16[128,1152]{1,0:T(8,128)(2,1)S(1)}, bf16[128,640]{1,0:T(8,128)(2,1)S(1)}, bf16[128,640]{1,0:T(8,128)(2,1)S(1)}) custom-call(bf16[64,2560]{1,0:T(8,128)(2,1)S(1)} %pad_maximum_fusion.8.mine_ref, bf16[64,2560]{1,0:T(8,128)(2,1)S(1)} %collective-permute-done.25.other_ref, f32[4,128,128]{2,1,0:T(8,128)S(1)} %pad_maximum_fusion.11.tab_ref.tab_hbm, ...), custom_call_target="tpu_custom_call" | custom-call | tf_op jit(solution)/shard_map/attend_back/pallas_call | solution.py:538
  336.9 6.3 %ffn_gradients.2 = (bf16[16,80,384]{2,1,0:T(8,128)(2,1)}, bf16[16,80,384]{2,1,0:T(8,128)(2,1)}, bf16[16,80,384]{2,1,0:T(8,128)(2,1)}, bf16[16,80,384]{2,1,0:T(8,...) custom-call(s32[2]{0:T(128)} %pad_add_fusion.1.own_ref, ...), custom_call_target="tpu_custom_call" | custom-call | flops 2013265920 | bytes 16777216 | tf_op jit(solution)/shard_map/ffn_gradients/pallas_call | solution.py:263
  394.4 8.4 %ffn_backward.3 = (bf16[256,2560]{1,0:T(8,128)(2,1)}, bf16[256,1024]{1,0:T(8,128)(2,1)}) custom-call(s32[2]{0:T(128)} %pad_add_fusion.own_ref, bf16[256,2560]{1,0:T(8,128)(2,1)} %bitcast.36.dm_ref, f32[256,1024]{1,0:T(8,128)} %get-tuple-element.187.gu_ref, bf16[2560,384]{1,0:T(8,128)(2,1)} %bitcast.169, bf16[2560,384]{1,0:T(8,128)(2,1)} %collective-permute-done.1.refs_1_, ...), custom_call_target="tpu_custom_call" | custom-call | tf_op jit(solution)/shard_map/ffn_backward/pallas_call | solution.py:204
  402.8 5.1 all-to-all-start.7
  441.9 6.3 %ffn_gradients.3 = (bf16[16,80,384]{2,1,0:T(8,128)(2,1)}, bf16[16,80,384]{2,1,0:T(8,128)(2,1)}, bf16[16,80,384]{2,1,0:T(8,128)(2,1)}, bf16[16,80,384]{2,1,0:T(8,...) custom-call(s32[2]{0:T(128)} %pad_add_fusion.own_ref, ...), custom_call_target="tpu_custom_call" | custom-call | flops 2013265920 | bytes 16777216 | tf_op jit(solution)/shard_map/ffn_gradients/pallas_call | solution.py:263
  448.6 6.2 %attend_back.3 = (bf16[128,1152]{1,0:T(8,128)(2,1)S(1)}, bf16[128,640]{1,0:T(8,128)(2,1)S(1)}, bf16[128,640]{1,0:T(8,128)(2,1)S(1)}) custom-call(bf16[64,2560]{1,0:T(8,128)(2,1)S(1)} %pad_maximum_fusion.10.mine_ref, bf16[64,2560]{1,0:T(8,128)(2,1)S(1)} %collective-permute-done.49.other_ref, f32[4,128,128]{2,1,0:T(8,128)S(1)} %pad_maximum_fusion.11.tab_ref.tab_hbm, ...), custom_call_target="tpu_custom_call" | custom-call | tf_op jit(solution)/shard_map/attend_back/pallas_call | solution.py:538
  457.1 5.2 collective-permute-start.50
  498.1 6.2 %collective-permute-done.58 = bf16[16,80,384]{2,1,0:T(8,128)(2,1)} collective-permute-done((bf16[16,80,384]{2,1,0:T(8,128)(2,1)}, bf16[16,80,384]{2,1,0:T(8,128)(2,1)}, u32[]{:S(2)}, u32[]{:S(2)}) %collective-permute-start.58) | collective-permute-done | bytes 983072 | tf_op jit(solution)/shard_map/ppermute | solution.py:929
  512.0 7.1 %all-to-all-start.10 = ((bf16[16,16,1152]{2,1,0:T(8,128)(2,1)}), bf16[16,16,1152]{2,1,0:T(8,128)(2,1)S(1)}, u32[]{:S(2)}, u32[]{:S(2)}) async-start(bf16[16,16,1152]{2,1,0:T(8,128)(2,1)} %broadcast_in_dim.150), calls=%async_computation.10 | async-start | bytes 1179648 | tf_op jit(solution)/shard_map/all_to_all | solution.py:1139
  558.8 6.4 %collective-permute-done.74 = bf16[160,1152]{1,0:T(8,128)(2,1)S(1)} collective-permute-done((bf16[160,1152]{1,0:T(8,128)(2,1)S(1)}, bf16[160,1152]{1,0:T(8,128)(2,1)S(1)}, u32[]{:S(2)}, u32[]{:S(2)}) %collective-permute-start.74) | collective-permute-done | bytes 368672 | tf_op jit(solution)/shard_map/ppermute | solution.py:49
  565.1 10.6 %collective-permute-start.79 = (f32[160,384]{1,0:T(8,128)S(1)}, f32[160,384]{1,0:T(8,128)S(1)}, u32[]{:S(2)}, u32[]{:S(2)}) collective-permute-start(f32[160,384]{1,0:T(8,128)S(1)} %wo_gradient.1.wo1_ref), channel_id=1, source_target_pairs={{64,0},{65,1},{66,2},{67,3},{68,4},{69,5},{70,6},{71,7},{72,8},{73... | collective-permute-start | bytes 737288 | tf_op jit(solution)/shard_map/ppermute | solution.py:1158
  596.8 5.0 ffn_unpack.1
  (583 shorter events, 337.9 us)
Async XLA Ops:
  7.3 92.1 %all-gather.7.cloned.1.call-start = ((), (), s32[]{:S(2)}) async-start(), calls=%async_computation.13 | async-start | bytes 6823936 | tf_op jit(solution)/shard_map/all_gather | solution.py:1038
  15.5 39.1 %all-to-all-start = ((bf16[16,160,384]{2,1,0:T(8,128)(2,1)}), bf16[16,160,384]{2,1,0:T(8,128)(2,1)S(1)}, u32[]{:S(2)}, u32[]{:S(2)}) async-start(bf16[16,160,384]{2,1,0:T(8,128)(2,1)} %ffn_pack.1), calls=%async_computation | async-start | bytes 3932160 | tf_op jit(solution)/shard_map/all_to_all | solution.py:1040
  22.4 194.8 %all-gather.9.cloned.1.call-start = ((), (), s32[]{:S(2)}) async-start(), calls=%async_computation.14 | async-start | bytes 9748480 | tf_op jit(solution)/shard_map/all_gather | solution.py:1070
  54.7 40.5 %collective-permute-start.2 = (bf16[2560,384]{1,0:T(8,128)(2,1)S(1)}, bf16[2560,384]{1,0:T(8,128)(2,1)S(1)}, u32[]{:S(2)}, u32[]{:S(2)}) collective-permute-start(bf16[2560,384]{1,0:T(8,128)(2,1)S(1)} %bitcast.163), channel_id=1, source_target_pairs={{0,48},{16,0},{32,16},{48,32},{64,80},{80,96},{96,112},{112,64},{1... | collective-permute-start | bytes 5898248 | tf_op jit(solution)/shard_map/ppermute | solution.py:929
  56.4 43.0 %collective-permute-start.1 = (bf16[2560,384]{1,0:T(8,128)(2,1)S(1)}, bf16[2560,384]{1,0:T(8,128)(2,1)}, u32[]{:S(2)}, u32[]{:S(2)}) collective-permute-start(bf16[2560,384]{1,0:T(8,128)(2,1)S(1)} %bitcast.164), channel_id=1, source_target_pairs={{0,16},{16,32},{32,48},{48,0},{64,112},{80,64},{96,80},{112,96},{1... | collective-permute-start | bytes 5898248 | tf_op jit(solution)/shard_map/ppermute | solution.py:929
  123.6 32.7 %collective-permute-start.8 = (bf16[2560,384]{1,0:T(8,128)(2,1)}, bf16[2560,384]{1,0:T(8,128)(2,1)}, u32[]{:S(2)}, u32[]{:S(2)}) collective-permute-start(bf16[2560,384]{1,0:T(8,128)(2,1)} %collective-permute-done.1.refs_1_), channel_id=1, source_target_pairs={{0,16},{16,32},{32,48},{48,0},{64,112},{80,64},{96,80},{112,96},{1... | collective-permute-start | bytes 5898248 | tf_op jit(solution)/shard_map/ppermute | solution.py:929
  131.1 25.1 %all-to-all-start.1 = ((bf16[16,16,2560]{2,1,0:T(8,128)(2,1)}), bf16[16,16,2560]{2,1,0:T(8,128)(2,1)}, u32[]{:S(2)}, u32[]{:S(2)}) async-start(bf16[16,16,2560]{2,1,0:T(8,128)(2,1)} %broadcast_in_dim.147), calls=%async_computation.1 | async-start | bytes 2621440 | tf_op jit(solution)/shard_map/all_to_all | solution.py:92
  135.5 171.4 %all-gather.11.cloned.1.call-start = ((), (), s32[]{:S(2)}) async-start(), calls=%async_computation.15 | async-start | bytes 1671168 | tf_op jit(solution)/shard_map/all_gather | solution.py:1091
  135.6 29.4 %collective-permute-start.9 = (bf16[2560,384]{1,0:T(8,128)(2,1)S(1)}, bf16[2560,384]{1,0:T(8,128)(2,1)}, u32[]{:S(2)}, u32[]{:S(2)}) collective-permute-start(bf16[2560,384]{1,0:T(8,128)(2,1)S(1)} %bitcast.165), channel_id=1, source_target_pairs={{0,64},{64,0},{1,65},{65,1},{2,66},{66,2},{3,67},{67,3},{4,68},{68... | collective-permute-start | bytes 5898248 | tf_op jit(solution)/shard_map/ppermute | solution.py:45
  137.2 27.8 %collective-permute-start.10 = (bf16[2560,384]{1,0:T(8,128)(2,1)}, bf16[2560,384]{1,0:T(8,128)(2,1)}, u32[]{:S(2)}, u32[]{:S(2)}) collective-permute-start(bf16[2560,384]{1,0:T(8,128)(2,1)} %collective-permute-done.1.refs_1_), channel_id=1, source_target_pairs={{0,64},{64,0},{1,65},{65,1},{2,66},{66,2},{3,67},{67,3},{4,68},{68... | collective-permute-start | bytes 5898248 | tf_op jit(solution)/shard_map/ppermute | solution.py:45
  137.3 27.7 %collective-permute-start.11 = (bf16[2560,384]{1,0:T(8,128)(2,1)}, bf16[2560,384]{1,0:T(8,128)(2,1)}, u32[]{:S(2)}, u32[]{:S(2)}) collective-permute-start(bf16[2560,384]{1,0:T(8,128)(2,1)} %copy-done.26), channel_id=1, source_target_pairs={{0,64},{64,0},{1,65},{65,1},{2,66},{66,2},{3,67},{67,3},{4,68},{68... | collective-permute-start | bytes 5898248 | tf_op jit(solution)/shard_map/ppermute | solution.py:45
  324.5 25.5 %all-to-all-start.5 = ((bf16[16,16,2560]{2,1,0:T(8,128)(2,1)}), bf16[16,16,2560]{2,1,0:T(8,128)(2,1)}, u32[]{:S(2)}, u32[]{:S(2)}) async-start(bf16[16,16,2560]{2,1,0:T(8,128)(2,1)} %bitcast.175), calls=%async_computation.5 | async-start | bytes 2621440 | tf_op jit(solution)/shard_map/all_to_all | solution.py:96
  371.1 23.3 %all-to-all-start.6 = ((bf16[16,16,2560]{2,1,0:T(8,128)(2,1)}), bf16[16,16,2560]{2,1,0:T(8,128)(2,1)}, u32[]{:S(2)}, u32[]{:S(2)}) async-start(bf16[16,16,2560]{2,1,0:T(8,128)(2,1)} %broadcast_in_dim.149), calls=%async_computation.6 | async-start | bytes 2621440 | tf_op jit(solution)/shard_map/all_to_all | solution.py:92
  385.8 33.6 %collective-permute-start.39 = (bf16[16,80,384]{2,1,0:T(8,128)(2,1)}, bf16[16,80,384]{2,1,0:T(8,128)(2,1)}, u32[]{:S(2)}, u32[]{:S(2)}) collective-permute-start(bf16[16,80,384]{2,1,0:T(8,128)(2,1)} %add_convert_fusion.6), channel_id=1, source_target_pairs={{0,16},{16,32},{32,48},{48,0},{64,112},{80,64},{96,80},{112,96},{1... | collective-permute-start | bytes 2949128 | tf_op jit(solution)/shard_map/ppermute | solution.py:929
  392.7 26.7 %collective-permute-start.41 = (bf16[16,80,384]{2,1,0:T(8,128)(2,1)}, bf16[16,80,384]{2,1,0:T(8,128)(2,1)}, u32[]{:S(2)}, u32[]{:S(2)}) collective-permute-start(bf16[16,80,384]{2,1,0:T(8,128)(2,1)} %add_convert_fusion.5), channel_id=1, source_target_pairs={{0,48},{16,0},{32,16},{48,32},{64,80},{80,96},{96,112},{112,64},{1... | collective-permute-start | bytes 2949128 | tf_op jit(solution)/shard_map/ppermute | solution.py:929
  436.1 142.1 %reduce-scatter.4.cloned.1.call-start = ((), (), s32[]{:S(2)}) async-start(), calls=%async_computation.16 | async-start | bytes 6057984
  469.4 38.4 %all-to-all-start.9 = ((bf16[16,80,640]{2,1,0:T(8,128)(2,1)}), bf16[16,80,640]{2,1,0:T(8,128)(2,1)S(1)}, u32[]{:S(2)}, u32[]{:S(2)}) async-start(bf16[16,80,640]{2,1,0:T(8,128)(2,1)} %low_gradients.1), calls=%async_computation.9 | async-start | bytes 3276800 | tf_op jit(solution)/shard_map/all_to_all | solution.py:1130
  482.2 25.6 %collective-permute-start.59 = (bf16[16,80,384]{2,1,0:T(8,128)(2,1)}, bf16[16,80,384]{2,1,0:T(8,128)(2,1)}, u32[]{:S(2)}, u32[]{:S(2)}) collective-permute-start(bf16[16,80,384]{2,1,0:T(8,128)(2,1)} %add_convert_fusion.2), channel_id=1, source_target_pairs={{0,16},{16,32},{32,48},{48,0},{64,112},{80,64},{96,80},{112,96},{1... | collective-permute-start | bytes 2949128 | tf_op jit(solution)/shard_map/ppermute | solution.py:929
  489.0 104.6 %collective-permute-start.87 = (bf16[16,80,384]{2,1,0:T(8,128)(2,1)}, bf16[16,80,384]{2,1,0:T(8,128)(2,1)}, u32[]{:S(2)}, u32[]{:S(2)}) collective-permute-start(bf16[16,80,384]{2,1,0:T(8,128)(2,1)} %all-to-all-done.8.two), channel_id=1, source_target_pairs={{0,64},{1,65},{2,66},{3,67},{4,68},{5,69},{6,70},{7,71},{8,72},{9,... | collective-permute-start | bytes 2949128 | tf_op jit(solution)/shard_map/ppermute | solution.py:1154
  493.5 25.6 %collective-permute-start.70 = (bf16[48,128]{1,0:T(8,128)(2,1)S(1)}, bf16[48,128]{1,0:T(8,128)(2,1)S(1)}, u32[]{:S(2)}, u32[]{:S(2)}) collective-permute-start(bf16[48,128]{1,0:T(8,128)(2,1)S(1)} %add_convert_fusion.12), channel_id=1, source_target_pairs={{0,16},{16,32},{32,48},{48,0},{1,17},{17,33},{33,49},{49,1},{2,18}... | collective-permute-start | bytes 36872 | tf_op jit(solution)/shard_map/ppermute | solution.py:49
  493.9 25.3 %collective-permute-start.69 = (bf16[48,128]{1,0:T(8,128)(2,1)S(1)}, bf16[48,128]{1,0:T(8,128)(2,1)S(1)}, u32[]{:S(2)}, u32[]{:S(2)}) collective-permute-start(bf16[48,128]{1,0:T(8,128)(2,1)S(1)} %add_convert_fusion.12), channel_id=1, source_target_pairs={{0,32},{16,48},{32,0},{48,16},{1,33},{17,49},{33,1},{49,17},{2,34}... | collective-permute-start | bytes 36872 | tf_op jit(solution)/shard_map/ppermute | solution.py:49
  541.4 60.5 %collective-permute-start.80 = (f32[64,640]{1,0:T(8,128)S(1)}, f32[64,640]{1,0:T(8,128)S(1)}, u32[]{:S(2)}, u32[]{:S(2)}) collective-permute-start(f32[64,640]{1,0:T(8,128)S(1)} %convert_reduce_fusion.low_ref), channel_id=1, source_target_pairs={{64,0},{65,1},{66,2},{67,3},{68,4},{69,5},{70,6},{71,7},{72,8},{73... | collective-permute-start | bytes 491528 | tf_op jit(solution)/shard_map/ppermute | solution.py:1158
  546.3 29.6 %all-to-all-start.11 = ((bf16[16,96,384]{2,1,0:T(8,128)(2,1)}), bf16[16,96,384]{2,1,0:T(8,128)(2,1)S(1)}, u32[]{:S(2)}, u32[]{:S(2)}) async-start(bf16[16,96,384]{2,1,0:T(8,128)(2,1)} %pad_maximum_fusion.1), calls=%async_computation.11 | async-start | bytes 2359296 | tf_op jit(solution)/shard_map/all_to_all | solution.py:1151
  565.1 36.7 %collective-permute-start.79 = (f32[160,384]{1,0:T(8,128)S(1)}, f32[160,384]{1,0:T(8,128)S(1)}, u32[]{:S(2)}, u32[]{:S(2)}) collective-permute-start(f32[160,384]{1,0:T(8,128)S(1)} %wo_gradient.1.wo1_ref), channel_id=1, source_target_pairs={{64,0},{65,1},{66,2},{67,3},{68,4},{69,5},{70,6},{71,7},{72,8},{73... | collective-permute-start | bytes 737288 | tf_op jit(solution)/shard_map/ppermute | solution.py:1158
  (161 other events, 1346.7 us)
Sparse Core Ops, SparseCore 0:
  15.6 79.5 all-gather.6
  104.7 93.5 all-gather.8
  238.2 49.8 all-gather.10
  442.0 98.7 reduce-scatter.3

commit v4 on v3

--- a/solution.py
+++ b/solution.py
@@ -306,41 +306,26 @@
     )(w_gate, w_up, w_down)
 
 
-def ffn_unpack_kernel(core_ref, one, one_got, two, two_got, gate_ref, up_ref, down_ref, wide_ref):
+def ffn_unpack_kernel(core_ref, blocks_ref, got_ref, gate_ref, up_ref, down_ref):
     first = core_ref[0] == 0
-    rows = slice(0, HALF_ROWS)
-    wide_ref[...] = jnp.zeros(wide_ref.shape, F32)
-    valid = lax.broadcasted_iota(jnp.int32, (HALF_ROWS, LANES), 1) < FF_PART
+    one, two = slice(0, HALF_ROWS), slice(HALF_ROWS, SLICE)
     for p in range(N_DP):
-        at = FF_PART * p // LANES * LANES
-        by = FF_PART * p - at
-        for m in range(3):
-            columns = slice(LANES * m, LANES * (m + 1))
-            low = jnp.where(first, one[p, rows, columns].astype(F32), two_got[p, :, columns].astype(F32))
-            high = jnp.where(first, one_got[p, rows, columns].astype(F32), two[p, :, columns].astype(F32))
-            for half, block in enumerate((low, high)):
-                block = jnp.where(valid, block, 0.0)
-                window = jnp.concatenate([block, jnp.zeros_like(block)], axis=1)
-                if by > 0:
-                    window = pltpu.roll(window, by, 1)
-                wide_ref[m, HALF_ROWS * half : HALF_ROWS * (half + 1), at : at + WINDOW] += window
-    gate_ref[...] = wide_ref[0, :, :FF]
-    up_ref[...] = wide_ref[1, :, :FF]
-    down_ref[...] = wide_ref[2, :, :FF]
+        columns = slice(FF_PART * p, FF_PART * (p + 1))
+        for m, out_ref in enumerate((gate_ref, up_ref, down_ref)):
+            lanes = slice(LANES * m, LANES * (m + 1))
+            low = jnp.where(first, blocks_ref[p, one, lanes], got_ref[p, two, lanes])
+            high = jnp.where(first, got_ref[p, one, lanes], blocks_ref[p, two, lanes])
+            out_ref[one, columns] = low[:, :FF_PART].astype(F32)
+            out_ref[two, columns] = high[:, :FF_PART].astype(F32)
 
 
 def ffn_unpack(core, *blocks):
     vmem = pl.BlockSpec(memory_space=pltpu.VMEM)
     return pl.pallas_call(
         ffn_unpack_kernel,
-        out_shape=(
-            jax.ShapeDtypeStruct((SLICE, FF), F32),
-            jax.ShapeDtypeStruct((SLICE, FF), F32),
-            jax.ShapeDtypeStruct((SLICE, FF), F32),
-        ),
-        in_specs=[pl.BlockSpec(memory_space=pltpu.SMEM)] + [vmem] * 4,
+        out_shape=(jax.ShapeDtypeStruct((SLICE, FF), F32),) * 3,
+        in_specs=[pl.BlockSpec(memory_space=pltpu.SMEM), vmem, vmem],
         out_specs=(vmem,) * 3,
-        scratch_shapes=[pltpu.VMEM((3, SLICE, FF_PADDED), F32)],
         compiler_params=pltpu.CompilerParams(vmem_limit_bytes=FF_VMEM),
         name="ffn_unpack",
     )(core, *blocks)
@@ -689,25 +674,30 @@
     )(rows, normed)
 
 
-L_ROWS = SLICE + 16
+L_ROWS = 2 * SLICE
 
 
 def late_kernel(rows_ref, gains_ref, normed_hbm, packs_ref, out_ref, late_ref, normed_ref, sem, out_sem):
     copy = pltpu.make_async_copy(normed_hbm, normed_ref, sem)
     copy.start()
-    late_ref[:, SLICE:, :HEAD] = gains_ref[...]
-    late_ref[:, SLICE:, HEAD : 2 * HEAD] = jnp.zeros(gains_ref.shape, BF16)
-    late_ref[:, :, 2 * HEAD :] = jnp.zeros((N_DP, L_ROWS, WO - 2 * HEAD), BF16)
+    late_ref[:, SLICE : SLICE + 16, 2 * HEAD :] = gains_ref[...]
+    late_ref[:, SLICE + 16 :, 2 * HEAD :] = jnp.zeros((N_DP, SLICE - 16, HEAD), BF16)
     copy.wait()
     grad = dot_tn(normed_ref[...], rows_ref[...]).astype(BF16)
-    late_ref[:, :SLICE, : 2 * HEAD] = grad.reshape(N_DP, SLICE, 2 * HEAD)
+    late_ref[:, :SLICE, :] = grad[:, :WO].reshape(N_DP, SLICE, WO)
+    late_ref[:, SLICE:, : 2 * HEAD] = grad[:, WO:].reshape(N_DP, SLICE, 2 * HEAD)
     copy = pltpu.make_async_copy(late_ref, out_ref.at[:, E_ROWS:], out_sem)
     copy.start()
     copy.wait()
 
 
+def gain_vectors(gains):
+    parts = (gains[:D], gains[D : 2 * D], gains[2 * D : 2 * D + QR], gains[2 * D + QR : 2 * D + QR + KVR])
+    return [x.reshape(N_DP, -1) for x in parts]
+
+
 def late_pack(normed, rows, gains, packs):
-    attn, q, kv, ffn = (g.reshape(N_DP, -1) for g in gains)
+    attn, ffn, q, kv = gain_vectors(gains)
     wide = ((0, 0), (0, 2 * HEAD - SLICE))
     row = jnp.concatenate([jnp.pad(attn, wide), jnp.pad(ffn, wide), q, kv], axis=1)
     row = jnp.pad(row, ((0, 0), (0, 16 * HEAD - row.shape[1]))).reshape(N_DP, 16, HEAD).astype(BF16)
@@ -751,8 +741,7 @@
 
 
 def home_kernel(
-    core_ref, lat_ref, wo1_ref, wo1_got_ref, low_ref, low_got_ref,
-    tiles_ref, tiles_got_ref, packs_ref, packs_got_ref,
+    core_ref, lat_ref, wo1_ref, wo1_got_ref, low_ref, low_got_ref, packs_ref, packs_got_ref,
     qa_ref, kva_ref, qb_ref, kvb_ref, wo_ref, gain_ref, heads_ref,
 ):
     first = core_ref[0] == 0
@@ -761,21 +750,17 @@
         return jnp.where(first, one.astype(F32), two.astype(F32))
 
     wide = slice(0, SLICE)
-    gains = jnp.zeros(gain_ref.shape, F32)
-    for z in range(N_Z):
-        low, high = tiles_got_ref[z], tiles_ref[z]
-        gains = gains + low[SLICE:].astype(F32) + high[SLICE:].astype(F32)
-        columns = slice(HEAD * z, HEAD * (z + 1))
-        qa_ref[:, columns] = pick(lat_ref[wide, columns], low[wide])
-        columns = slice(HEAD * (z + 4), HEAD * (z + 5))
-        both = pick(lat_ref[wide, columns], high[wide])
-        if z < 2:
-            qa_ref[:, columns] = both
-        else:
-            kva_ref[:, HEAD * (z - 2) : HEAD * (z - 1)] = both
-    gain_ref[...] = gains
-    rope = pick(lat_ref[wide, QR + KVR :], packs_ref[E_ROWS : E_ROWS + SLICE, HEAD : 2 * HEAD])
-    kva_ref[:, KVR:] = rope[:, :ROPE]
+    late, more = slice(E_ROWS, E_ROWS + SLICE), slice(E_ROWS + SLICE, E_ROWS + L_ROWS)
+    gain_rows = slice(E_ROWS + SLICE, E_ROWS + SLICE + 16)
+    gain_ref[...] = (
+        packs_ref[gain_rows, 2 * HEAD :].astype(F32) + packs_got_ref[gain_rows, 2 * HEAD :].astype(F32)
+    )
+    qa_ref[:, :WO] = pick(lat_ref[wide, :WO], packs_got_ref[late])
+    qa_ref[:, WO:512] = pick(lat_ref[wide, WO:512], packs_got_ref[more, :HEAD])
+    qa_ref[:, 512:] = pick(lat_ref[wide, 512:QR], packs_ref[late, : 2 * HEAD])
+    kva_ref[:, :HEAD] = pick(lat_ref[wide, QR : QR + HEAD], packs_ref[late, 2 * HEAD :])
+    kva_ref[:, HEAD:KVR] = pick(lat_ref[wide, QR + HEAD : QR + KVR], packs_ref[more, :HEAD])
+    kva_ref[:, KVR:] = pick(lat_ref[wide, QR + KVR :], packs_ref[more, HEAD : 2 * HEAD])[:, :ROPE]
     at = WO - HEADS * VD
     low, high = pick(wo1_ref[...], packs_got_ref[wide]), pick(wo1_got_ref[...], packs_ref[wide])
     wo_ref[...] = jnp.concatenate([low[:, at:], high[:, at:]], axis=1)
@@ -978,9 +963,8 @@
     return d_middle + grad_own, ffn_gain
 
 
-def attention_backward(part, d_middle, saved, pack, gains, also=()):
+def attention_backward(part, d_middle, saved, pack, gains, also=(), after=()):
     core = lax.axis_index("section")
-    t = lax.axis_index("tensor")
     x_own, _, _, _, _, _, latent_own, _ = saved
     d_latent, also = tie((scatter_tokens(part), also))
     d_q, q_gain = norm_back(latent_own[:, :QR], gains["q"], d_latent[:, :QR])
@@ -992,19 +976,12 @@
     mine = jnp.where(core == 0, d_first, d_second)
     other = to_core(jnp.where(core == 0, d_second, d_first))
     both = jnp.concatenate([mine, other], axis=0)
+    both, after = tie((both, after))
     part = normed_back(both, pack)
     d_normed = part[:SHARD] + to_core(part[SHARD:])
     d_block, attn_gain = norm_back(x_own, gains["attn"], d_normed)
     d_block = (d_block + d_middle).astype(BF16)
-    columns = both.reshape(2 * SHARD, LAT // HEAD, HEAD).transpose(1, 0, 2)
-
-    def piece(by):
-        tile = lax.dynamic_index_in_dim(columns, (t + by) % N_Z, 0, keepdims=False)
-        return jnp.concatenate([tile, columns[N_Z]], axis=1)
-
-    rows = jnp.stack([piece(0), z_hop(piece(3), -1), z_hop(piece(2), 2), z_hop(piece(1), 1)])
-    rows = rows.reshape(N_Z, 2, SHARD, 2 * HEAD).transpose(1, 0, 2, 3).reshape(ROWS, 2 * HEAD)
-    return d_block, rows, jnp.concatenate([d_q, d_c, d_rope, blank[:, ROPE:]], axis=1), (attn_gain, q_gain, kv_gain), also
+    return d_block, both, jnp.concatenate([d_q, d_c, d_rope, blank[:, ROPE:]], axis=1), (attn_gain, q_gain, kv_gain), also, after
 
 
 def scatter_sum(x):
@@ -1094,16 +1071,22 @@
     part, d_gu = ffn_backward(own_two, d_rows_two, gu, ffn_weights)
     grads_two = ffn_gradients(own_two, d_rows_two, ffn_rows, d_gu, hidden)
     d_normed_two = scatter_dp(part)
-    d_normed_two, mixed_one = tie((d_normed_two, mixed_one))
+    d_normed_two, mixed_one, normed_one = tie((d_normed_two, mixed_one, normed_one))
     ring_two = ring_pairs(grads_two)
     d_middle, ffn_gain_two = middle_backward(cot_own, d_normed_two, saved_two, gains_two)
     d_attended = d_attended_rows(d_middle)
     part, d_query, d_key_value = attend_back(d_attended, tab, saved_two[-1], attn_two)
     packs_two = attend_gradients(d_attended, saved_two[-1], d_query, d_key_value)
-    in_grad_two, rows, _, dg_two, part_two = attention_backward(
+    in_grad_two, rows, _, dg_two, part_two, _ = attention_backward(
         part, d_middle, saved_two, attn_two, gains_two, scatter_dp(part_two)
     )
-    packs_two = late_pack(saved_two[5], rows, (*dg_two, ffn_gain_two), packs_two).reshape(-1, WO)
+    attn, q, kv = dg_two
+    dg_two = jnp.concatenate([attn, ffn_gain_two, q, kv])
+    dg_two = jnp.pad(dg_two, (0, 10 * LAT - dg_two.shape[0])).astype(BF16).reshape(10, LAT)
+    rows = jnp.stack(gather_z(jnp.concatenate([rows, dg_two], axis=0)))
+    dg_two = jnp.sum(rows[:, 2 * SHARD :].astype(F32), axis=0).reshape(-1)
+    rows = rows[:, : 2 * SHARD].reshape(N_Z, 2, SHARD, LAT).transpose(1, 0, 2, 3).reshape(ROWS, LAT)
+    packs_two = late_pack(saved_two[5], rows, dg_two, packs_two).reshape(-1, WO)
     in_grad_two, ring_two = tie((in_grad_two, ring_two))
     ring_two = ring_first(ring_two)
 
@@ -1116,76 +1099,78 @@
     d_normed_two = scatter_dp(part)
     total_two = ring_last(ring_two)
     rows_two = gather_tokens(layer_out_rows(part_two, saved_two))
-    d_normed_two, total_two, rows_two = tie((d_normed_two, total_two, rows_two))
+    d_normed_two, total_two, rows_two, grads_one = tie((d_normed_two, total_two, rows_two, grads_one))
     d_middle, ffn_gain_one = middle_backward(grad_one, d_normed_two, saved_one, gains_one)
     d_att_own = (RES_SCALE * d_middle).astype(BF16)
     columns = d_att_own.reshape(SHARD, N_DP, SLICE).transpose(1, 0, 2)
-    home_two = lax.all_to_all(total_two, "dp", 0, 0)
-    d_attended, grads_one, columns, home_two = tie(
-        (gather_tokens(d_att_own), grads_one, columns, home_two)
-    )
+    d_attended = gather_tokens(d_att_own)
     part, d_query, d_key_value = attend_back(d_attended, tab, saved_one[-1], attn_one)
     low_one = low_gradients(saved_one[-1], d_query, d_key_value, columns)
     part, low_one = tie((part, low_one))
     low_one = lax.all_to_all(low_one, "dp", 0, 0)
-    in_grad_one, _, d_lat_own, dg_one, pairs = attention_backward(
-        part, d_middle, saved_one, attn_one, gains_one, ring_pairs(grads_one)
+    first = ring_first(ring_pairs(grads_one))
+    in_grad_one, _, d_lat_own, dg_one, low_one, first = attention_backward(
+        part, d_middle, saved_one, attn_one, gains_one, low_one, first
     )
     d_lat = jnp.broadcast_to(d_lat_own.astype(BF16)[None], (N_DP, SHARD, LAT_ALL))
-    d_lat, low_one, first = tie((d_lat, low_one, ring_first(pairs)))
     columns = gather_tokens(low_one[:, LOW_ROWS:, :SLICE].reshape(TOKENS, SLICE))
     wo_one = wo_gradient(columns, mixed_one)
     low_one = jnp.sum(low_one[:, :LOW_ROWS].astype(F32), axis=0)
     d_lat = lax.all_to_all(d_lat, "dp", 0, 0)
     lat_one = latent_gradient(d_lat, normed_one)
-    total_one, lat_one, in_grad_one = tie((ring_last(first), lat_one, in_grad_one))
-
+    total_one, lat_one = tie((ring_last(first), lat_one))
+
+    attn, q, kv = dg_one
+    dg_one = jnp.concatenate([attn, ffn_gain_one, q, kv])
+    dg_one = jnp.pad(dg_one, (0, 3 * D - dg_one.shape[0])).astype(BF16).reshape(3, D)
+    got = to_core(jnp.concatenate([jnp.where(core == 0, in_grad_two, in_grad_one), dg_one], axis=0))
+    mine = jnp.where(core == 0, in_grad_one, in_grad_two)
+    dg_one = add(dg_one, got[SHARD:])
+    both = jnp.concatenate(
+        [jnp.concatenate([mine, dg_one], axis=0), jnp.pad(got[:SHARD], ((0, 3), (0, 0)))], axis=1
+    )
+    both = jnp.stack(gather_z(both))
+    dg_one = jnp.sum(both[:, SHARD:, :D].astype(F32), axis=0).reshape(-1)
+    both = both[:, :SHARD].reshape(PACK, 2 * D)
+    input_grad = in_order(both[:, :D], both[:, D:])[None]
+
+    row = jnp.concatenate(gain_vectors(dg_one), axis=1).astype(BF16)
+    row = jnp.pad(row[:, None], ((0, 0), (0, 15), (0, 0)))
     total_one = total_one.reshape(N_DP, HALF_ROWS, MATS)
-    attn, q, kv = dg_one
-    dg_one = jnp.concatenate([attn, ffn_gain_one, q, kv]).astype(BF16).reshape(-1, HEAD)
-    dg_one = add(dg_one, to_core(dg_one))
-    dg_one = sum(x.astype(F32) for x in gather_z(dg_one)).reshape(-1)
-    row = [dg_one[:D], dg_one[D : 2 * D], dg_one[2 * D : 2 * D + QR], dg_one[2 * D + QR :]]
-    row = jnp.concatenate([x.reshape(N_DP, -1) for x in row], axis=1).astype(BF16)
-    row = jnp.pad(row[:, None], ((0, 0), (0, 15), (0, 0)))
-    home_one = lax.all_to_all(jnp.concatenate([total_one, row], axis=1), "dp", 0, 0)
-    dg_one = jnp.sum(home_one[:, HALF_ROWS].astype(F32), axis=0)
-    got_one = lax.ppermute(home_one, "section", [(1, 0)])
-    got_two = lax.ppermute(home_two, "section", [(0, 1)])
-    gate_grad, up_grad, down_grad = ffn_unpack(core.reshape(1), home_one, got_one, home_two, got_two)
-
     def from_other(x, layer):
         return lax.ppermute(x, "section", [(1 - layer, layer)])
 
+    layer_out = in_order(*(jnp.where(core == 0, one, two) for one, two in zip(rows_one, rows_two)))
+    total_one, pieces, layer_out, input_grad = tie(
+        (
+            total_one,
+            (
+                wo_one,
+                from_other(wo_one, 0),
+                low_one,
+                from_other(low_one, 0),
+                packs_two,
+                from_other(packs_two, 1),
+            ),
+            layer_out,
+            input_grad,
+        )
+    )
+    blocks = jnp.concatenate([total_one, total_two.reshape(N_DP, HALF_ROWS, MATS), row], axis=1)
+    blocks = lax.all_to_all(blocks, "dp", 0, 0)
     lat_one = add(lat_one, from_other(lat_one, 0))
     lat_one = sum(x.astype(F32) for x in gather_z(lat_one))
-    packs_two, lat_one = tie((packs_two, lat_one))
-    tiles = from_zero(jnp.stack(gather_z(packs_two[E_ROWS:, :HEAD])))
-    qa_grad, kva_grad, qb_grad, kvb_grad, wo_grad, gains = home(
-        core.reshape(1),
-        lat_one,
-        wo_one,
-        from_other(wo_one, 0),
-        low_one,
-        from_other(low_one, 0),
-        tiles,
-        from_other(tiles, 1),
-        packs_two,
-        from_other(packs_two, 1),
-    )
+    blocks, attention = tie((blocks, home(core.reshape(1), lat_one, *pieces)))
+    qa_grad, kva_grad, qb_grad, kvb_grad, wo_grad, gains = attention
     gains = gains.reshape(-1)
+    dg_one = jnp.sum(blocks[:, SLICE].astype(F32), axis=0)
+    gate_grad, up_grad, down_grad = ffn_unpack(core.reshape(1), blocks, to_core(blocks))
 
     def gain_part(one, two, width):
         return jnp.where(core == 0, dg_one[one : one + width], gains[two : two + width])[None]
 
-    layer_out = in_order(*(jnp.where(core == 0, one, two) for one, two in zip(rows_one, rows_two)))[None]
-    give = jnp.where(core == 0, in_grad_two, in_grad_one)
-    mine = jnp.where(core == 0, in_grad_one, in_grad_two)
-    both = jnp.concatenate([mine, to_core(give)], axis=1)
-    both = jnp.concatenate(gather_z(both), axis=0)
-    input_grad = in_order(both[:, :D], both[:, D:])[None]
     return (
-        layer_out,
+        layer_out[None],
         input_grad,
         gain_part(0, 0, SLICE),
         qa_grad[None],

time: 622 us -> 606 us (0.974)
  starting transfers between devices: 197 us -> 158 us
  waiting for transfers between devices: 162 us -> 183 us
  local copies, waits for them, and re-layouts: 39.1 us -> 32 us
    ppermute x42 -> x36, starting transfers between devices: 62.4 us -> 46.6 us  [z_hop(): return lax.ppermute(x, 'tensor', [(i, (i + by) % N_Z) for i in range(N_Z)])]
    all_to_all x1, waiting for transfers between devices: 0.01 us -> 14.1 us  [body(): low_one = lax.all_to_all(low_one, 'dp', 0, 0)]
    ppermute x30, starting transfers between devices: 48.7 us -> 36.2 us  [to_core(): return lax.ppermute(x, 'section', [(0, 1), (1, 0)])]
    all_to_all x2 -> x0, starting transfers between devices: 8.66 us -> none  [the longest x1 4.34 us: body(): lax.all_to_all(jnp.concatenate([total_one, row], axis=1), 'dp', 0, 0)]
    ppermute x5 -> x4, starting transfers between devices: 17.8 us -> 9.6 us  [from_other(): return lax.ppermute(x, 'section', [(1 - layer, layer)])]
    all_to_all x1 -> x2, starting transfers between devices: 6.85 us -> 13.6 us  [body(): blocks = lax.all_to_all(blocks, 'dp', 0, 0)]
    all_to_all x1 -> x2, waiting for transfers between devices: 31.1 us -> 37 us  [body(): blocks = lax.all_to_all(blocks, 'dp', 0, 0)]
    ppermute x42 -> x36, waiting for transfers between devices: 28.3 us -> 34.2 us  [z_hop(): return lax.ppermute(x, 'tensor', [(i, (i + by) % N_Z) for i in range(N_Z)])]
  transfers between devices with their start and end apart: 103 -> 93, of which waited for: 35 -> 39; matrix products, arithmetic and copies ran while one was open for 15% -> 15% of each run, Pallas kernels for 14% -> 14%
where the time goes in v4:
time: 606 us; the launch traced here: 595 us
  waiting for transfers between devices  183 us (30%)
  starting transfers between devices  158 us (26%)
  Pallas kernels  98.5 us (16%)
  other arithmetic  74.4 us (12%)
  blocking collectives  32.9 us (5%)
  local copies, waits for them, and re-layouts  32 us (5%)
  between operations  16.4 us (3%)
    ppermute x36, starting transfers between devices, z_hop(): return lax.ppermute(x, 'tensor', [(i, (i + by) % N_Z) for i in range(N_Z)])  46.6 us
    ppermute x9, waiting for transfers between devices, ring_hop(): return lax.ppermute(x, ('section', 'tensor'), pairs)  43 us
    all_to_all x2, waiting for transfers between devices, body(): blocks = lax.all_to_all(blocks, 'dp', 0, 0)  37 us
    ppermute x30, starting transfers between devices, to_core(): return lax.ppermute(x, 'section', [(0, 1), (1, 0)])  36.2 us
    ppermute x36, waiting for transfers between devices, z_hop(): return lax.ppermute(x, 'tensor', [(i, (i + by) % N_Z) for i in range(N_Z)])  34.2 us
    all_to_all x1, blocking collectives, scatter_dp(): pieces = lax.all_to_all(part.reshape(N_DP, SHARD, D), 'dp', 0, 0)  32.9 us
    all_to_all x3, waiting for transfers between devices, gather_dp(): lax.all_to_all(copies, 'dp', 0, 0).reshape(N_DP * x.shape[0], x.shape[1])  30.8 us
    convert_element_type x10, other arithmetic, add(): return sum((x.astype(F32) for x in terms)).astype(BF16)  20.6 us
  transfers between devices with their start and end apart: 93, of which 39 were waited for; matrix products, arithmetic and copies ran while one was open for 15% of the time, Pallas kernels for 14%

profile of v4, /device:TPU:1, one launch (start us, length us, event | category | flops | bytes accessed | tf_op | source)
XLA Modules:
  0.0 595.5 jit_solution(11589945911564260722)
XLA Ops:
  15.3 6.8 %all-to-all-start = ((bf16[16,160,384]{2,1,0:T(8,128)(2,1)}), bf16[16,160,384]{2,1,0:T(8,128)(2,1)S(1)}, u32[]{:S(2)}, u32[]{:S(2)}) async-start(bf16[16,160,384]{2,1,0:T(8,128)(2,1)} %ffn_pack.1), calls=%async_computation | async-start | bytes 3932160 | tf_op jit(solution)/shard_map/all_to_all | solution.py:1017
  23.4 31.1 %all-to-all-done = bf16[16,160,384]{2,1,0:T(8,128)(2,1)S(1)} async-done(((bf16[16,160,384]{2,1,0:T(8,128)(2,1)}), bf16[16,160,384]{2,1,0:T(8,128)(2,1)S(1)}, u32[]{:S(2)}, u32[]{:S(2)}) %all-to-all-start) | async-done | bytes 1966112 | tf_op jit(solution)/shard_map/all_to_all | solution.py:1017
  61.5 33.5 %collective-permute-done.2.refs_2_ = bf16[2560,384]{1,0:T(8,128)(2,1)S(1)} collective-permute-done((bf16[2560,384]{1,0:T(8,128)(2,1)S(1)}, bf16[2560,384]{1,0:T(8,128)(2,1)S(1)}, u32[]{:S(2)}, u32[]{:S(2)}) %collective-permute-start.2) | collective-permute-done | bytes 1966112 | tf_op jit(solution)/shard_map/ppermute | solution.py:914
  133.1 16.3 %all-to-all-done.1 = bf16[16,16,2560]{2,1,0:T(8,128)(2,1)} async-done(((bf16[16,16,2560]{2,1,0:T(8,128)(2,1)}), bf16[16,16,2560]{2,1,0:T(8,128)(2,1)}, u32[]{:S(2)}, u32[]{:S(2)}) %all-to-all-start.1) | async-done | bytes 1310752 | tf_op jit(solution)/shard_map/all_to_all | solution.py:92
  149.4 6.4 %collective-permute-start.12 = (bf16[2560,384]{1,0:T(8,128)(2,1)}, bf16[2560,384]{1,0:T(8,128)(2,1)}, u32[]{:S(2)}, u32[]{:S(2)}) collective-permute-start(bf16[2560,384]{1,0:T(8,128)(2,1)} %collective-permute-done.8.refs_3_), channel_id=1, source_target_pairs={{0,64},{64,0},{1,65},{65,1},{2,66},{66,2},{3,67},{67,3},{4,68},{68... | collective-permute-start | bytes 5898248 | tf_op jit(solution)/shard_map/ppermute | solution.py:45
  159.7 8.1 %ffn_forward.2 = (bf16[256,2560]{1,0:T(8,128)(2,1)}, f32[256,1024]{1,0:T(8,128)}, bf16[256,512]{1,0:T(8,128)(2,1)}) custom-call(s32[2]{0:T(128)} %pad_add_fusion.own_ref, bf16[256,2560]{1,0:T(8,128)(2,1)} %bitcast.24.n_ref, bf16[2560,384]{1,0:T(8,128)(2,1)} %bitcast.146, bf16[2560,384]{1,0:T(8,128)(2,1)} %collective-permute-done.1.refs_1_, ...), custom_call_target="tpu_custom_call" | custom-call | tf_op jit(solution)/shard_map/ffn_forward/pallas_call | solution.py:162
  167.9 32.9 %all_to_all.55 = bf16[16,16,2560]{2,1,0:T(8,128)(2,1)S(1)} all-to-all(bf16[16,16,2560]{2,1,0:T(8,128)(2,1)} %bitcast.160), channel_id=1, replica_groups=mesh['section'=2,'tensor'=4,'dp'=16] {'dp'}, dimensions={0} | all-to-all | bytes 2621440 | tf_op jit(solution)/shard_map/all_to_all | solution.py:96
  247.1 14.5 %all-to-all-done.3 = bf16[16,16,2560]{2,1,0:T(8,128)(2,1)S(1)} async-done(((bf16[16,16,2560]{2,1,0:T(8,128)(2,1)}), bf16[16,16,2560]{2,1,0:T(8,128)(2,1)S(1)}, u32[]{:S(2)}, u32[]{:S(2)}) %all-to-all-start.3) | async-done | bytes 1310752 | tf_op jit(solution)/shard_map/all_to_all | solution.py:92
  262.6 8.1 %ffn_forward.3 = (bf16[256,2560]{1,0:T(8,128)(2,1)}, f32[256,1024]{1,0:T(8,128)}, bf16[256,512]{1,0:T(8,128)(2,1)}) custom-call(s32[2]{0:T(128)} %pad_add_fusion.1.own_ref, bf16[256,2560]{1,0:T(8,128)(2,1)} %bitcast.151, bf16[2560,384]{1,0:T(8,128)(2,1)} %bitcast.147, bf16[2560,384]{1,0:T(8,128)(2,1)} %collective-permute-done.1.refs_1_, ...), custom_call_target="tpu_custom_call" | custom-call | tf_op jit(solution)/shard_map/ffn_forward/pallas_call | solution.py:162
  270.8 8.4 %ffn_backward.2 = (bf16[256,2560]{1,0:T(8,128)(2,1)}, bf16[256,1024]{1,0:T(8,128)(2,1)}) custom-call(s32[2]{0:T(128)} %pad_add_fusion.1.own_ref, bf16[256,2560]{1,0:T(8,128)(2,1)} %bitcast.153, f32[256,1024]{1,0:T(8,128)} %get-tuple-element.164.gu_ref, bf16[2560,384]{1,0:T(8,128)(2,1)} %bitcast.148, bf16[2560,384]{1,0:T(8,128)(2,1)} %collective-permute-done.1.refs_1_, ...), custom_call_target="tpu_custom_call" | custom-call | tf_op jit(solution)/shard_map/ffn_backward/pallas_call | solution.py:204
  290.0 10.5 %all-to-all-done.4 = bf16[16,16,2560]{2,1,0:T(8,128)(2,1)S(1)} async-done(((bf16[16,16,2560]{2,1,0:T(8,128)(2,1)}), bf16[16,16,2560]{2,1,0:T(8,128)(2,1)S(1)}, u32[]{:S(2)}, u32[]{:S(2)}) %all-to-all-start.4) | async-done | bytes 1310752 | tf_op jit(solution)/shard_map/all_to_all | solution.py:96
  312.5 5.6 collective-permute-start.25
  324.0 6.1 %attend_back.2 = (bf16[128,1152]{1,0:T(8,128)(2,1)S(1)}, bf16[128,640]{1,0:T(8,128)(2,1)S(1)}, bf16[128,640]{1,0:T(8,128)(2,1)S(1)}) custom-call(bf16[64,2560]{1,0:T(8,128)(2,1)S(1)} %pad_maximum_fusion.8.mine_ref, bf16[64,2560]{1,0:T(8,128)(2,1)S(1)} %collective-permute-done.25.other_ref, f32[4,128,128]{2,1,0:T(8,128)S(1)} %pad_maximum_fusion.11.tab_ref.tab_hbm, ...), custom_call_target="tpu_custom_call" | custom-call | tf_op jit(solution)/shard_map/attend_back/pallas_call | solution.py:523
  330.6 6.3 %ffn_gradients.2 = (bf16[16,80,384]{2,1,0:T(8,128)(2,1)}, bf16[16,80,384]{2,1,0:T(8,128)(2,1)}, bf16[16,80,384]{2,1,0:T(8,128)(2,1)}, bf16[16,80,384]{2,1,0:T(8,...) custom-call(s32[2]{0:T(128)} %pad_add_fusion.1.own_ref, ...), custom_call_target="tpu_custom_call" | custom-call | flops 2013265920 | bytes 16777216 | tf_op jit(solution)/shard_map/ffn_gradients/pallas_call | solution.py:263
  388.7 8.4 %ffn_backward.3 = (bf16[256,2560]{1,0:T(8,128)(2,1)}, bf16[256,1024]{1,0:T(8,128)(2,1)}) custom-call(s32[2]{0:T(128)} %pad_add_fusion.own_ref, bf16[256,2560]{1,0:T(8,128)(2,1)} %bitcast.36.dm_ref, f32[256,1024]{1,0:T(8,128)} %get-tuple-element.192.gu_ref, bf16[2560,384]{1,0:T(8,128)(2,1)} %bitcast.149, bf16[2560,384]{1,0:T(8,128)(2,1)} %collective-permute-done.1.refs_1_, ...), custom_call_target="tpu_custom_call" | custom-call | tf_op jit(solution)/shard_map/ffn_backward/pallas_call | solution.py:204
  397.1 6.8 %all-to-all-start.7 = ((bf16[16,16,2560]{2,1,0:T(8,128)(2,1)}), bf16[16,16,2560]{2,1,0:T(8,128)(2,1)S(1)}, u32[]{:S(2)}, u32[]{:S(2)}) async-start(bf16[16,16,2560]{2,1,0:T(8,128)(2,1)} %bitcast.159), calls=%async_computation.7 | async-start | bytes 2621440 | tf_op jit(solution)/shard_map/all_to_all | solution.py:96
  416.1 6.5 %ffn_gradients.3 = (bf16[16,80,384]{2,1,0:T(8,128)(2,1)}, bf16[16,80,384]{2,1,0:T(8,128)(2,1)}, bf16[16,80,384]{2,1,0:T(8,128)(2,1)}, bf16[16,80,384]{2,1,0:T(8,...) custom-call(s32[2]{0:T(128)} %pad_add_fusion.own_ref, ...), custom_call_target="tpu_custom_call" | custom-call | flops 2013265920 | bytes 16777216 | tf_op jit(solution)/shard_map/ffn_gradients/pallas_call | solution.py:263
  437.6 6.2 %attend_back.3 = (bf16[128,1152]{1,0:T(8,128)(2,1)S(1)}, bf16[128,640]{1,0:T(8,128)(2,1)S(1)}, bf16[128,640]{1,0:T(8,128)(2,1)S(1)}) custom-call(bf16[64,2560]{1,0:T(8,128)(2,1)S(1)} %pad_maximum_fusion.10.mine_ref, bf16[64,2560]{1,0:T(8,128)(2,1)S(1)} %collective-permute-done.49.other_ref, f32[4,128,128]{2,1,0:T(8,128)S(1)} %pad_maximum_fusion.11.tab_ref.tab_hbm, ...), custom_call_target="tpu_custom_call" | custom-call | tf_op jit(solution)/shard_map/attend_back/pallas_call | solution.py:523
  448.1 6.9 %all-to-all-start.8 = ((bf16[16,80,640]{2,1,0:T(8,128)(2,1)}), bf16[16,80,640]{2,1,0:T(8,128)(2,1)S(1)}, u32[]{:S(2)}, u32[]{:S(2)}) async-start(bf16[16,80,640]{2,1,0:T(8,128)(2,1)} %low_gradients.1), calls=%async_computation.8 | async-start | bytes 3276800 | tf_op jit(solution)/shard_map/all_to_all | solution.py:1110
  470.6 14.1 %all-to-all-done.8 = bf16[16,80,640]{2,1,0:T(8,128)(2,1)S(1)} async-done(((bf16[16,80,640]{2,1,0:T(8,128)(2,1)}), bf16[16,80,640]{2,1,0:T(8,128)(2,1)S(1)}, u32[]{:S(2)}, u32[]{:S(2)}) %all-to-all-start.8) | async-done | bytes 1638432 | tf_op jit(solution)/shard_map/all_to_all | solution.py:1110
  529.3 6.7 %collective-permute-done.61 = bf16[16,80,384]{2,1,0:T(8,128)(2,1)} collective-permute-done((bf16[16,80,384]{2,1,0:T(8,128)(2,1)}, bf16[16,80,384]{2,1,0:T(8,128)(2,1)}, u32[]{:S(2)}, u32[]{:S(2)}) %collective-permute-start.61) | collective-permute-done | bytes 983072 | tf_op jit(solution)/shard_map/ppermute | solution.py:914
  540.2 6.7 %all-to-all-start.10 = ((bf16[16,176,384]{2,1,0:T(8,128)(2,1)}), bf16[16,176,384]{2,1,0:T(8,128)(2,1)}, u32[]{:S(2)}, u32[]{:S(2)}) async-start(bf16[16,176,384]{2,1,0:T(8,128)(2,1)} %pad_maximum_fusion.1), calls=%async_computation.11 | async-start | bytes 4325376 | tf_op jit(solution)/shard_map/all_to_all | solution.py:1160
  561.3 8.9 %collective-permute-done.76 = bf16[160,1152]{1,0:T(8,128)(2,1)S(1)} collective-permute-done((bf16[160,1152]{1,0:T(8,128)(2,1)S(1)}, bf16[160,1152]{1,0:T(8,128)(2,1)S(1)}, u32[]{:S(2)}, u32[]{:S(2)}) %collective-permute-start.76) | collective-permute-done | bytes 368672 | tf_op jit(solution)/shard_map/ppermute | solution.py:49
  571.6 5.9 all-to-all-done.10.blocks_ref
  (600 shorter events, 307.6 us)
Async XLA Ops:
  7.3 91.9 %all-gather.7.cloned.1.call-start = ((), (), s32[]{:S(2)}) async-start(), calls=%async_computation.13 | async-start | bytes 6823936 | tf_op jit(solution)/shard_map/all_gather | solution.py:1015
  15.3 39.1 %all-to-all-start = ((bf16[16,160,384]{2,1,0:T(8,128)(2,1)}), bf16[16,160,384]{2,1,0:T(8,128)(2,1)S(1)}, u32[]{:S(2)}, u32[]{:S(2)}) async-start(bf16[16,160,384]{2,1,0:T(8,128)(2,1)} %ffn_pack.1), calls=%async_computation | async-start | bytes 3932160 | tf_op jit(solution)/shard_map/all_to_all | solution.py:1017
  22.2 190.0 %all-gather.9.cloned.1.call-start = ((), (), s32[]{:S(2)}) async-start(), calls=%async_computation.14 | async-start | bytes 9748480 | tf_op jit(solution)/shard_map/all_gather | solution.py:1047
  54.5 40.5 %collective-permute-start.2 = (bf16[2560,384]{1,0:T(8,128)(2,1)S(1)}, bf16[2560,384]{1,0:T(8,128)(2,1)S(1)}, u32[]{:S(2)}, u32[]{:S(2)}) collective-permute-start(bf16[2560,384]{1,0:T(8,128)(2,1)S(1)} %bitcast.144), channel_id=1, source_target_pairs={{0,48},{16,0},{32,16},{48,32},{64,80},{80,96},{96,112},{112,64},{1... | collective-permute-start | bytes 5898248 | tf_op jit(solution)/shard_map/ppermute | solution.py:914
  56.2 43.0 %collective-permute-start.1 = (bf16[2560,384]{1,0:T(8,128)(2,1)S(1)}, bf16[2560,384]{1,0:T(8,128)(2,1)}, u32[]{:S(2)}, u32[]{:S(2)}) collective-permute-start(bf16[2560,384]{1,0:T(8,128)(2,1)S(1)} %bitcast.145), channel_id=1, source_target_pairs={{0,16},{16,32},{32,48},{48,0},{64,112},{80,64},{96,80},{112,96},{1... | collective-permute-start | bytes 5898248 | tf_op jit(solution)/shard_map/ppermute | solution.py:914
  120.0 29.4 %collective-permute-start.8 = (bf16[2560,384]{1,0:T(8,128)(2,1)}, bf16[2560,384]{1,0:T(8,128)(2,1)}, u32[]{:S(2)}, u32[]{:S(2)}) collective-permute-start(bf16[2560,384]{1,0:T(8,128)(2,1)} %collective-permute-done.1.refs_1_), channel_id=1, source_target_pairs={{0,16},{16,32},{32,48},{48,0},{64,112},{80,64},{96,80},{112,96},{1... | collective-permute-start | bytes 5898248 | tf_op jit(solution)/shard_map/ppermute | solution.py:914
  130.8 170.5 %all-gather.11.cloned.1.call-start = ((), (), s32[]{:S(2)}) async-start(), calls=%async_computation.15 | async-start | bytes 1671168 | tf_op jit(solution)/shard_map/all_gather | solution.py:1068
  130.9 25.5 %collective-permute-start.9 = (bf16[2560,384]{1,0:T(8,128)(2,1)S(1)}, bf16[2560,384]{1,0:T(8,128)(2,1)}, u32[]{:S(2)}, u32[]{:S(2)}) collective-permute-start(bf16[2560,384]{1,0:T(8,128)(2,1)S(1)} %bitcast.150), channel_id=1, source_target_pairs={{0,64},{64,0},{1,65},{65,1},{2,66},{66,2},{3,67},{67,3},{4,68},{68... | collective-permute-start | bytes 5898248 | tf_op jit(solution)/shard_map/ppermute | solution.py:45
  318.2 25.5 %all-to-all-start.5 = ((bf16[16,16,2560]{2,1,0:T(8,128)(2,1)}), bf16[16,16,2560]{2,1,0:T(8,128)(2,1)}, u32[]{:S(2)}, u32[]{:S(2)}) async-start(bf16[16,16,2560]{2,1,0:T(8,128)(2,1)} %bitcast.157), calls=%async_computation.5 | async-start | bytes 2621440 | tf_op jit(solution)/shard_map/all_to_all | solution.py:96
  361.6 24.6 %collective-permute-start.40 = (bf16[16,80,384]{2,1,0:T(8,128)(2,1)}, bf16[16,80,384]{2,1,0:T(8,128)(2,1)}, u32[]{:S(2)}, u32[]{:S(2)}) collective-permute-start(bf16[16,80,384]{2,1,0:T(8,128)(2,1)} %add_convert_fusion.7), channel_id=1, source_target_pairs={{0,48},{16,0},{32,16},{48,32},{64,80},{80,96},{96,112},{112,64},{1... | collective-permute-start | bytes 2949128 | tf_op jit(solution)/shard_map/ppermute | solution.py:914
  377.6 45.0 %collective-permute-start.39 = (bf16[16,80,384]{2,1,0:T(8,128)(2,1)}, bf16[16,80,384]{2,1,0:T(8,128)(2,1)}, u32[]{:S(2)}, u32[]{:S(2)}) collective-permute-start(bf16[16,80,384]{2,1,0:T(8,128)(2,1)} %add_convert_fusion.6), channel_id=1, source_target_pairs={{0,16},{16,32},{32,48},{48,0},{64,112},{80,64},{96,80},{112,96},{1... | collective-permute-start | bytes 2949128 | tf_op jit(solution)/shard_map/ppermute | solution.py:914
  388.7 34.0 %collective-permute-start.41 = (bf16[16,80,384]{2,1,0:T(8,128)(2,1)}, bf16[16,80,384]{2,1,0:T(8,128)(2,1)}, u32[]{:S(2)}, u32[]{:S(2)}) collective-permute-start(bf16[16,80,384]{2,1,0:T(8,128)(2,1)} %add_convert_fusion.5), channel_id=1, source_target_pairs={{0,48},{16,0},{32,16},{48,32},{64,80},{80,96},{96,112},{112,64},{1... | collective-permute-start | bytes 2949128 | tf_op jit(solution)/shard_map/ppermute | solution.py:914
  397.1 28.6 %all-to-all-start.7 = ((bf16[16,16,2560]{2,1,0:T(8,128)(2,1)}), bf16[16,16,2560]{2,1,0:T(8,128)(2,1)S(1)}, u32[]{:S(2)}, u32[]{:S(2)}) async-start(bf16[16,16,2560]{2,1,0:T(8,128)(2,1)} %bitcast.159), calls=%async_computation.7 | async-start | bytes 2621440 | tf_op jit(solution)/shard_map/all_to_all | solution.py:96
  403.9 123.3 %reduce-scatter.2.cloned.1.call-start = ((), (), s32[]{:S(2)}) async-start(), calls=%async_computation.12 | async-start | bytes 7938048 | tf_op jit(solution)/shard_map/reduce_scatter | solution.py:1095
  431.0 31.9 %collective-permute-start.55 = (bf16[16,80,384]{2,1,0:T(8,128)(2,1)}, bf16[16,80,384]{2,1,0:T(8,128)(2,1)}, u32[]{:S(2)}, u32[]{:S(2)}) collective-permute-start(bf16[16,80,384]{2,1,0:T(8,128)(2,1)} %get-tuple-element.224), channel_id=1, source_target_pairs={{0,64},{64,0},{1,65},{65,1},{2,66},{66,2},{3,67},{67,3},{4,68},{68... | collective-permute-start | bytes 2949128 | tf_op jit(solution)/shard_map/ppermute | solution.py:45
  431.8 33.7 %collective-permute-start.57 = (bf16[16,80,384]{2,1,0:T(8,128)(2,1)}, bf16[16,80,384]{2,1,0:T(8,128)(2,1)}, u32[]{:S(2)}, u32[]{:S(2)}) collective-permute-start(bf16[16,80,384]{2,1,0:T(8,128)(2,1)} %get-tuple-element.226), channel_id=1, source_target_pairs={{0,64},{64,0},{1,65},{65,1},{2,66},{66,2},{3,67},{67,3},{4,68},{68... | collective-permute-start | bytes 2949128 | tf_op jit(solution)/shard_map/ppermute | solution.py:45
  448.1 36.5 %all-to-all-start.8 = ((bf16[16,80,640]{2,1,0:T(8,128)(2,1)}), bf16[16,80,640]{2,1,0:T(8,128)(2,1)S(1)}, u32[]{:S(2)}, u32[]{:S(2)}) async-start(bf16[16,80,640]{2,1,0:T(8,128)(2,1)} %low_gradients.1), calls=%async_computation.8 | async-start | bytes 3276800 | tf_op jit(solution)/shard_map/all_to_all | solution.py:1110
  460.3 28.9 %collective-permute-start.59 = (bf16[16,80,384]{2,1,0:T(8,128)(2,1)}, bf16[16,80,384]{2,1,0:T(8,128)(2,1)}, u32[]{:S(2)}, u32[]{:S(2)}) collective-permute-start(bf16[16,80,384]{2,1,0:T(8,128)(2,1)} %get-tuple-element.228), channel_id=1, source_target_pairs={{0,64},{64,0},{1,65},{65,1},{2,66},{66,2},{3,67},{67,3},{4,68},{68... | collective-permute-start | bytes 2949128 | tf_op jit(solution)/shard_map/ppermute | solution.py:45
  460.9 31.9 %collective-permute-start.60 = (bf16[16,80,384]{2,1,0:T(8,128)(2,1)}, bf16[16,80,384]{2,1,0:T(8,128)(2,1)}, u32[]{:S(2)}, u32[]{:S(2)}) collective-permute-start(bf16[16,80,384]{2,1,0:T(8,128)(2,1)} %get-tuple-element.230), channel_id=1, source_target_pairs={{0,64},{64,0},{1,65},{65,1},{2,66},{66,2},{3,67},{67,3},{4,68},{68... | collective-permute-start | bytes 2949128 | tf_op jit(solution)/shard_map/ppermute | solution.py:45
  465.4 28.0 %collective-permute-start.56 = (bf16[16,80,384]{2,1,0:T(8,128)(2,1)}, bf16[16,80,384]{2,1,0:T(8,128)(2,1)}, u32[]{:S(2)}, u32[]{:S(2)}) collective-permute-start(bf16[16,80,384]{2,1,0:T(8,128)(2,1)} %add_convert_fusion.3), channel_id=1, source_target_pairs={{0,48},{16,0},{32,16},{48,32},{64,80},{80,96},{96,112},{112,64},{1... | collective-permute-start | bytes 2949128 | tf_op jit(solution)/shard_map/ppermute | solution.py:914
  467.9 25.5 %collective-permute-start.58 = (bf16[16,80,384]{2,1,0:T(8,128)(2,1)}, bf16[16,80,384]{2,1,0:T(8,128)(2,1)}, u32[]{:S(2)}, u32[]{:S(2)}) collective-permute-start(bf16[16,80,384]{2,1,0:T(8,128)(2,1)} %add_convert_fusion.2), channel_id=1, source_target_pairs={{0,16},{16,32},{32,48},{48,0},{64,112},{80,64},{96,80},{112,96},{1... | collective-permute-start | bytes 2949128 | tf_op jit(solution)/shard_map/ppermute | solution.py:914
  498.2 40.4 %collective-permute-start.67 = (f32[64,640]{1,0:T(8,128)S(1)}, f32[64,640]{1,0:T(8,128)S(1)}, u32[]{:S(2)}, u32[]{:S(2)}) collective-permute-start(f32[64,640]{1,0:T(8,128)S(1)} %convert_reduce_fusion.low_ref), channel_id=1, source_target_pairs={{64,0},{65,1},{66,2},{67,3},{68,4},{69,5},{70,6},{71,7},{72,8},{73... | collective-permute-start | bytes 491528 | tf_op jit(solution)/shard_map/ppermute | solution.py:1141
  501.0 28.0 %all-to-all-start.9 = ((bf16[16,16,1152]{2,1,0:T(8,128)(2,1)}), bf16[16,16,1152]{2,1,0:T(8,128)(2,1)S(1)}, u32[]{:S(2)}, u32[]{:S(2)}) async-start(bf16[16,16,1152]{2,1,0:T(8,128)(2,1)} %broadcast_in_dim.153), calls=%async_computation.9 | async-start | bytes 1179648 | tf_op jit(solution)/shard_map/all_to_all | solution.py:1119
  540.2 37.3 %all-to-all-start.10 = ((bf16[16,176,384]{2,1,0:T(8,128)(2,1)}), bf16[16,176,384]{2,1,0:T(8,128)(2,1)}, u32[]{:S(2)}, u32[]{:S(2)}) async-start(bf16[16,176,384]{2,1,0:T(8,128)(2,1)} %pad_maximum_fusion.1), calls=%async_computation.11 | async-start | bytes 4325376 | tf_op jit(solution)/shard_map/all_to_all | solution.py:1160
  (172 other events, 1479.1 us)
Sparse Core Ops, SparseCore 0:
  15.4 79.5 all-gather.6
  103.9 94.8 all-gather.8
  231.6 50.6 all-gather.10
  408.6 103.6 reduce-scatter.1

commit v5 on v4

--- a/solution.py
+++ b/solution.py
@@ -172,6 +172,45 @@
         compiler_params=pltpu.CompilerParams(vmem_limit_bytes=FF_VMEM),
         name="ffn_forward",
     )(own, rows, *weights)
+
+
+def ffn_both_kernel(own_ref, n_ref, dm_ref, *refs):
+    mine, other = refs[:N_Z], refs[N_Z : 2 * N_Z]
+    part_ref, hid_ref, d_part_ref, dgu_ref, w_ref, sems = refs[2 * N_Z :]
+    copies = ffn_copies(own_ref, mine, other, w_ref, sems)
+    for z in range(0, N_Z, 2):
+        copies[z].wait()
+        copies[z + 1].wait()
+        d_hidden = dot(dm_ref[...], down_pair(w_ref, z))
+        for k in range(2):
+            gu = dot(n_ref[...], w_ref[z + k, :, : 2 * LANES])
+            gate, up = gu[:, :LANES], gu[:, LANES:]
+            s = jax.nn.sigmoid(gate)
+            hid_ref[:, LANES * (z + k) : LANES * (z + k + 1)] = (gate * s * up).astype(BF16)
+            d_h = d_hidden[:, LANES * k : LANES * (k + 1)]
+            at = 2 * LANES * (z + k)
+            dgu_ref[:, at : at + LANES] = (d_h * up * (s + gate * s * (1.0 - s))).astype(BF16)
+            dgu_ref[:, at + LANES : at + 2 * LANES] = (d_h * (gate * s)).astype(BF16)
+    out = None
+    for z in range(N_Z):
+        term = dot_nt(dgu_ref[:, 2 * LANES * z : 2 * LANES * (z + 1)], w_ref[z, :, : 2 * LANES])
+        out = term if z == 0 else out + term
+    d_part_ref[...] = out.astype(BF16)
+    out = dot_nt(hid_ref[:, : 2 * LANES], down_pair(w_ref, 0))
+    part_ref[...] = (out + dot_nt(hid_ref[:, 2 * LANES :], down_pair(w_ref, 2))).astype(BF16)
+
+
+def ffn_both(own, rows, d_rows, weights):
+    widths = (D, LANES * N_Z, D, 2 * LANES * N_Z)
+    return pl.pallas_call(
+        ffn_both_kernel,
+        out_shape=tuple(jax.ShapeDtypeStruct((TOKENS, w), BF16) for w in widths),
+        in_specs=ffn_specs(2),
+        out_specs=(pl.BlockSpec(memory_space=pltpu.VMEM),) * 4,
+        scratch_shapes=FF_SCRATCH,
+        compiler_params=pltpu.CompilerParams(vmem_limit_bytes=FF_VMEM),
+        name="ffn_both",
+    )(own, rows, d_rows, *weights)
 
 
 HALF_ROWS = SLICE // 2
@@ -1063,13 +1102,13 @@
     x_own = out_one.astype(F32)
     normed, latent = latents(rows_one, gains_two["attn"], attn_two)
     middle, saved = attention_forward(normed, latent, x_own, attn_two, gains_two, tab)
-    part_two, saved_two, _ = layer_forward(own_two, x_own, middle, saved, gains_two, ffn_weights)
+    rows_ffn = gather_dp(norm(middle, gains_two["ffn"]).astype(BF16))
+    part_two, hidden, part, d_gu = ffn_both(own_two, rows_ffn, d_rows_two, ffn_weights)
+    saved_two = (x_own, middle, rows_ffn, None, hidden) + saved
 
     mixed_one = lax.all_gather(saved_one[-1][5], "dp")
 
-    ffn_rows, gu, hidden = saved_two[2:5]
-    part, d_gu = ffn_backward(own_two, d_rows_two, gu, ffn_weights)
-    grads_two = ffn_gradients(own_two, d_rows_two, ffn_rows, d_gu, hidden)
+    grads_two = ffn_gradients(own_two, d_rows_two, rows_ffn, d_gu, hidden)
     d_normed_two = scatter_dp(part)
     d_normed_two, mixed_one, normed_one = tie((d_normed_two, mixed_one, normed_one))
     ring_two = ring_pairs(grads_two)

time: 606 us -> 600 us (0.990)
  waiting for transfers between devices: 183 us -> 191 us
  starting transfers between devices: 158 us -> 151 us
  Pallas kernels: 98.5 us -> 92 us
    pallas_call x0 -> x1, Pallas kernels: none -> 10.1 us  [ffn_both(): pl.pallas_call(ffn_both_kernel, out_shape=tuple((jax.ShapeDtypeStruct((TO...]
    pallas_call x2 -> x1, Pallas kernels: 16.7 us -> 8.34 us  [ffn_backward(): pl.pallas_call(ffn_backward_kernel, out_shape=(jax.ShapeDtypeStruct((TOKE...]
    pallas_call x2 -> x1, Pallas kernels: 16.3 us -> 8.15 us  [ffn_forward(): pl.pallas_call(ffn_forward_kernel, out_shape=(jax.ShapeDtypeStruct((TOKEN...]
  transfers between devices with their start and end apart: 93 -> 93, of which waited for: 39 -> 40; matrix products, arithmetic and copies ran while one was open for 15% -> 15% of each run, Pallas kernels for 14% -> 13%
where the time goes in v5:
time: 600 us; the launch traced here: 590 us
  waiting for transfers between devices  191 us (32%)
  starting transfers between devices  151 us (25%)
  Pallas kernels  92 us (15%)
  other arithmetic  74.7 us (12%)
  blocking collectives  32.9 us (5%)
  local copies, waits for them, and re-layouts  31.9 us (5%)
  between operations  16.4 us (3%)
    ppermute x36, starting transfers between devices, z_hop(): return lax.ppermute(x, 'tensor', [(i, (i + by) % N_Z) for i in range(N_Z)])  43.2 us
    ppermute x9, waiting for transfers between devices, ring_hop(): return lax.ppermute(x, ('section', 'tensor'), pairs)  43 us
    ppermute x36, waiting for transfers between devices, z_hop(): return lax.ppermute(x, 'tensor', [(i, (i + by) % N_Z) for i in range(N_Z)])  38 us
    all_to_all x2, waiting for transfers between devices, body(): blocks = lax.all_to_all(blocks, 'dp', 0, 0)  37.6 us
    ppermute x30, starting transfers between devices, to_core(): return lax.ppermute(x, 'section', [(0, 1), (1, 0)])  34 us
    all_to_all x1, blocking collectives, scatter_dp(): pieces = lax.all_to_all(part.reshape(N_DP, SHARD, D), 'dp', 0, 0)  32.9 us
    all_to_all x3, waiting for transfers between devices, gather_dp(): lax.all_to_all(copies, 'dp', 0, 0).reshape(N_DP * x.shape[0], x.shape[1])  30.6 us
    convert_element_type x10, other arithmetic, add(): return sum((x.astype(F32) for x in terms)).astype(BF16)  20.6 us
  transfers between devices with their start and end apart: 93, of which 40 were waited for; matrix products, arithmetic and copies ran while one was open for 15% of the time, Pallas kernels for 13%

profile of v5, /device:TPU:1, one launch (start us, length us, event | category | flops | bytes accessed | tf_op | source)
XLA Modules:
  0.0 589.8 jit_solution(1227994993719196187)
XLA Ops:
  15.3 6.8 %all-to-all-start = ((bf16[16,160,384]{2,1,0:T(8,128)(2,1)}), bf16[16,160,384]{2,1,0:T(8,128)(2,1)S(1)}, u32[]{:S(2)}, u32[]{:S(2)}) async-start(bf16[16,160,384]{2,1,0:T(8,128)(2,1)} %ffn_pack.1), calls=%async_computation | async-start | bytes 3932160 | tf_op jit(solution)/shard_map/all_to_all | solution.py:1056
  23.4 31.1 %all-to-all-done = bf16[16,160,384]{2,1,0:T(8,128)(2,1)S(1)} async-done(((bf16[16,160,384]{2,1,0:T(8,128)(2,1)}), bf16[16,160,384]{2,1,0:T(8,128)(2,1)S(1)}, u32[]{:S(2)}, u32[]{:S(2)}) %all-to-all-start) | async-done | bytes 1966112 | tf_op jit(solution)/shard_map/all_to_all | solution.py:1056
  61.5 33.5 %collective-permute-done.2.refs_2_ = bf16[2560,384]{1,0:T(8,128)(2,1)S(1)} collective-permute-done((bf16[2560,384]{1,0:T(8,128)(2,1)S(1)}, bf16[2560,384]{1,0:T(8,128)(2,1)S(1)}, u32[]{:S(2)}, u32[]{:S(2)}) %collective-permute-start.2) | collective-permute-done | bytes 1966112 | tf_op jit(solution)/shard_map/ppermute | solution.py:953
  133.2 16.3 %all-to-all-done.1 = bf16[16,16,2560]{2,1,0:T(8,128)(2,1)} async-done(((bf16[16,16,2560]{2,1,0:T(8,128)(2,1)}), bf16[16,16,2560]{2,1,0:T(8,128)(2,1)}, u32[]{:S(2)}, u32[]{:S(2)}) %all-to-all-start.1) | async-done | bytes 1310752 | tf_op jit(solution)/shard_map/all_to_all | solution.py:92
  149.5 6.4 %collective-permute-start.12 = (bf16[2560,384]{1,0:T(8,128)(2,1)}, bf16[2560,384]{1,0:T(8,128)(2,1)}, u32[]{:S(2)}, u32[]{:S(2)}) collective-permute-start(bf16[2560,384]{1,0:T(8,128)(2,1)} %collective-permute-done.8.refs_3_), channel_id=1, source_target_pairs={{0,64},{64,0},{1,65},{65,1},{2,66},{66,2},{3,67},{67,3},{4,68},{68... | collective-permute-start | bytes 5898248 | tf_op jit(solution)/shard_map/ppermute | solution.py:45
  159.8 8.1 %ffn_forward.1 = (bf16[256,2560]{1,0:T(8,128)(2,1)}, f32[256,1024]{1,0:T(8,128)}, bf16[256,512]{1,0:T(8,128)(2,1)}) custom-call(s32[2]{0:T(128)} %pad_add_fusion.own_ref, bf16[256,2560]{1,0:T(8,128)(2,1)} %bitcast.24.n_ref, bf16[2560,384]{1,0:T(8,128)(2,1)} %bitcast.146, bf16[2560,384]{1,0:T(8,128)(2,1)} %collective-permute-done.1.refs_1_, ...), custom_call_target="tpu_custom_call" | custom-call | tf_op jit(solution)/shard_map/ffn_forward/pallas_call | solution.py:162
  168.0 32.9 %all_to_all.55 = bf16[16,16,2560]{2,1,0:T(8,128)(2,1)S(1)} all-to-all(bf16[16,16,2560]{2,1,0:T(8,128)(2,1)} %bitcast.159), channel_id=1, replica_groups=mesh['section'=2,'tensor'=4,'dp'=16] {'dp'}, dimensions={0} | all-to-all | bytes 2621440 | tf_op jit(solution)/shard_map/all_to_all | solution.py:96
  247.1 14.3 %all-to-all-done.3 = bf16[16,16,2560]{2,1,0:T(8,128)(2,1)S(1)} async-done(((bf16[16,16,2560]{2,1,0:T(8,128)(2,1)}), bf16[16,16,2560]{2,1,0:T(8,128)(2,1)S(1)}, u32[]{:S(2)}, u32[]{:S(2)}) %all-to-all-start.3) | async-done | bytes 1310752 | tf_op jit(solution)/shard_map/all_to_all | solution.py:92
  262.4 10.1 %ffn_both.1 = (bf16[256,2560]{1,0:T(8,128)(2,1)}, bf16[256,512]{1,0:T(8,128)(2,1)}, bf16[256,2560]{1,0:T(8,128)(2,1)}, bf16[256,1024]{1,0:T(8,128)(2,1)}) custom-call(s32[2]{0:T(128)} %pad_add_fusion.1.own_ref, bf16[256,2560]{1,0:T(8,128)(2,1)} %bitcast.152, bf16[256,2560]{1,0:T(8,128)(2,1)} %bitcast.150, bf16[2560,384]{1,0:T(8,128)(2,1)} %bitcast.147, ...), custom_call_target="tpu_custom_call" | custom-call | tf_op jit(solution)/shard_map/ffn_both/pallas_call | solution.py:205
  283.5 14.6 %all-to-all-done.4 = bf16[16,16,2560]{2,1,0:T(8,128)(2,1)S(1)} async-done(((bf16[16,16,2560]{2,1,0:T(8,128)(2,1)}), bf16[16,16,2560]{2,1,0:T(8,128)(2,1)S(1)}, u32[]{:S(2)}, u32[]{:S(2)}) %all-to-all-start.4) | async-done | bytes 1310752 | tf_op jit(solution)/shard_map/all_to_all | solution.py:96
  318.8 6.1 %attend_back.2 = (bf16[128,1152]{1,0:T(8,128)(2,1)S(1)}, bf16[128,640]{1,0:T(8,128)(2,1)S(1)}, bf16[128,640]{1,0:T(8,128)(2,1)S(1)}) custom-call(bf16[64,2560]{1,0:T(8,128)(2,1)S(1)} %pad_maximum_fusion.8.mine_ref, bf16[64,2560]{1,0:T(8,128)(2,1)S(1)} %collective-permute-done.25.other_ref, f32[4,128,128]{2,1,0:T(8,128)S(1)} %pad_maximum_fusion.11.tab_ref.tab_hbm, ...), custom_call_target="tpu_custom_call" | custom-call | tf_op jit(solution)/shard_map/attend_back/pallas_call | solution.py:562
  325.5 6.3 %ffn_gradients.2 = (bf16[16,80,384]{2,1,0:T(8,128)(2,1)}, bf16[16,80,384]{2,1,0:T(8,128)(2,1)}, bf16[16,80,384]{2,1,0:T(8,128)(2,1)}, bf16[16,80,384]{2,1,0:T(8,...) custom-call(s32[2]{0:T(128)} %pad_add_fusion.1.own_ref, ...), custom_call_target="tpu_custom_call" | custom-call | flops 2013265920 | bytes 16777216 | tf_op jit(solution)/shard_map/ffn_gradients/pallas_call | solution.py:302
  359.1 5.4 all-to-all-start.6
  383.5 8.3 %ffn_backward.1 = (bf16[256,2560]{1,0:T(8,128)(2,1)}, bf16[256,1024]{1,0:T(8,128)(2,1)}) custom-call(s32[2]{0:T(128)} %pad_add_fusion.own_ref, bf16[256,2560]{1,0:T(8,128)(2,1)} %bitcast.36.dm_ref, f32[256,1024]{1,0:T(8,128)} %get-tuple-element.190.gu_ref, bf16[2560,384]{1,0:T(8,128)(2,1)} %bitcast.148, bf16[2560,384]{1,0:T(8,128)(2,1)} %collective-permute-done.1.refs_1_, ...), custom_call_target="tpu_custom_call" | custom-call | tf_op jit(solution)/shard_map/ffn_backward/pallas_call | solution.py:243
  391.9 6.8 %all-to-all-start.7 = ((bf16[16,16,2560]{2,1,0:T(8,128)(2,1)}), bf16[16,16,2560]{2,1,0:T(8,128)(2,1)S(1)}, u32[]{:S(2)}, u32[]{:S(2)}) async-start(bf16[16,16,2560]{2,1,0:T(8,128)(2,1)} %bitcast.158), calls=%async_computation.7 | async-start | bytes 2621440 | tf_op jit(solution)/shard_map/all_to_all | solution.py:96
  411.3 6.5 %ffn_gradients.3 = (bf16[16,80,384]{2,1,0:T(8,128)(2,1)}, bf16[16,80,384]{2,1,0:T(8,128)(2,1)}, bf16[16,80,384]{2,1,0:T(8,128)(2,1)}, bf16[16,80,384]{2,1,0:T(8,...) custom-call(s32[2]{0:T(128)} %pad_add_fusion.own_ref, ...), custom_call_target="tpu_custom_call" | custom-call | flops 2013265920 | bytes 16777216 | tf_op jit(solution)/shard_map/ffn_gradients/pallas_call | solution.py:302
  432.8 6.2 %attend_back.3 = (bf16[128,1152]{1,0:T(8,128)(2,1)S(1)}, bf16[128,640]{1,0:T(8,128)(2,1)S(1)}, bf16[128,640]{1,0:T(8,128)(2,1)S(1)}) custom-call(bf16[64,2560]{1,0:T(8,128)(2,1)S(1)} %pad_maximum_fusion.10.mine_ref, bf16[64,2560]{1,0:T(8,128)(2,1)S(1)} %collective-permute-done.49.other_ref, f32[4,128,128]{2,1,0:T(8,128)S(1)} %pad_maximum_fusion.11.tab_ref.tab_hbm, ...), custom_call_target="tpu_custom_call" | custom-call | tf_op jit(solution)/shard_map/attend_back/pallas_call | solution.py:562
  443.3 6.9 %all-to-all-start.8 = ((bf16[16,80,640]{2,1,0:T(8,128)(2,1)}), bf16[16,80,640]{2,1,0:T(8,128)(2,1)S(1)}, u32[]{:S(2)}, u32[]{:S(2)}) async-start(bf16[16,80,640]{2,1,0:T(8,128)(2,1)} %low_gradients.1), calls=%async_computation.8 | async-start | bytes 3276800 | tf_op jit(solution)/shard_map/all_to_all | solution.py:1149
  465.8 13.4 %all-to-all-done.8 = bf16[16,80,640]{2,1,0:T(8,128)(2,1)S(1)} async-done(((bf16[16,80,640]{2,1,0:T(8,128)(2,1)}), bf16[16,80,640]{2,1,0:T(8,128)(2,1)S(1)}, u32[]{:S(2)}, u32[]{:S(2)}) %all-to-all-start.8) | async-done | bytes 1638432 | tf_op jit(solution)/shard_map/all_to_all | solution.py:1149
  524.6 6.7 %collective-permute-done.61 = bf16[16,80,384]{2,1,0:T(8,128)(2,1)} collective-permute-done((bf16[16,80,384]{2,1,0:T(8,128)(2,1)}, bf16[16,80,384]{2,1,0:T(8,128)(2,1)}, u32[]{:S(2)}, u32[]{:S(2)}) %collective-permute-start.61) | collective-permute-done | bytes 983072 | tf_op jit(solution)/shard_map/ppermute | solution.py:953
  535.5 6.7 %all-to-all-start.10 = ((bf16[16,176,384]{2,1,0:T(8,128)(2,1)}), bf16[16,176,384]{2,1,0:T(8,128)(2,1)}, u32[]{:S(2)}, u32[]{:S(2)}) async-start(bf16[16,176,384]{2,1,0:T(8,128)(2,1)} %pad_maximum_fusion.1), calls=%async_computation.11 | async-start | bytes 4325376 | tf_op jit(solution)/shard_map/all_to_all | solution.py:1199
  549.6 6.6 %collective-permute-done.77 = bf16[160,1152]{1,0:T(8,128)(2,1)S(1)} collective-permute-done((bf16[160,1152]{1,0:T(8,128)(2,1)S(1)}, bf16[160,1152]{1,0:T(8,128)(2,1)S(1)}, u32[]{:S(2)}, u32[]{:S(2)}) %collective-permute-start.77) | collective-permute-done | bytes 368672 | tf_op jit(solution)/shard_map/ppermute | solution.py:49
  556.2 8.3 %collective-permute-done.76 = bf16[160,1152]{1,0:T(8,128)(2,1)S(1)} collective-permute-done((bf16[160,1152]{1,0:T(8,128)(2,1)S(1)}, bf16[160,1152]{1,0:T(8,128)(2,1)S(1)}, u32[]{:S(2)}, u32[]{:S(2)}) %collective-permute-start.76) | collective-permute-done | bytes 368672 | tf_op jit(solution)/shard_map/ppermute | solution.py:49
  566.0 6.5 %all-to-all-done.10.blocks_ref = bf16[16,176,384]{2,1,0:T(8,128)(2,1)} async-done(((bf16[16,176,384]{2,1,0:T(8,128)(2,1)}), bf16[16,176,384]{2,1,0:T(8,128)(2,1)}, u32[]{:S(2)}, u32[]{:S(2)}) %all-to-all-start.10) | async-done | bytes 2162720 | tf_op jit(solution)/shard_map/all_to_all | solution.py:1199
  (599 shorter events, 298.6 us)
Async XLA Ops:
  7.3 91.9 %all-gather.7.cloned.1.call-start = ((), (), s32[]{:S(2)}) async-start(), calls=%async_computation.13 | async-start | bytes 6823936 | tf_op jit(solution)/shard_map/all_gather | solution.py:1054
  15.3 39.1 %all-to-all-start = ((bf16[16,160,384]{2,1,0:T(8,128)(2,1)}), bf16[16,160,384]{2,1,0:T(8,128)(2,1)S(1)}, u32[]{:S(2)}, u32[]{:S(2)}) async-start(bf16[16,160,384]{2,1,0:T(8,128)(2,1)} %ffn_pack.1), calls=%async_computation | async-start | bytes 3932160 | tf_op jit(solution)/shard_map/all_to_all | solution.py:1056
  22.2 190.0 %all-gather.9.cloned.1.call-start = ((), (), s32[]{:S(2)}) async-start(), calls=%async_computation.14 | async-start | bytes 9748480 | tf_op jit(solution)/shard_map/all_gather | solution.py:1086
  54.5 40.5 %collective-permute-start.2 = (bf16[2560,384]{1,0:T(8,128)(2,1)S(1)}, bf16[2560,384]{1,0:T(8,128)(2,1)S(1)}, u32[]{:S(2)}, u32[]{:S(2)}) collective-permute-start(bf16[2560,384]{1,0:T(8,128)(2,1)S(1)} %bitcast.144), channel_id=1, source_target_pairs={{0,48},{16,0},{32,16},{48,32},{64,80},{80,96},{96,112},{112,64},{1... | collective-permute-start | bytes 5898248 | tf_op jit(solution)/shard_map/ppermute | solution.py:953
  56.2 43.0 %collective-permute-start.1 = (bf16[2560,384]{1,0:T(8,128)(2,1)S(1)}, bf16[2560,384]{1,0:T(8,128)(2,1)}, u32[]{:S(2)}, u32[]{:S(2)}) collective-permute-start(bf16[2560,384]{1,0:T(8,128)(2,1)S(1)} %bitcast.145), channel_id=1, source_target_pairs={{0,16},{16,32},{32,48},{48,0},{64,112},{80,64},{96,80},{112,96},{1... | collective-permute-start | bytes 5898248 | tf_op jit(solution)/shard_map/ppermute | solution.py:953
  120.0 29.5 %collective-permute-start.8 = (bf16[2560,384]{1,0:T(8,128)(2,1)}, bf16[2560,384]{1,0:T(8,128)(2,1)}, u32[]{:S(2)}, u32[]{:S(2)}) collective-permute-start(bf16[2560,384]{1,0:T(8,128)(2,1)} %collective-permute-done.1.refs_1_), channel_id=1, source_target_pairs={{0,16},{16,32},{32,48},{48,0},{64,112},{80,64},{96,80},{112,96},{1... | collective-permute-start | bytes 5898248 | tf_op jit(solution)/shard_map/ppermute | solution.py:953
  130.8 168.1 %all-gather.11.cloned.1.call-start = ((), (), s32[]{:S(2)}) async-start(), calls=%async_computation.15 | async-start | bytes 1671168 | tf_op jit(solution)/shard_map/all_gather | solution.py:1109
  130.9 25.6 %collective-permute-start.9 = (bf16[2560,384]{1,0:T(8,128)(2,1)S(1)}, bf16[2560,384]{1,0:T(8,128)(2,1)}, u32[]{:S(2)}, u32[]{:S(2)}) collective-permute-start(bf16[2560,384]{1,0:T(8,128)(2,1)S(1)} %bitcast.149), channel_id=1, source_target_pairs={{0,64},{64,0},{1,65},{65,1},{2,66},{66,2},{3,67},{67,3},{4,68},{68... | collective-permute-start | bytes 5898248 | tf_op jit(solution)/shard_map/ppermute | solution.py:45
  272.6 25.5 %all-to-all-start.4 = ((bf16[16,16,2560]{2,1,0:T(8,128)(2,1)}), bf16[16,16,2560]{2,1,0:T(8,128)(2,1)S(1)}, u32[]{:S(2)}, u32[]{:S(2)}) async-start(bf16[16,16,2560]{2,1,0:T(8,128)(2,1)} %bitcast.157), calls=%async_computation.4 | async-start | bytes 2621440 | tf_op jit(solution)/shard_map/all_to_all | solution.py:96
  313.1 25.6 %all-to-all-start.5 = ((bf16[16,16,2560]{2,1,0:T(8,128)(2,1)}), bf16[16,16,2560]{2,1,0:T(8,128)(2,1)}, u32[]{:S(2)}, u32[]{:S(2)}) async-start(bf16[16,16,2560]{2,1,0:T(8,128)(2,1)} %bitcast.156), calls=%async_computation.5 | async-start | bytes 2621440 | tf_op jit(solution)/shard_map/all_to_all | solution.py:96
  372.9 45.0 %collective-permute-start.39 = (bf16[16,80,384]{2,1,0:T(8,128)(2,1)}, bf16[16,80,384]{2,1,0:T(8,128)(2,1)}, u32[]{:S(2)}, u32[]{:S(2)}) collective-permute-start(bf16[16,80,384]{2,1,0:T(8,128)(2,1)} %add_convert_fusion.6), channel_id=1, source_target_pairs={{0,16},{16,32},{32,48},{48,0},{64,112},{80,64},{96,80},{112,96},{1... | collective-permute-start | bytes 2949128 | tf_op jit(solution)/shard_map/ppermute | solution.py:953
  383.5 34.3 %collective-permute-start.41 = (bf16[16,80,384]{2,1,0:T(8,128)(2,1)}, bf16[16,80,384]{2,1,0:T(8,128)(2,1)}, u32[]{:S(2)}, u32[]{:S(2)}) collective-permute-start(bf16[16,80,384]{2,1,0:T(8,128)(2,1)} %add_convert_fusion.5), channel_id=1, source_target_pairs={{0,48},{16,0},{32,16},{48,32},{64,80},{80,96},{96,112},{112,64},{1... | collective-permute-start | bytes 2949128 | tf_op jit(solution)/shard_map/ppermute | solution.py:953
  391.9 28.9 %all-to-all-start.7 = ((bf16[16,16,2560]{2,1,0:T(8,128)(2,1)}), bf16[16,16,2560]{2,1,0:T(8,128)(2,1)S(1)}, u32[]{:S(2)}, u32[]{:S(2)}) async-start(bf16[16,16,2560]{2,1,0:T(8,128)(2,1)} %bitcast.158), calls=%async_computation.7 | async-start | bytes 2621440 | tf_op jit(solution)/shard_map/all_to_all | solution.py:96
  398.7 123.8 %reduce-scatter.2.cloned.1.call-start = ((), (), s32[]{:S(2)}) async-start(), calls=%async_computation.12 | async-start | bytes 7938048 | tf_op jit(solution)/shard_map/reduce_scatter | solution.py:1134
  426.2 31.9 %collective-permute-start.55 = (bf16[16,80,384]{2,1,0:T(8,128)(2,1)}, bf16[16,80,384]{2,1,0:T(8,128)(2,1)}, u32[]{:S(2)}, u32[]{:S(2)}) collective-permute-start(bf16[16,80,384]{2,1,0:T(8,128)(2,1)} %get-tuple-element.222), channel_id=1, source_target_pairs={{0,64},{64,0},{1,65},{65,1},{2,66},{66,2},{3,67},{67,3},{4,68},{68... | collective-permute-start | bytes 2949128 | tf_op jit(solution)/shard_map/ppermute | solution.py:45
  426.9 33.8 %collective-permute-start.57 = (bf16[16,80,384]{2,1,0:T(8,128)(2,1)}, bf16[16,80,384]{2,1,0:T(8,128)(2,1)}, u32[]{:S(2)}, u32[]{:S(2)}) collective-permute-start(bf16[16,80,384]{2,1,0:T(8,128)(2,1)} %get-tuple-element.224), channel_id=1, source_target_pairs={{0,64},{64,0},{1,65},{65,1},{2,66},{66,2},{3,67},{67,3},{4,68},{68... | collective-permute-start | bytes 2949128 | tf_op jit(solution)/shard_map/ppermute | solution.py:45
  443.3 35.8 %all-to-all-start.8 = ((bf16[16,80,640]{2,1,0:T(8,128)(2,1)}), bf16[16,80,640]{2,1,0:T(8,128)(2,1)S(1)}, u32[]{:S(2)}, u32[]{:S(2)}) async-start(bf16[16,80,640]{2,1,0:T(8,128)(2,1)} %low_gradients.1), calls=%async_computation.8 | async-start | bytes 3276800 | tf_op jit(solution)/shard_map/all_to_all | solution.py:1149
  455.5 28.7 %collective-permute-start.59 = (bf16[16,80,384]{2,1,0:T(8,128)(2,1)}, bf16[16,80,384]{2,1,0:T(8,128)(2,1)}, u32[]{:S(2)}, u32[]{:S(2)}) collective-permute-start(bf16[16,80,384]{2,1,0:T(8,128)(2,1)} %get-tuple-element.226), channel_id=1, source_target_pairs={{0,64},{64,0},{1,65},{65,1},{2,66},{66,2},{3,67},{67,3},{4,68},{68... | collective-permute-start | bytes 2949128 | tf_op jit(solution)/shard_map/ppermute | solution.py:45
  456.1 31.2 %collective-permute-start.60 = (bf16[16,80,384]{2,1,0:T(8,128)(2,1)}, bf16[16,80,384]{2,1,0:T(8,128)(2,1)}, u32[]{:S(2)}, u32[]{:S(2)}) collective-permute-start(bf16[16,80,384]{2,1,0:T(8,128)(2,1)} %get-tuple-element.228), channel_id=1, source_target_pairs={{0,64},{64,0},{1,65},{65,1},{2,66},{66,2},{3,67},{67,3},{4,68},{68... | collective-permute-start | bytes 2949128 | tf_op jit(solution)/shard_map/ppermute | solution.py:45
  460.6 28.1 %collective-permute-start.56 = (bf16[16,80,384]{2,1,0:T(8,128)(2,1)}, bf16[16,80,384]{2,1,0:T(8,128)(2,1)}, u32[]{:S(2)}, u32[]{:S(2)}) collective-permute-start(bf16[16,80,384]{2,1,0:T(8,128)(2,1)} %add_convert_fusion.3), channel_id=1, source_target_pairs={{0,48},{16,0},{32,16},{48,32},{64,80},{80,96},{96,112},{112,64},{1... | collective-permute-start | bytes 2949128 | tf_op jit(solution)/shard_map/ppermute | solution.py:953
  463.1 25.5 %collective-permute-start.58 = (bf16[16,80,384]{2,1,0:T(8,128)(2,1)}, bf16[16,80,384]{2,1,0:T(8,128)(2,1)}, u32[]{:S(2)}, u32[]{:S(2)}) collective-permute-start(bf16[16,80,384]{2,1,0:T(8,128)(2,1)} %add_convert_fusion.2), channel_id=1, source_target_pairs={{0,16},{16,32},{32,48},{48,0},{64,112},{80,64},{96,80},{112,96},{1... | collective-permute-start | bytes 2949128 | tf_op jit(solution)/shard_map/ppermute | solution.py:953
  493.5 40.3 %collective-permute-start.67 = (f32[64,640]{1,0:T(8,128)S(1)}, f32[64,640]{1,0:T(8,128)S(1)}, u32[]{:S(2)}, u32[]{:S(2)}) collective-permute-start(f32[64,640]{1,0:T(8,128)S(1)} %convert_reduce_fusion.low_ref), channel_id=1, source_target_pairs={{64,0},{65,1},{66,2},{67,3},{68,4},{69,5},{70,6},{71,7},{72,8},{73... | collective-permute-start | bytes 491528 | tf_op jit(solution)/shard_map/ppermute | solution.py:1180
  496.3 28.0 %all-to-all-start.9 = ((bf16[16,16,1152]{2,1,0:T(8,128)(2,1)}), bf16[16,16,1152]{2,1,0:T(8,128)(2,1)S(1)}, u32[]{:S(2)}, u32[]{:S(2)}) async-start(bf16[16,16,1152]{2,1,0:T(8,128)(2,1)} %broadcast_in_dim.153), calls=%async_computation.9 | async-start | bytes 1179648 | tf_op jit(solution)/shard_map/all_to_all | solution.py:1158
  535.5 37.0 %all-to-all-start.10 = ((bf16[16,176,384]{2,1,0:T(8,128)(2,1)}), bf16[16,176,384]{2,1,0:T(8,128)(2,1)}, u32[]{:S(2)}, u32[]{:S(2)}) async-start(bf16[16,176,384]{2,1,0:T(8,128)(2,1)} %pad_maximum_fusion.1), calls=%async_computation.11 | async-start | bytes 4325376 | tf_op jit(solution)/shard_map/all_to_all | solution.py:1199
  (172 other events, 1470.8 us)
Sparse Core Ops, SparseCore 0:
  15.4 79.5 all-gather.6
  103.9 94.8 all-gather.8
  231.7 50.8 all-gather.10
  403.4 104.1 reduce-scatter.1

commit v6 on v5

--- a/solution.py
+++ b/solution.py
@@ -92,9 +92,12 @@
     return lax.all_to_all(copies, "dp", 0, 0).reshape(N_DP * x.shape[0], x.shape[1])
 
 
+def swap_dp(part):
+    return lax.all_to_all(part.reshape(N_DP, SHARD, D), "dp", 0, 0)
+
+
 def scatter_dp(part):
-    pieces = lax.all_to_all(part.reshape(N_DP, SHARD, D), "dp", 0, 0)
-    return jnp.sum(pieces.astype(F32), axis=0)
+    return jnp.sum(swap_dp(part).astype(F32), axis=0)
 
 
 def norm_scale(x):
@@ -1117,7 +1120,7 @@
     part, d_query, d_key_value = attend_back(d_attended, tab, saved_two[-1], attn_two)
     packs_two = attend_gradients(d_attended, saved_two[-1], d_query, d_key_value)
     in_grad_two, rows, _, dg_two, part_two, _ = attention_backward(
-        part, d_middle, saved_two, attn_two, gains_two, scatter_dp(part_two)
+        part, d_middle, saved_two, attn_two, gains_two, swap_dp(part_two)
     )
     attn, q, kv = dg_two
     dg_two = jnp.concatenate([attn, ffn_gain_two, q, kv])
@@ -1137,8 +1140,7 @@
     grads_one = ffn_gradients(own_one, d_rows, ffn_rows, d_gu, hidden)
     d_normed_two = scatter_dp(part)
     total_two = ring_last(ring_two)
-    rows_two = gather_tokens(layer_out_rows(part_two, saved_two))
-    d_normed_two, total_two, rows_two, grads_one = tie((d_normed_two, total_two, rows_two, grads_one))
+    d_normed_two, total_two, part_two, grads_one = tie((d_normed_two, total_two, part_two, grads_one))
     d_middle, ffn_gain_one = middle_backward(grad_one, d_normed_two, saved_one, gains_one)
     d_att_own = (RES_SCALE * d_middle).astype(BF16)
     columns = d_att_own.reshape(SHARD, N_DP, SLICE).transpose(1, 0, 2)
@@ -1148,8 +1150,10 @@
     part, low_one = tie((part, low_one))
     low_one = lax.all_to_all(low_one, "dp", 0, 0)
     first = ring_first(ring_pairs(grads_one))
-    in_grad_one, _, d_lat_own, dg_one, low_one, first = attention_backward(
-        part, d_middle, saved_one, attn_one, gains_one, low_one, first
+    part, part_two = tie((part, part_two))
+    rows_two = gather_tokens(layer_out_rows(jnp.sum(part_two.astype(F32), axis=0), saved_two))
+    in_grad_one, _, d_lat_own, dg_one, (low_one, rows_two), first = attention_backward(
+        part, d_middle, saved_one, attn_one, gains_one, (low_one, rows_two), first
     )
     d_lat = jnp.broadcast_to(d_lat_own.astype(BF16)[None], (N_DP, SHARD, LAT_ALL))
     columns = gather_tokens(low_one[:, LOW_ROWS:, :SLICE].reshape(TOKENS, SLICE))

time: 600 us -> 601 us (level)
  other arithmetic: 74.7 us -> 61.8 us
  starting transfers between devices: 151 us -> 159 us
    all_to_all x3, waiting for transfers between devices: 17.5 us -> 28.5 us  [swap_dp(): return lax.all_to_all(part.reshape(N_DP, SHARD, D), 'dp', 0, 0)]
    ppermute x30, starting transfers between devices: 34 us -> 41.3 us  [to_core(): return lax.ppermute(x, 'section', [(0, 1), (1, 0)])]
  transfers between devices with their start and end apart: 93 -> 93, of which waited for: 40 -> 39; matrix products, arithmetic and copies ran while one was open for 15% -> 13% of each run, Pallas kernels for 13% -> 11%
where the time goes in v6:
time: 601 us; the launch traced here: 591 us
  waiting for transfers between devices  196 us (33%)
  starting transfers between devices  159 us (26%)
  Pallas kernels  92.2 us (15%)
  other arithmetic  61.8 us (10%)
  blocking collectives  33 us (5%)
  local copies, waits for them, and re-layouts  32.5 us (5%)
  between operations  16.3 us (3%)
    ppermute x36, starting transfers between devices, z_hop(): return lax.ppermute(x, 'tensor', [(i, (i + by) % N_Z) for i in range(N_Z)])  48.1 us
    ppermute x9, waiting for transfers between devices, ring_hop(): return lax.ppermute(x, ('section', 'tensor'), pairs)  44 us
    ppermute x30, starting transfers between devices, to_core(): return lax.ppermute(x, 'section', [(0, 1), (1, 0)])  41.3 us
    all_to_all x2, waiting for transfers between devices, body(): blocks = lax.all_to_all(blocks, 'dp', 0, 0)  36.8 us
    ppermute x36, waiting for transfers between devices, z_hop(): return lax.ppermute(x, 'tensor', [(i, (i + by) % N_Z) for i in range(N_Z)])  35.2 us
    all_to_all x1, blocking collectives, swap_dp(): return lax.all_to_all(part.reshape(N_DP, SHARD, D), 'dp', 0, 0)  33 us
    all_to_all x3, waiting for transfers between devices, gather_dp(): lax.all_to_all(copies, 'dp', 0, 0).reshape(N_DP * x.shape[0], x.shape[1])  30.6 us
    all_to_all x3, waiting for transfers between devices, swap_dp(): return lax.all_to_all(part.reshape(N_DP, SHARD, D), 'dp', 0, 0)  28.5 us
  transfers between devices with their start and end apart: 93, of which 39 were waited for; matrix products, arithmetic and copies ran while one was open for 13% of the time, Pallas kernels for 11%

profile of v6, /device:TPU:1, one launch (start us, length us, event | category | flops | bytes accessed | tf_op | source)
XLA Modules:
  0.0 591.5 jit_solution(9759549622917810894)
XLA Ops:
  15.5 7.0 %all-to-all-start = ((bf16[16,160,384]{2,1,0:T(8,128)(2,1)}), bf16[16,160,384]{2,1,0:T(8,128)(2,1)S(1)}, u32[]{:S(2)}, u32[]{:S(2)}) async-start(bf16[16,160,384]{2,1,0:T(8,128)(2,1)} %ffn_pack.1), calls=%async_computation | async-start | bytes 3932160 | tf_op jit(solution)/shard_map/all_to_all | solution.py:1059
  23.7 31.1 %all-to-all-done = bf16[16,160,384]{2,1,0:T(8,128)(2,1)S(1)} async-done(((bf16[16,160,384]{2,1,0:T(8,128)(2,1)}), bf16[16,160,384]{2,1,0:T(8,128)(2,1)S(1)}, u32[]{:S(2)}, u32[]{:S(2)}) %all-to-all-start) | async-done | bytes 1966112 | tf_op jit(solution)/shard_map/all_to_all | solution.py:1059
  60.8 34.6 %collective-permute-done.2.refs_2_ = bf16[2560,384]{1,0:T(8,128)(2,1)S(1)} collective-permute-done((bf16[2560,384]{1,0:T(8,128)(2,1)S(1)}, bf16[2560,384]{1,0:T(8,128)(2,1)S(1)}, u32[]{:S(2)}, u32[]{:S(2)}) %collective-permute-start.2) | collective-permute-done | bytes 1966112 | tf_op jit(solution)/shard_map/ppermute | solution.py:956
  133.4 16.3 %all-to-all-done.1 = bf16[16,16,2560]{2,1,0:T(8,128)(2,1)} async-done(((bf16[16,16,2560]{2,1,0:T(8,128)(2,1)}), bf16[16,16,2560]{2,1,0:T(8,128)(2,1)}, u32[]{:S(2)}, u32[]{:S(2)}) %all-to-all-start.1) | async-done | bytes 1310752 | tf_op jit(solution)/shard_map/all_to_all | solution.py:92
  149.7 6.3 %collective-permute-start.12 = (bf16[2560,384]{1,0:T(8,128)(2,1)}, bf16[2560,384]{1,0:T(8,128)(2,1)}, u32[]{:S(2)}, u32[]{:S(2)}) collective-permute-start(bf16[2560,384]{1,0:T(8,128)(2,1)} %collective-permute-done.8.refs_3_), channel_id=1, source_target_pairs={{0,64},{64,0},{1,65},{65,1},{2,66},{66,2},{3,67},{67,3},{4,68},{68... | collective-permute-start | bytes 5898248 | tf_op jit(solution)/shard_map/ppermute | solution.py:45
  160.0 8.2 %ffn_forward.1 = (bf16[256,2560]{1,0:T(8,128)(2,1)}, f32[256,1024]{1,0:T(8,128)}, bf16[256,512]{1,0:T(8,128)(2,1)}) custom-call(s32[2]{0:T(128)} %pad_add_fusion.own_ref, bf16[256,2560]{1,0:T(8,128)(2,1)} %bitcast.24.n_ref, bf16[2560,384]{1,0:T(8,128)(2,1)} %bitcast.146, bf16[2560,384]{1,0:T(8,128)(2,1)} %collective-permute-done.1.refs_1_, ...), custom_call_target="tpu_custom_call" | custom-call | tf_op jit(solution)/shard_map/ffn_forward/pallas_call | solution.py:165
  168.2 33.0 %all_to_all.55 = bf16[16,16,2560]{2,1,0:T(8,128)(2,1)S(1)} all-to-all(bf16[16,16,2560]{2,1,0:T(8,128)(2,1)} %bitcast.159), channel_id=1, replica_groups=mesh['section'=2,'tensor'=4,'dp'=16] {'dp'}, dimensions={0} | all-to-all | bytes 2621440 | tf_op jit(solution)/shard_map/all_to_all | solution.py:96
  247.1 14.3 %all-to-all-done.3 = bf16[16,16,2560]{2,1,0:T(8,128)(2,1)S(1)} async-done(((bf16[16,16,2560]{2,1,0:T(8,128)(2,1)}), bf16[16,16,2560]{2,1,0:T(8,128)(2,1)S(1)}, u32[]{:S(2)}, u32[]{:S(2)}) %all-to-all-start.3) | async-done | bytes 1310752 | tf_op jit(solution)/shard_map/all_to_all | solution.py:92
  262.4 10.1 %ffn_both.1 = (bf16[256,2560]{1,0:T(8,128)(2,1)}, bf16[256,512]{1,0:T(8,128)(2,1)}, bf16[256,2560]{1,0:T(8,128)(2,1)}, bf16[256,1024]{1,0:T(8,128)(2,1)}) custom-call(s32[2]{0:T(128)} %pad_add_fusion.1.own_ref, bf16[256,2560]{1,0:T(8,128)(2,1)} %bitcast.152, bf16[256,2560]{1,0:T(8,128)(2,1)} %bitcast.150, bf16[2560,384]{1,0:T(8,128)(2,1)} %bitcast.147, ...), custom_call_target="tpu_custom_call" | custom-call | tf_op jit(solution)/shard_map/ffn_both/pallas_call | solution.py:208
  280.2 14.3 %all-to-all-done.4 = bf16[16,16,2560]{2,1,0:T(8,128)(2,1)} async-done(((bf16[16,16,2560]{2,1,0:T(8,128)(2,1)}), bf16[16,16,2560]{2,1,0:T(8,128)(2,1)}, u32[]{:S(2)}, u32[]{:S(2)}) %all-to-all-start.4) | async-done | bytes 1310752 | tf_op jit(solution)/shard_map/all_to_all | solution.py:96
  305.3 6.1 %collective-permute-start.25 = (bf16[64,2560]{1,0:T(8,128)(2,1)S(1)}, bf16[64,2560]{1,0:T(8,128)(2,1)S(1)}, u32[]{:S(2)}, u32[]{:S(2)}) collective-permute-start(bf16[64,2560]{1,0:T(8,128)(2,1)S(1)} %pad_maximum_fusion.8.mine_ref), channel_id=1, source_target_pairs={{0,64},{64,0},{1,65},{65,1},{2,66},{66,2},{3,67},{67,3},{4,68},{68... | collective-permute-start | bytes 983048 | tf_op jit(solution)/shard_map/ppermute | solution.py:45
  314.5 6.1 %attend_back.2 = (bf16[128,1152]{1,0:T(8,128)(2,1)S(1)}, bf16[128,640]{1,0:T(8,128)(2,1)S(1)}, bf16[128,640]{1,0:T(8,128)(2,1)S(1)}) custom-call(bf16[64,2560]{1,0:T(8,128)(2,1)S(1)} %pad_maximum_fusion.8.mine_ref, bf16[64,2560]{1,0:T(8,128)(2,1)S(1)} %collective-permute-done.25.other_ref, f32[4,128,128]{2,1,0:T(8,128)S(1)} %pad_maximum_fusion.11.tab_ref.tab_hbm, ...), custom_call_target="tpu_custom_call" | custom-call | tf_op jit(solution)/shard_map/attend_back/pallas_call | solution.py:565
  330.8 6.3 %ffn_gradients.2 = (bf16[16,80,384]{2,1,0:T(8,128)(2,1)}, bf16[16,80,384]{2,1,0:T(8,128)(2,1)}, bf16[16,80,384]{2,1,0:T(8,128)(2,1)}, bf16[16,80,384]{2,1,0:T(8,...) custom-call(s32[2]{0:T(128)} %pad_add_fusion.1.own_ref, ...), custom_call_target="tpu_custom_call" | custom-call | flops 2013265920 | bytes 16777216 | tf_op jit(solution)/shard_map/ffn_gradients/pallas_call | solution.py:305
  338.8 8.8 %all-to-all-done.5 = bf16[16,16,2560]{2,1,0:T(8,128)(2,1)} async-done(((bf16[16,16,2560]{2,1,0:T(8,128)(2,1)}), bf16[16,16,2560]{2,1,0:T(8,128)(2,1)}, u32[]{:S(2)}, u32[]{:S(2)}) %all-to-all-start.5) | async-done | bytes 1310752 | tf_op jit(solution)/shard_map/all_to_all | solution.py:96
  387.0 8.3 %ffn_backward.1 = (bf16[256,2560]{1,0:T(8,128)(2,1)}, bf16[256,1024]{1,0:T(8,128)(2,1)}) custom-call(s32[2]{0:T(128)} %pad_add_fusion.own_ref, bf16[256,2560]{1,0:T(8,128)(2,1)} %bitcast.36.dm_ref, f32[256,1024]{1,0:T(8,128)} %get-tuple-element.193.gu_ref, bf16[2560,384]{1,0:T(8,128)(2,1)} %bitcast.148, bf16[2560,384]{1,0:T(8,128)(2,1)} %collective-permute-done.1.refs_1_, ...), custom_call_target="tpu_custom_call" | custom-call | tf_op jit(solution)/shard_map/ffn_backward/pallas_call | solution.py:246
  395.4 6.7 %all-to-all-start.7 = ((bf16[16,16,2560]{2,1,0:T(8,128)(2,1)}), bf16[16,16,2560]{2,1,0:T(8,128)(2,1)S(1)}, u32[]{:S(2)}, u32[]{:S(2)}) async-start(bf16[16,16,2560]{2,1,0:T(8,128)(2,1)} %bitcast.157), calls=%async_computation.7 | async-start | bytes 2621440 | tf_op jit(solution)/shard_map/all_to_all | solution.py:96
  403.6 6.5 %ffn_gradients.3 = (bf16[16,80,384]{2,1,0:T(8,128)(2,1)}, bf16[16,80,384]{2,1,0:T(8,128)(2,1)}, bf16[16,80,384]{2,1,0:T(8,128)(2,1)}, bf16[16,80,384]{2,1,0:T(8,...) custom-call(s32[2]{0:T(128)} %pad_add_fusion.own_ref, ...), custom_call_target="tpu_custom_call" | custom-call | flops 2013265920 | bytes 16777216 | tf_op jit(solution)/shard_map/ffn_gradients/pallas_call | solution.py:305
  436.3 6.2 %attend_back.3 = (bf16[128,1152]{1,0:T(8,128)(2,1)S(1)}, bf16[128,640]{1,0:T(8,128)(2,1)S(1)}, bf16[128,640]{1,0:T(8,128)(2,1)S(1)}) custom-call(bf16[64,2560]{1,0:T(8,128)(2,1)S(1)} %pad_maximum_fusion.9.mine_ref, bf16[64,2560]{1,0:T(8,128)(2,1)S(1)} %collective-permute-done.45.other_ref, f32[4,128,128]{2,1,0:T(8,128)S(1)} %pad_maximum_fusion.11.tab_ref.tab_hbm, ...), custom_call_target="tpu_custom_call" | custom-call | tf_op jit(solution)/shard_map/attend_back/pallas_call | solution.py:565
  472.3 9.5 %all-to-all-done.8 = bf16[16,80,640]{2,1,0:T(8,128)(2,1)} async-done(((bf16[16,80,640]{2,1,0:T(8,128)(2,1)}), bf16[16,80,640]{2,1,0:T(8,128)(2,1)}, u32[]{:S(2)}, u32[]{:S(2)}) %all-to-all-start.8) | async-done | bytes 1638432 | tf_op jit(solution)/shard_map/all_to_all | solution.py:1151
  525.1 6.7 %collective-permute-done.61 = bf16[16,80,384]{2,1,0:T(8,128)(2,1)} collective-permute-done((bf16[16,80,384]{2,1,0:T(8,128)(2,1)}, bf16[16,80,384]{2,1,0:T(8,128)(2,1)}, u32[]{:S(2)}, u32[]{:S(2)}) %collective-permute-start.61) | collective-permute-done | bytes 983072 | tf_op jit(solution)/shard_map/ppermute | solution.py:956
  536.0 7.0 %all-to-all-start.10 = ((bf16[16,176,384]{2,1,0:T(8,128)(2,1)}), bf16[16,176,384]{2,1,0:T(8,128)(2,1)}, u32[]{:S(2)}, u32[]{:S(2)}) async-start(bf16[16,176,384]{2,1,0:T(8,128)(2,1)} %pad_maximum_fusion.1), calls=%async_computation.11 | async-start | bytes 4325376 | tf_op jit(solution)/shard_map/all_to_all | solution.py:1203
  550.9 6.7 %collective-permute-done.77 = bf16[160,1152]{1,0:T(8,128)(2,1)S(1)} collective-permute-done((bf16[160,1152]{1,0:T(8,128)(2,1)S(1)}, bf16[160,1152]{1,0:T(8,128)(2,1)S(1)}, u32[]{:S(2)}, u32[]{:S(2)}) %collective-permute-start.77) | collective-permute-done | bytes 368672 | tf_op jit(solution)/shard_map/ppermute | solution.py:49
  557.6 8.8 %collective-permute-done.76 = bf16[160,1152]{1,0:T(8,128)(2,1)S(1)} collective-permute-done((bf16[160,1152]{1,0:T(8,128)(2,1)S(1)}, bf16[160,1152]{1,0:T(8,128)(2,1)S(1)}, u32[]{:S(2)}, u32[]{:S(2)}) %collective-permute-start.76) | collective-permute-done | bytes 368672 | tf_op jit(solution)/shard_map/ppermute | solution.py:49
  567.7 5.7 all-to-all-done.10.blocks_ref
  (597 shorter events, 300.7 us)
Async XLA Ops:
  7.3 92.1 %all-gather.7.cloned.1.call-start = ((), (), s32[]{:S(2)}) async-start(), calls=%async_computation.13 | async-start | bytes 6823936 | tf_op jit(solution)/shard_map/all_gather | solution.py:1057
  15.5 39.3 %all-to-all-start = ((bf16[16,160,384]{2,1,0:T(8,128)(2,1)}), bf16[16,160,384]{2,1,0:T(8,128)(2,1)S(1)}, u32[]{:S(2)}, u32[]{:S(2)}) async-start(bf16[16,160,384]{2,1,0:T(8,128)(2,1)} %ffn_pack.1), calls=%async_computation | async-start | bytes 3932160 | tf_op jit(solution)/shard_map/all_to_all | solution.py:1059
  22.5 189.7 %all-gather.9.cloned.1.call-start = ((), (), s32[]{:S(2)}) async-start(), calls=%async_computation.14 | async-start | bytes 9748480 | tf_op jit(solution)/shard_map/all_gather | solution.py:1089
  54.8 40.5 %collective-permute-start.2 = (bf16[2560,384]{1,0:T(8,128)(2,1)S(1)}, bf16[2560,384]{1,0:T(8,128)(2,1)S(1)}, u32[]{:S(2)}, u32[]{:S(2)}) collective-permute-start(bf16[2560,384]{1,0:T(8,128)(2,1)S(1)} %bitcast.144), channel_id=1, source_target_pairs={{0,48},{16,0},{32,16},{48,32},{64,80},{80,96},{96,112},{112,64},{1... | collective-permute-start | bytes 5898248 | tf_op jit(solution)/shard_map/ppermute | solution.py:956
  56.4 43.0 %collective-permute-start.1 = (bf16[2560,384]{1,0:T(8,128)(2,1)S(1)}, bf16[2560,384]{1,0:T(8,128)(2,1)}, u32[]{:S(2)}, u32[]{:S(2)}) collective-permute-start(bf16[2560,384]{1,0:T(8,128)(2,1)S(1)} %bitcast.145), channel_id=1, source_target_pairs={{0,16},{16,32},{32,48},{48,0},{64,112},{80,64},{96,80},{112,96},{1... | collective-permute-start | bytes 5898248 | tf_op jit(solution)/shard_map/ppermute | solution.py:956
  120.3 29.4 %collective-permute-start.8 = (bf16[2560,384]{1,0:T(8,128)(2,1)}, bf16[2560,384]{1,0:T(8,128)(2,1)}, u32[]{:S(2)}, u32[]{:S(2)}) collective-permute-start(bf16[2560,384]{1,0:T(8,128)(2,1)} %collective-permute-done.1.refs_1_), channel_id=1, source_target_pairs={{0,16},{16,32},{32,48},{48,0},{64,112},{80,64},{96,80},{112,96},{1... | collective-permute-start | bytes 5898248 | tf_op jit(solution)/shard_map/ppermute | solution.py:956
  131.2 164.9 %all-gather.11.cloned.1.call-start = ((), (), s32[]{:S(2)}) async-start(), calls=%async_computation.15 | async-start | bytes 1671168 | tf_op jit(solution)/shard_map/all_gather | solution.py:1112
  131.2 25.5 %collective-permute-start.9 = (bf16[2560,384]{1,0:T(8,128)(2,1)S(1)}, bf16[2560,384]{1,0:T(8,128)(2,1)}, u32[]{:S(2)}, u32[]{:S(2)}) collective-permute-start(bf16[2560,384]{1,0:T(8,128)(2,1)S(1)} %bitcast.149), channel_id=1, source_target_pairs={{0,64},{64,0},{1,65},{65,1},{2,66},{66,2},{3,67},{67,3},{4,68},{68... | collective-permute-start | bytes 5898248 | tf_op jit(solution)/shard_map/ppermute | solution.py:45
  132.9 23.8 %collective-permute-start.10 = (bf16[2560,384]{1,0:T(8,128)(2,1)}, bf16[2560,384]{1,0:T(8,128)(2,1)}, u32[]{:S(2)}, u32[]{:S(2)}) collective-permute-start(bf16[2560,384]{1,0:T(8,128)(2,1)} %collective-permute-done.1.refs_1_), channel_id=1, source_target_pairs={{0,64},{64,0},{1,65},{65,1},{2,66},{66,2},{3,67},{67,3},{4,68},{68... | collective-permute-start | bytes 5898248 | tf_op jit(solution)/shard_map/ppermute | solution.py:45
  322.2 25.4 %all-to-all-start.5 = ((bf16[16,16,2560]{2,1,0:T(8,128)(2,1)}), bf16[16,16,2560]{2,1,0:T(8,128)(2,1)}, u32[]{:S(2)}, u32[]{:S(2)}) async-start(bf16[16,16,2560]{2,1,0:T(8,128)(2,1)} %bitcast.156), calls=%async_computation.5 | async-start | bytes 2621440 | tf_op jit(solution)/shard_map/all_to_all | solution.py:96
  360.5 26.5 %all-to-all-start.6 = ((bf16[16,16,2560]{2,1,0:T(8,128)(2,1)}), bf16[16,16,2560]{2,1,0:T(8,128)(2,1)}, u32[]{:S(2)}, u32[]{:S(2)}) async-start(bf16[16,16,2560]{2,1,0:T(8,128)(2,1)} %broadcast_in_dim.152), calls=%async_computation.6 | async-start | bytes 2621440 | tf_op jit(solution)/shard_map/all_to_all | solution.py:92
  374.6 35.5 %collective-permute-start.39 = (bf16[16,80,384]{2,1,0:T(8,128)(2,1)}, bf16[16,80,384]{2,1,0:T(8,128)(2,1)}, u32[]{:S(2)}, u32[]{:S(2)}) collective-permute-start(bf16[16,80,384]{2,1,0:T(8,128)(2,1)} %add_convert_fusion.6), channel_id=1, source_target_pairs={{0,16},{16,32},{32,48},{48,0},{64,112},{80,64},{96,80},{112,96},{1... | collective-permute-start | bytes 2949128 | tf_op jit(solution)/shard_map/ppermute | solution.py:956
  383.4 26.8 %collective-permute-start.41 = (bf16[16,80,384]{2,1,0:T(8,128)(2,1)}, bf16[16,80,384]{2,1,0:T(8,128)(2,1)}, u32[]{:S(2)}, u32[]{:S(2)}) collective-permute-start(bf16[16,80,384]{2,1,0:T(8,128)(2,1)} %add_convert_fusion.5), channel_id=1, source_target_pairs={{0,48},{16,0},{32,16},{48,32},{64,80},{80,96},{96,112},{112,64},{1... | collective-permute-start | bytes 2949128 | tf_op jit(solution)/shard_map/ppermute | solution.py:956
  402.0 121.0 %reduce-scatter.2.cloned.1.call-start = ((), (), s32[]{:S(2)}) async-start(), calls=%async_computation.12 | async-start | bytes 7938048 | tf_op jit(solution)/shard_map/reduce_scatter | solution.py:1137
  435.5 28.9 %collective-permute-start.55 = (bf16[16,80,384]{2,1,0:T(8,128)(2,1)}, bf16[16,80,384]{2,1,0:T(8,128)(2,1)}, u32[]{:S(2)}, u32[]{:S(2)}) collective-permute-start(bf16[16,80,384]{2,1,0:T(8,128)(2,1)} %get-tuple-element.228), channel_id=1, source_target_pairs={{0,64},{64,0},{1,65},{65,1},{2,66},{66,2},{3,67},{67,3},{4,68},{68... | collective-permute-start | bytes 2949128 | tf_op jit(solution)/shard_map/ppermute | solution.py:45
  435.6 31.8 %collective-permute-start.57 = (bf16[16,80,384]{2,1,0:T(8,128)(2,1)}, bf16[16,80,384]{2,1,0:T(8,128)(2,1)}, u32[]{:S(2)}, u32[]{:S(2)}) collective-permute-start(bf16[16,80,384]{2,1,0:T(8,128)(2,1)} %get-tuple-element.230), channel_id=1, source_target_pairs={{0,64},{64,0},{1,65},{65,1},{2,66},{66,2},{3,67},{67,3},{4,68},{68... | collective-permute-start | bytes 2949128 | tf_op jit(solution)/shard_map/ppermute | solution.py:45
  448.8 33.0 %all-to-all-start.8 = ((bf16[16,80,640]{2,1,0:T(8,128)(2,1)}), bf16[16,80,640]{2,1,0:T(8,128)(2,1)}, u32[]{:S(2)}, u32[]{:S(2)}) async-start(bf16[16,80,640]{2,1,0:T(8,128)(2,1)} %low_gradients.1), calls=%async_computation.8 | async-start | bytes 3276800 | tf_op jit(solution)/shard_map/all_to_all | solution.py:1151
  459.4 35.0 %collective-permute-start.59 = (bf16[16,80,384]{2,1,0:T(8,128)(2,1)}, bf16[16,80,384]{2,1,0:T(8,128)(2,1)}, u32[]{:S(2)}, u32[]{:S(2)}) collective-permute-start(bf16[16,80,384]{2,1,0:T(8,128)(2,1)} %get-tuple-element.232), channel_id=1, source_target_pairs={{0,64},{64,0},{1,65},{65,1},{2,66},{66,2},{3,67},{67,3},{4,68},{68... | collective-permute-start | bytes 2949128 | tf_op jit(solution)/shard_map/ppermute | solution.py:45
  461.4 35.3 %collective-permute-start.60 = (bf16[16,80,384]{2,1,0:T(8,128)(2,1)}, bf16[16,80,384]{2,1,0:T(8,128)(2,1)}, u32[]{:S(2)}, u32[]{:S(2)}) collective-permute-start(bf16[16,80,384]{2,1,0:T(8,128)(2,1)} %get-tuple-element.234), channel_id=1, source_target_pairs={{0,64},{64,0},{1,65},{65,1},{2,66},{66,2},{3,67},{67,3},{4,68},{68... | collective-permute-start | bytes 2949128 | tf_op jit(solution)/shard_map/ppermute | solution.py:45
  467.2 30.3 %collective-permute-start.56 = (bf16[16,80,384]{2,1,0:T(8,128)(2,1)}, bf16[16,80,384]{2,1,0:T(8,128)(2,1)}, u32[]{:S(2)}, u32[]{:S(2)}) collective-permute-start(bf16[16,80,384]{2,1,0:T(8,128)(2,1)} %add_convert_fusion.3), channel_id=1, source_target_pairs={{0,48},{16,0},{32,16},{48,32},{64,80},{80,96},{96,112},{112,64},{1... | collective-permute-start | bytes 2949128 | tf_op jit(solution)/shard_map/ppermute | solution.py:956
  469.8 29.5 %collective-permute-start.58 = (bf16[16,80,384]{2,1,0:T(8,128)(2,1)}, bf16[16,80,384]{2,1,0:T(8,128)(2,1)}, u32[]{:S(2)}, u32[]{:S(2)}) collective-permute-start(bf16[16,80,384]{2,1,0:T(8,128)(2,1)} %add_convert_fusion.2), channel_id=1, source_target_pairs={{0,16},{16,32},{32,48},{48,0},{64,112},{80,64},{96,80},{112,96},{1... | collective-permute-start | bytes 2949128 | tf_op jit(solution)/shard_map/ppermute | solution.py:956
  485.9 38.9 %all-to-all-start.9 = ((bf16[16,16,1152]{2,1,0:T(8,128)(2,1)}), bf16[16,16,1152]{2,1,0:T(8,128)(2,1)S(1)}, u32[]{:S(2)}, u32[]{:S(2)}) async-start(bf16[16,16,1152]{2,1,0:T(8,128)(2,1)} %broadcast_in_dim.153), calls=%async_computation.9 | async-start | bytes 1179648 | tf_op jit(solution)/shard_map/all_to_all | solution.py:1162
  497.5 36.9 %collective-permute-start.67 = (f32[64,640]{1,0:T(8,128)S(1)}, f32[64,640]{1,0:T(8,128)S(1)}, u32[]{:S(2)}, u32[]{:S(2)}) collective-permute-start(f32[64,640]{1,0:T(8,128)S(1)} %convert_reduce_fusion.low_ref), channel_id=1, source_target_pairs={{64,0},{65,1},{66,2},{67,3},{68,4},{69,5},{70,6},{71,7},{72,8},{73... | collective-permute-start | bytes 491528 | tf_op jit(solution)/shard_map/ppermute | solution.py:1184
  536.0 37.4 %all-to-all-start.10 = ((bf16[16,176,384]{2,1,0:T(8,128)(2,1)}), bf16[16,176,384]{2,1,0:T(8,128)(2,1)}, u32[]{:S(2)}, u32[]{:S(2)}) async-start(bf16[16,176,384]{2,1,0:T(8,128)(2,1)} %pad_maximum_fusion.1), calls=%async_computation.11 | async-start | bytes 4325376 | tf_op jit(solution)/shard_map/all_to_all | solution.py:1203
  (171 other events, 1594.9 us)
Sparse Core Ops, SparseCore 0:
  15.6 79.7 all-gather.6
  104.3 94.8 all-gather.8
  232.2 49.9 all-gather.10
  406.1 104.5 reduce-scatter.1
